TPU v7x, 128 devices: a whole 4x4x4 slice. The times are simulated.
128 devices in a mesh: row: 8 (over y, core), col: 16 (over z, x).
Axes of the slice: x: 4, y: 4, z: 4, core: 2. Of those that a mesh axis runs over, the one named last changes fastest.
Arguments:
- embedded: bfloat16 [128, 393216], P('row', 'col'), may hold values from -6 to 6
- window_target_device: int32 [16, 256], P('row', 'col'), may hold values from -1 to 127, as said below
- window_device_slot: int32 [16, 256], P('row', 'col'), may hold values from -1 to 15, as said below
- cloud_mask_token: bfloat16 [192], replicated, may hold values from -4 to 4
- query_key_value_weight: bfloat16 [2, 192, 576], replicated, may hold values from -0.4375 to 0.4375
- projection_weight: bfloat16 [2, 192, 192], replicated, may hold values from -0.4375 to 0.4375
- up_weight: bfloat16 [2, 192, 768], replicated, may hold values from -0.4375 to 0.4375
- down_weight: bfloat16 [2, 768, 192], replicated, may hold values from -0.21875 to 0.21875
- bias_net_input_weight: float32 [2, 2, 512], replicated, may hold values from -4 to 4
- bias_net_first_bias: float32 [2, 512], replicated, may hold values from -3 to 3
- bias_net_output_weight: float32 [2, 512, 6], replicated, may hold values from -0.25 to 0.25
- temper: float32 [2, 6], replicated, may hold values from 1 to 10
- norm_gain_values: float32 [2, 2, 192], replicated, may hold values from 0.25 to 1.75
Outputs:
- features: bfloat16 [128, 393216], P('row', 'col')
- packed: bfloat16 [2048, 12288], P(('row', 'col'))
Inputs may be any that keep to these rules, and one draw needn't show every extreme that they name: `window_target_device`: devices are numbered row index * 16 + col index. A quarter of the devices hold 32 visible windows each, a quarter 3 * 8, a quarter 32 / 4 and a quarter none; which devices and which windows are drawn. Every device is named by exactly 16 visible windows, and by at most 1 windows of any one device. `window_device_slot`: -1 exactly where window_target_device is -1; the windows that name one device carry the slots 0 to 15, each once.
All inputs are finite; a program needn't handle non-finite values.
Results may differ from a plain program's by a relative error of at most 0.02.
Values may be sent and summed in bfloat16 or wider, within the bound.
No kernel may reach another device: no remote copies, remote signals or barrier semaphores. Data moves between devices by JAX's collectives and lax.ppermute only.
A program may use at most 128 MiB of HBM per device.

v0:
```python
import jax
import jax.numpy as jnp
from jax import lax
from jax.sharding import PartitionSpec as P

WIN = 8


finest = lax.Precision.HIGHEST


def passed_along(block, axis, distance):
    devices = range(lax.axis_size(axis))
    route = [((i - distance) % len(devices), i) for i in devices]
    return lax.ppermute(block, axis, route)


def layer_norm(values, gain_row):
    row_mean = jnp.mean(values, -1, keepdims=True)
    centred = values - row_mean
    spread = jnp.mean(centred * centred, -1, keepdims=True)
    return centred * lax.rsqrt(spread + 1e-05) * gain_row


def relative_position_bias(first_layer, first_bias, second_layer):
    cell_ids = jnp.arange(WIN * WIN)
    across = cell_ids // WIN
    along_row = cell_ids % WIN
    offsets = jnp.stack(
        [across[:, None] - across[None, :], along_row[:, None] - along_row[None, :]], -1
    ).astype(jnp.float32)
    scaled = offsets * (8.0 / (WIN - 1))
    coords = jnp.sign(scaled) * jnp.log2(jnp.abs(scaled) + 1.0) / 3.0
    hidden_units = jax.nn.relu(
        jnp.dot(coords.reshape(-1, 2), first_layer, precision=finest) + first_bias
    )
    logits = jnp.dot(hidden_units, second_layer, precision=finest)
    n_heads = second_layer.shape[1]
    return (16.0 * jax.nn.sigmoid(logits)).T.reshape(n_heads, WIN * WIN, WIN * WIN)


def swin_block(
    windows,
    region,
    query_key_value_weight,
    projection_weight,
    up_weight,
    down_weight,
    bias_term,
    temper,
    gains,
):
    n_windows, n_places, n_feat = windows.shape
    n_heads = temper.shape[0]
    flat_rows = windows.reshape(n_windows * n_places, n_feat)
    triple = jnp.dot(flat_rows, query_key_value_weight, preferred_element_type=jnp.float32).astype(
        jnp.bfloat16
    )
    triple = triple.reshape(n_windows, n_places, 3, n_heads, n_feat // n_heads)
    queries = triple[:, :, 0].astype(jnp.float32)
    keys_now = triple[:, :, 1].astype(jnp.float32)
    values_now = triple[:, :, 2]
    queries = queries * lax.rsqrt(jnp.sum(queries * queries, -1, keepdims=True) + 1e-06)
    keys_now = keys_now * lax.rsqrt(jnp.sum(keys_now * keys_now, -1, keepdims=True) + 1e-06)
    scores = (
        jnp.einsum("nqhd,nkhd->nhqk", queries, keys_now, precision=finest) * temper[:, None, None]
        + bias_term
    )
    if region is not None:
        scores = scores + jnp.where(region[:, :, None] == region[:, None, :], 0.0, -100.0)[
            :, None
        ].astype(scores.dtype)
    weights_now = jax.nn.softmax(scores, axis=-1).astype(jnp.bfloat16)
    mixed_heads = jnp.einsum(
        "nhqk,nkhd->nqhd", weights_now, values_now, preferred_element_type=jnp.float32
    )
    mixed_heads = mixed_heads.astype(jnp.bfloat16).reshape(n_windows * n_places, n_feat)
    attended = jnp.dot(mixed_heads, projection_weight, preferred_element_type=jnp.float32)
    hidden = (flat_rows.astype(jnp.float32) + layer_norm(attended, gains[0])).astype(jnp.bfloat16)
    expanded = jax.nn.gelu(
        jnp.dot(hidden, up_weight, preferred_element_type=jnp.float32), approximate=False
    ).astype(jnp.bfloat16)
    reduced = jnp.dot(expanded, down_weight, preferred_element_type=jnp.float32)
    result = hidden.astype(jnp.float32) + layer_norm(reduced, gains[1])
    return result.astype(jnp.bfloat16).reshape(n_windows, n_places, n_feat)


def to_windows(token_grid):
    n_rows, n_cols, n_chan = token_grid.shape
    tiled = token_grid.reshape(n_rows // WIN, WIN, n_cols // WIN, WIN, n_chan).transpose(
        0, 2, 1, 3, 4
    )
    return tiled.reshape(n_rows // WIN * (n_cols // WIN), WIN * WIN, n_chan)


def from_windows(win_tiles, n_rows, n_cols):
    n_chan = win_tiles.shape[-1]
    tiled = win_tiles.reshape(n_rows // WIN, n_cols // WIN, WIN, WIN, n_chan).transpose(
        0, 2, 1, 3, 4
    )
    return tiled.reshape(n_rows, n_cols, n_chan)


def band_of(ids, extent, shift_by):
    return (ids >= extent - WIN).astype(jnp.int32) + (ids >= extent - shift_by).astype(jnp.int32)


def local(
    embedded,
    window_target_device,
    window_device_slot,
    cloud_mask_token,
    query_key_value_weight,
    projection_weight,
    up_weight,
    down_weight,
    bias_net_input_weight,
    bias_net_first_bias,
    bias_net_output_weight,
    temper,
    norm_gain_values,
):
    n_feat = cloud_mask_token.shape[0]
    rows_dev = embedded.shape[0]
    cols_dev = embedded.shape[1] // n_feat
    shift_by = WIN // 2
    own_tile = embedded.reshape(rows_dev, cols_dev, n_feat)
    windows = to_windows(own_tile)
    n_local = windows.shape[0]
    n_slots = n_local // 2

    def layer_params(layer_number):
        bias_term = relative_position_bias(
            bias_net_input_weight[layer_number],
            bias_net_first_bias[layer_number],
            bias_net_output_weight[layer_number],
        )
        return (
            query_key_value_weight[layer_number],
            projection_weight[layer_number],
            up_weight[layer_number],
            down_weight[layer_number],
            bias_term,
            temper[layer_number],
            norm_gain_values[layer_number],
        )

    first_params = layer_params(0)
    targets = window_target_device.reshape(-1)
    slots_in = window_device_slot.reshape(-1)
    visible = targets >= 0
    devices = lax.axis_size("row") * lax.axis_size("col")
    capacity = (n_local + devices - 1) // devices
    entries = devices * capacity
    win_order = jnp.arange(n_local, dtype=jnp.int32)
    earlier = (targets[:, None] == targets[None, :]) & (win_order[None, :] < win_order[:, None])
    within = jnp.sum(earlier.astype(jnp.int32), axis=1)
    entry_at = jnp.where(visible, targets * capacity + within, entries)
    source = jnp.full((entries,), n_local, jnp.int32).at[entry_at].set(win_order, mode="drop")
    slots_out = jnp.concatenate([slots_in, jnp.full((1,), -1, jnp.int32)])[source]
    blank = jnp.zeros((1,) + windows.shape[1:], jnp.bfloat16)
    first_out = swin_block(windows, None, *first_params)
    padded_out = jnp.concatenate([first_out, blank], 0)
    arrived, arrived_slots = (
        lax.all_to_all(padded_out[source], ("row", "col"), split_axis=0, concat_axis=0, tiled=True),
        lax.all_to_all(slots_out, ("row", "col"), split_axis=0, concat_axis=0, tiled=True),
    )
    is_live = arrived_slots >= 0
    slot_entry = (
        jnp.zeros((n_slots,), jnp.int32)
        .at[jnp.where(is_live, arrived_slots, n_slots)]
        .set(jnp.arange(entries, dtype=jnp.int32), mode="drop")
    )
    packed_rows = arrived[slot_entry]
    kept_out = jnp.where(visible[:, None, None], first_out, cloud_mask_token[None, None, :])
    middle = from_windows(kept_out, rows_dev, cols_dev)
    total_rows = rows_dev * lax.axis_size("row")
    total_cols = cols_dev * lax.axis_size("col")
    second_params = layer_params(1)
    from_below = passed_along(middle[:shift_by], "row", -1)
    rolled = jnp.concatenate([middle[shift_by:], from_below], 0)
    from_right = passed_along(rolled[:, :shift_by], "col", -1)
    rolled = jnp.concatenate([rolled[:, shift_by:], from_right], 1)
    row_ids = lax.axis_index("row") * rows_dev + jnp.arange(rows_dev, dtype=jnp.int32)
    col_ids = lax.axis_index("col") * cols_dev + jnp.arange(cols_dev, dtype=jnp.int32)
    region = (
        band_of(row_ids, total_rows, shift_by)[:, None] * 3
        + band_of(col_ids, total_cols, shift_by)[None, :]
    )
    region_tiles = to_windows(region[:, :, None])[..., 0]
    second = swin_block(to_windows(rolled), region_tiles, *second_params)
    out_grid = from_windows(second, rows_dev, cols_dev)
    down_rows = passed_along(out_grid[rows_dev - shift_by :], "row", 1)
    restored = jnp.concatenate([down_rows, out_grid[: rows_dev - shift_by]], 0)
    down_cols = passed_along(restored[:, cols_dev - shift_by :], "col", 1)
    restored = jnp.concatenate([down_cols, restored[:, : cols_dev - shift_by]], 1)
    return (restored.reshape(rows_dev, cols_dev * n_feat), packed_rows.reshape(n_slots, -1))


def solution(mesh):
    in_specs = (
        P("row", "col"),
        P("row", "col"),
        P("row", "col"),
        P(),
        P(),
        P(),
        P(),
        P(),
        P(),
        P(),
        P(),
        P(),
        P(),
    )
    out_specs = (P("row", "col"), P(("row", "col"), None))
    return jax.shard_map(local, mesh=mesh, in_specs=in_specs, out_specs=out_specs, check_vma=False)
```

profile of v0, /device:TPU:0, one launch (start us, length us, event | category | flops | bytes accessed | tf_op | source)
XLA Modules:
  0.0 266.5 jit_solution(9246633808708431571)
XLA Ops:
  0.6 0.8 eq.41
  1.4 0.8 reshape.381
  2.1 0.8 reshape.382
  3.1 0.7 scatter_custom_fusion
  3.9 1.2 gather_fusion.1
  5.1 0.7 copy.129
  5.9 11.7 %all-to-all-start.1 = ((s32[128,1,1]{2,1,0:T(1,128)}), s32[128,1,1]{2,1,0:T(1,128)}, u32[]{:S(2)}, u32[]{:S(2)}) async-start(s32[128,1,1]{2,1,0:T(1,128)} %copy.129), calls=%async_computation.1 | async-start | bytes 131072 | tf_op jit(solution)/shard_map/all_to_all | solution.py:166
  17.6 1.2 broadcast_compare_fusion
  18.7 1.3 slice_bitcast_fusion
  20.1 1.4 fusion.205
  21.4 1.3 fusion.206
  22.8 1.4 fusion.204
  24.7 2.3 reshape_reshape.12
  27.2 1.2 copy.105
  28.4 1.8 convolution_convert_fusion.1
  30.2 6.3 %reshape.371 = bf16[32,64,3,6,32]{1,0,4,3,2:T(8,128)(2,1)} reshape(bf16[2048,576]{0,1:T(8,128)(2,1)S(1)} %convolution_convert_fusion.1) | data formatting | bytes 4718592 | tf_op jit(solution)/shard_map/reshape | solution.py:59
  36.5 4.6 %fusion.203 = (bf16[32,64,1,6,32]{1,0,4,3,2:T(8,128)(2,1)}, bf16[32,64,1,6,32]{1,0,4,3,2:T(8,128)(2,1)S(1)}, bf16[32,64,1,6,32]{1,0,4,3,2:T(8,128)(2,1)S(1)}) fusion(bf16[32,64,3,6,32]{1,0,4,3,2:T(8,128)(2,1)} %reshape.371), kind=kLoop, calls=%fused_computation.272 | loop fusion | bytes 4718592 | tf_op jit(solution)/shard_map/slice | solution.py:62
  41.1 1.8 fusion.70
  42.9 0.7 add_rsqrt_fusion.3
  43.6 0.7 add_rsqrt_fusion.2
  44.3 6.7 %fusion.126 = f32[4096,512]{1,0:T(8,128)S(1)} fusion(f32[2,2,512]{2,1,0:T(2,128)S(1)} %copy-done.12, s32[4096,1]{0,1:T(1,128)S(1)} %sub.130, s32[4096,1]{0,1:T(1,128)S(1)} %sub.125), kind=kOutput, calls=%fused_computation.171 | convolution fusion | flops 50405376 | bytes 8425472 | tf_op jit(solution)/shard_map/dot_general | solution.py:35
  51.1 20.7 %fusion.62 = f32[6,4096]{1,0:T(8,128)S(1)} fusion(f32[4096,512]{1,0:T(8,128)S(1)} %fusion.126, f32[512]{0:T(512)S(1)} %bitcast.180, f32[1,512,6]{1,0,2:T(1,128)S(1)} %get-tuple-element.9), kind=kOutput, calls=%fused_computation.69 | convolution fusion | flops 155287552 | bytes 8501248 | tf_op jit(solution)/shard_map/dot_general | solution.py:37
  72.0 12.5 %fusion.71 = f32[32,6,64,64]{2,3,1,0:T(8,128)S(1)} fusion(f32[32,64,6]{1,2,0:T(8,128)} %add_rsqrt_fusion.2, f32[32,64,6]{1,2,0:T(8,128)} %add_rsqrt_fusion.3, bf16[32,64,1,6,32]{1,0,4,3,2:T(8,128)(2,1)S(1)} %get-tuple-element.6, bf16[32,64,1,6,32]{1,0,4,3,2:T(8,128)(2,1)S(1)} %get-tuple-element.7), kind=kOutput, calls=%fused_computation.84 | convolution fusion | flops 303562752 | bytes 4816896 | tf_op jit(solution)/shard_map/nqhd,nkhd->nhqk/dot_general | solution.py:66
  84.6 2.8 %fusion.207 = (f32[32,6,64]{2,1,0:T(8,128)S(1)}, f32[32,6,64,64]{2,3,1,0:T(8,128)S(1)}) fusion(f32[32,6,64,64]{2,3,1,0:T(8,128)S(1)} %fusion.71, f32[6,64,64]{1,2,0:T(8,128)S(1)} %copy.110, f32[6]{0:T(128)S(1)} %copy-done.19), kind=kOutput, calls=%fused_computation.276 | output fusion | flops 4718655 | bytes 6438936 | tf_op jit(solution)/shard_map/sub | solution.py:73
  87.4 1.2 fusion.97
  88.7 1.0 copy.112
  89.7 1.7 reshape.372
  91.4 0.4 fusion.208
  92.1 0.4 add_convert_fusion.3
  92.5 16.3 %fusion.209 = (f32[2048]{0:T(1024)S(1)}, f32[2048,192]{0,1:T(8,128)S(1)}) fusion(bf16[2,768,192]{1,2,0:T(8,128)(2,1)} %param.20, bf16[2048,192]{0,1:T(8,128)(2,1)S(1)} %add_convert_fusion.3, bf16[2,192,768]{2,1,0:T(8,128)(2,1)} %param.19), kind=kOutput, calls=%fused_computation.278 | convolution fusion | flops 1310586880 | bytes 2957312 | tf_op jit(solution)/shard_map/dot_general | solution.py:83
  109.1 1.5 add_convert_fusion.2
  110.6 0.5 copy.113
  111.4 0.7 slice.156
  112.1 1.9 collective-permute-start
  114.0 9.0 %fusion.124 = f32[4096,512]{1,0:T(8,128)} fusion(f32[2,2,512]{2,1,0:T(2,128)S(1)} %copy-done.13, s32[4096,1]{0,1:T(1,128)S(1)} %sub.130, s32[4096,1]{0,1:T(1,128)S(1)} %copy-done.9), kind=kOutput, calls=%fused_computation.169 | convolution fusion | flops 50405376 | bytes 8425472 | tf_op jit(solution)/shard_map/dot_general | solution.py:35
  123.3 9.9 %fusion.50 = f32[6,4096]{1,0:T(8,128)S(1)} fusion(f32[4096,512]{1,0:T(8,128)} %fusion.124, f32[512]{0:T(512)S(1)} %bitcast.179, f32[1,512,6]{1,0,2:T(1,128)S(1)} %copy-done.10), kind=kOutput, calls=%fused_computation.65 | convolution fusion | flops 155287552 | bytes 8501248 | tf_op jit(solution)/shard_map/dot_general | solution.py:37
  133.2 1.3 compare_select_fusion
  134.7 0.8 copy.121
  135.7 3.0 %gather_fusion = bf16[128,64,192]{2,1,0:T(8,128)(2,1)} fusion(bf16[33,64,192]{2,1,0:T(8,128)(2,1)S(1)} %concatenate.23, s32[1024]{0:T(1024)} %copy-done.14), kind=kCustom, calls=%fused_computation | custom fusion | bytes 6291968 | tf_op jit(solution)/shard_map/gather | solution.py:165
  138.7 8.6 %all-to-all-start = ((bf16[128,64,192]{2,1,0:T(8,128)(2,1)}), bf16[128,64,192]{2,1,0:T(8,128)(2,1)}, u32[]{:S(2)}, u32[]{:S(2)}) async-start(bf16[128,64,192]{2,1,0:T(8,128)(2,1)} %gather_fusion), calls=%async_computation | async-start | bytes 8388608 | tf_op jit(solution)/shard_map/all_to_all | solution.py:165
  147.3 3.2 %reduce = s32[128]{0:T(128)S(1)} reduce(s32[128,1,1]{2,1,0:T(1,128)} %all-to-all-done.1, s32[]{:T(128)} %constant.58.clone.1), dimensions={1,2}, to_apply=%all_to_all.13.reduce_sub_computation | reduce | bytes 1028 | tf_op jit(solution)/shard_map/all_to_all | solution.py:166
  150.5 1.0 scatter_custom_fusion.1
  151.6 5.0 %collective-permute-start.1 = (bf16[16,4,192]{2,1,0:T(4,128)(2,1)S(1)}, bf16[16,4,192]{2,1,0:T(4,128)(2,1)S(1)}, u32[]{:S(2)}, u32[]{:S(2)}) collective-permute-start(bf16[16,4,192]{2,1,0:T(4,128)(2,1)S(1)} %pad_maximum_fusion.3), channel_id=1, source_target_pairs={{1,0},{2,1},{3,2},{4,3},{5,4},{6,5},{7,6},{8,7},{9,8},{10,9},{11,1... | collective-permute-start | bytes 73736 | tf_op jit(solution)/shard_map/ppermute | solution.py:15
  156.9 36.9 %collective-permute-done.1 = bf16[16,4,192]{2,1,0:T(4,128)(2,1)S(1)} collective-permute-done((bf16[16,4,192]{2,1,0:T(4,128)(2,1)S(1)}, bf16[16,4,192]{2,1,0:T(4,128)(2,1)S(1)}, u32[]{:S(2)}, u32[]{:S(2)}) %collective-permute-start.1) | collective-permute-done | bytes 24608 | tf_op jit(solution)/shard_map/ppermute | solution.py:15
  194.1 1.2 copy.116
  195.3 1.8 convolution_convert_fusion
  197.1 6.3 %reshape.376 = bf16[32,64,3,6,32]{1,0,4,3,2:T(8,128)(2,1)} reshape(bf16[2048,576]{0,1:T(8,128)(2,1)S(1)} %convolution_convert_fusion) | data formatting | bytes 4718592 | tf_op jit(solution)/shard_map/reshape | solution.py:59
  203.4 3.2 %fusion.202 = (bf16[32,64,1,6,32]{1,0,4,3,2:T(8,128)(2,1)S(1)}, bf16[32,64,1,6,32]{1,0,4,3,2:T(8,128)(2,1)S(1)}, bf16[32,64,1,6,32]{1,0,4,3,2:T(8,128)(2,1)S(1)}) fusion(bf16[32,64,3,6,32]{1,0,4,3,2:T(8,128)(2,1)} %reshape.376), kind=kLoop, calls=%fused_computation.271 | loop fusion | bytes 4718592 | tf_op jit(solution)/shard_map/slice | solution.py:62
  206.6 1.0 fusion.73
  207.6 1.0 fusion.75
  208.7 11.6 %fusion.74 = f32[32,6,64,64]{2,3,1,0:T(8,128)S(1)} fusion(f32[32,64,6]{1,2,0:T(8,128)S(1)} %add_rsqrt_fusion, f32[32,64,6]{1,2,0:T(8,128)S(1)} %add_rsqrt_fusion.1, bf16[32,64,1,6,32]{1,0,4,3,2:T(8,128)(2,1)S(1)} %get-tuple-element.3, bf16[32,64,1,6,32]{1,0,4,3,2:T(8,128)(2,1)S(1)} %get-tuple-element.4), kind=kOutput, calls=%fused_computation.87 | convolution fusion | flops 303562752 | bytes 4816896 | tf_op jit(solution)/shard_map/nqhd,nkhd->nhqk/dot_general | solution.py:66
  220.3 2.8 %fusion.212 = (f32[32,6,64]{2,1,0:T(8,128)S(1)}, f32[32,6,64,64]{2,3,1,0:T(8,128)S(1)}) fusion(f32[32,6,64,64]{2,3,1,0:T(8,128)S(1)} %fusion.74, f32[32,64,64]{1,2,0:T(8,128)S(1)} %copy-done.4, f32[6,64,64]{1,2,0:T(8,128)S(1)} %copy-done.7, f32[6]{0:T(128)S(1)} %copy-done.20), kind=kOutput, calls=%fused_computation.279 | output fusion | flops 6291519 | bytes 6963224 | tf_op jit(solution)/shard_map/sub | solution.py:73
  223.1 1.2 fusion.98
  224.4 1.0 copy.125
  225.4 1.5 reshape.377
  226.9 0.4 fusion.213
  228.0 16.1 %fusion.214 = (f32[2048]{0:T(1024)S(1)}, f32[2048,192]{0,1:T(8,128)S(1)}) fusion(bf16[2,768,192]{1,2,0:T(8,128)(2,1)} %param.20, bf16[2048,192]{0,1:T(8,128)(2,1)S(1)} %add_convert_fusion.1, bf16[2,192,768]{2,1,0:T(8,128)(2,1)} %param.19), kind=kOutput, calls=%fused_computation.281 | convolution fusion | flops 1310586880 | bytes 2957312 | tf_op jit(solution)/shard_map/dot_general | solution.py:83
  244.7 0.5 copy.126
  245.4 6.9 %collective-permute-done.2 = bf16[4,128,192]{2,1,0:T(8,128)(2,1)S(1)} collective-permute-done((bf16[4,128,192]{2,1,0:T(8,128)(2,1)S(1)}, bf16[4,128,192]{2,1,0:T(8,128)(2,1)S(1)}, u32[]{:S(2)}, u32[]{:S(2)}) %collective-permute-start.2) | collective-permute-done | bytes 196640 | tf_op jit(solution)/shard_map/ppermute | solution.py:15
  252.4 1.1 collective-permute-start.3
  253.5 6.2 %collective-permute-done.3 = bf16[16,4,192]{2,1,0:T(4,128)(2,1)S(1)} collective-permute-done((bf16[16,4,192]{2,1,0:T(4,128)(2,1)S(1)}, bf16[16,4,192]{2,1,0:T(4,128)(2,1)S(1)}, u32[]{:S(2)}, u32[]{:S(2)}) %collective-permute-start.3) | collective-permute-done | bytes 24608 | tf_op jit(solution)/shard_map/ppermute | solution.py:15
  260.1 2.0 reshape.379
  262.1 2.8 %gather_fusion.2 = bf16[16,64,192]{2,1,0:T(8,128)(2,1)S(1)} fusion(bf16[128,64,192]{2,1,0:T(8,128)(2,1)} %all-to-all-done, s32[1024]{0:T(1024)S(1)} %pad_clamp_fusion), kind=kCustom, calls=%fused_computation.2 | custom fusion | bytes 786496 | tf_op jit(solution)/shard_map/gather | solution.py:174
  264.9 1.3 reshape.383
  (110 shorter events, 5.0 us)
Async XLA Ops:
  3.8 19.0 %copy-start.14 = (s32[1024]{0:T(1024)}, s32[1024]{0:T(1024)S(1)}, u32[]{:S(2)}) copy-start(s32[1024]{0:T(1024)S(1)} %pad_clamp_fusion.1) | copy-start | bytes 12292
  5.9 132.8 %all-to-all-start.1 = ((s32[128,1,1]{2,1,0:T(1,128)}), s32[128,1,1]{2,1,0:T(1,128)}, u32[]{:S(2)}, u32[]{:S(2)}) async-start(s32[128,1,1]{2,1,0:T(1,128)} %copy.129), calls=%async_computation.1 | async-start | bytes 131072 | tf_op jit(solution)/shard_map/all_to_all | solution.py:166
  36.5 7.8 %copy-start.12 = (f32[2,2,512]{2,1,0:T(2,128)S(1)}, f32[2,2,512]{2,1,0:T(2,128)}, u32[]{:S(2)}) copy-start(f32[2,2,512]{2,1,0:T(2,128)} %param.21) | copy-start | bytes 24580
  44.3 6.8 %copy-start.8 = (s32[4096,1]{0,1:T(1,128)}, s32[4096,1]{0,1:T(1,128)S(1)}, u32[]{:S(2)}) copy-start(s32[4096,1]{0,1:T(1,128)S(1)} %sub.125) | copy-start | bytes 49156
  72.0 12.5 %copy-start.19 = (f32[6]{0:T(128)S(1)}, f32[6]{0:T(128)}, u32[]{:S(2)}) copy-start(f32[6]{0:T(128)} %get-tuple-element.17) | copy-start | bytes 76
  84.5 2.9 %copy-start.3 = (bf16[32,64,1,6,32]{1,0,4,3,2:T(8,128)(2,1)S(1)}, bf16[32,64,1,6,32]{1,0,4,3,2:T(8,128)(2,1)}, u32[]{:S(2)}) copy-start(bf16[32,64,1,6,32]{1,0,4,3,2:T(8,128)(2,1)} %get-tuple-element.5) | copy-start | bytes 2359300
  87.4 4.0 %copy-start.5 = (bf16[2,192,192]{2,1,0:T(8,128)(2,1)S(1)}, bf16[2,192,192]{2,1,0:T(8,128)(2,1)}, u32[]{:S(2)}) copy-start(bf16[2,192,192]{2,1,0:T(8,128)(2,1)} %param.18) | copy-start | bytes 442372
  88.7 3.4 %copy-start = (bf16[2048,192]{0,1:T(8,128)(2,1)S(1)}, bf16[2048,192]{0,1:T(8,128)(2,1)}, u32[]{:S(2)}) copy-start(bf16[2048,192]{0,1:T(8,128)(2,1)} %copy.105) | copy-start | bytes 2359300
  88.7 3.4 %copy-start.18 = (f32[1,1,192]{2,1,0:T(1,128)S(1)}, f32[1,1,192]{2,1,0:T(1,128)}, u32[]{:S(2)}) copy-start(f32[1,1,192]{2,1,0:T(1,128)} %get-tuple-element.12) | copy-start | bytes 2308
  92.5 16.3 %copy-start.2 = (bf16[2048,192]{0,1:T(8,128)(2,1)}, bf16[2048,192]{0,1:T(8,128)(2,1)S(1)}, u32[]{:S(2)}) copy-start(bf16[2048,192]{0,1:T(8,128)(2,1)S(1)} %add_convert_fusion.3) | copy-start | bytes 2359300
  92.5 16.6 %copy-start.17 = (f32[1,1,192]{2,1,0:T(1,128)S(1)}, f32[1,1,192]{2,1,0:T(1,128)}, u32[]{:S(2)}) copy-start(f32[1,1,192]{2,1,0:T(1,128)} %get-tuple-element.11) | copy-start | bytes 2308
  108.8 2.3 copy-start.21
  108.8 2.3 copy-start.22
  108.8 5.2 %copy-start.9 = (s32[4096,1]{0,1:T(1,128)S(1)}, s32[4096,1]{0,1:T(1,128)}, u32[]{:S(2)}) copy-start(s32[4096,1]{0,1:T(1,128)} %copy-done.8) | copy-start | bytes 49156
  108.8 5.2 %copy-start.13 = (f32[2,2,512]{2,1,0:T(2,128)S(1)}, f32[2,2,512]{2,1,0:T(2,128)}, u32[]{:S(2)}) copy-start(f32[2,2,512]{2,1,0:T(2,128)} %param.21) | copy-start | bytes 24580
  112.1 39.4 %collective-permute-start = (bf16[4,128,192]{2,1,0:T(8,128)(2,1)}, bf16[4,128,192]{2,1,0:T(8,128)(2,1)S(1)}, u32[]{:S(2)}, u32[]{:S(2)}) collective-permute-start(bf16[4,128,192]{2,1,0:T(8,128)(2,1)} %slice.156), channel_id=1, source_target_pairs={{16,0},{32,16},{48,32},{64,48},{80,64},{96,80},{112,96},{0,112},{1... | collective-permute-start | bytes 589832 | tf_op jit(solution)/shard_map/ppermute | solution.py:15
  114.0 9.3 %copy-start.10 = (f32[1,512,6]{1,0,2:T(1,128)S(1)}, f32[1,512,6]{1,0,2:T(1,128)}, u32[]{:S(2)}) copy-start(f32[1,512,6]{1,0,2:T(1,128)} %get-tuple-element.8) | copy-start | bytes 36868
  114.0 9.3 %copy-start.11 = (f32[1,512]{1,0:T(1,128)S(1)}, f32[1,512]{1,0:T(1,128)}, u32[]{:S(2)}) copy-start(f32[1,512]{1,0:T(1,128)} %get-tuple-element.14) | copy-start | bytes 6148
  138.7 123.4 %all-to-all-start = ((bf16[128,64,192]{2,1,0:T(8,128)(2,1)}), bf16[128,64,192]{2,1,0:T(8,128)(2,1)}, u32[]{:S(2)}, u32[]{:S(2)}) async-start(bf16[128,64,192]{2,1,0:T(8,128)(2,1)} %gather_fusion), calls=%async_computation | async-start | bytes 8388608 | tf_op jit(solution)/shard_map/all_to_all | solution.py:165
  151.6 42.2 %collective-permute-start.1 = (bf16[16,4,192]{2,1,0:T(4,128)(2,1)S(1)}, bf16[16,4,192]{2,1,0:T(4,128)(2,1)S(1)}, u32[]{:S(2)}, u32[]{:S(2)}) collective-permute-start(bf16[16,4,192]{2,1,0:T(4,128)(2,1)S(1)} %pad_maximum_fusion.3), channel_id=1, source_target_pairs={{1,0},{2,1},{3,2},{4,3},{5,4},{6,5},{7,6},{8,7},{9,8},{10,9},{11,1... | collective-permute-start | bytes 73736 | tf_op jit(solution)/shard_map/ppermute | solution.py:15
  207.6 12.7 %copy-start.4 = (f32[32,64,64]{1,2,0:T(8,128)S(1)}, f32[32,64,64]{1,2,0:T(8,128)}, u32[]{:S(2)}) copy-start(f32[32,64,64]{1,2,0:T(8,128)} %compare_select_fusion) | copy-start | bytes 1572868
  207.6 12.7 %copy-start.7 = (f32[6,64,64]{1,2,0:T(8,128)S(1)}, f32[6,64,64]{1,2,0:T(8,128)}, u32[]{:S(2)}) copy-start(f32[6,64,64]{1,2,0:T(8,128)} %copy.121) | copy-start | bytes 294916
  207.6 12.7 %copy-start.20 = (f32[6]{0:T(128)S(1)}, f32[6]{0:T(128)}, u32[]{:S(2)}) copy-start(f32[6]{0:T(128)} %get-tuple-element.16) | copy-start | bytes 76
  223.1 3.8 %copy-start.6 = (bf16[2,192,192]{2,1,0:T(8,128)(2,1)S(1)}, bf16[2,192,192]{2,1,0:T(8,128)(2,1)}, u32[]{:S(2)}) copy-start(bf16[2,192,192]{2,1,0:T(8,128)(2,1)} %param.18) | copy-start | bytes 442372
  224.4 3.2 %copy-start.1 = (bf16[2048,192]{0,1:T(8,128)(2,1)S(1)}, bf16[2048,192]{0,1:T(8,128)(2,1)}, u32[]{:S(2)}) copy-start(bf16[2048,192]{0,1:T(8,128)(2,1)} %copy.116) | copy-start | bytes 2359300
  224.4 3.2 %copy-start.16 = (f32[1,1,192]{2,1,0:T(1,128)S(1)}, f32[1,1,192]{2,1,0:T(1,128)}, u32[]{:S(2)}) copy-start(f32[1,1,192]{2,1,0:T(1,128)} %get-tuple-element.13) | copy-start | bytes 2308
  228.0 16.3 %copy-start.15 = (f32[1,1,192]{2,1,0:T(1,128)S(1)}, f32[1,1,192]{2,1,0:T(1,128)}, u32[]{:S(2)}) copy-start(f32[1,1,192]{2,1,0:T(1,128)} %get-tuple-element.10) | copy-start | bytes 2308
  245.3 7.0 %collective-permute-start.2 = (bf16[4,128,192]{2,1,0:T(8,128)(2,1)S(1)}, bf16[4,128,192]{2,1,0:T(8,128)(2,1)S(1)}, u32[]{:S(2)}, u32[]{:S(2)}) collective-permute-start(bf16[4,128,192]{2,1,0:T(8,128)(2,1)S(1)} %slice.162), channel_id=1, source_target_pairs={{112,0},{0,16},{16,32},{32,48},{48,64},{64,80},{80,96},{96,112},{1... | collective-permute-start | bytes 589832 | tf_op jit(solution)/shard_map/ppermute | solution.py:15
  252.4 7.3 %collective-permute-start.3 = (bf16[16,4,192]{2,1,0:T(4,128)(2,1)S(1)}, bf16[16,4,192]{2,1,0:T(4,128)(2,1)S(1)}, u32[]{:S(2)}, u32[]{:S(2)}) collective-permute-start(bf16[16,4,192]{2,1,0:T(4,128)(2,1)S(1)} %pad_maximum_fusion.2), channel_id=1, source_target_pairs={{15,0},{0,1},{1,2},{2,3},{3,4},{4,5},{5,6},{6,7},{7,8},{8,9},{9,10... | collective-permute-start | bytes 73736 | tf_op jit(solution)/shard_map/ppermute | solution.py:15
where the time goes:
time: 271 us; the launch traced here: 266 us
  matrix products  110 us (41%)
  local copies, waits for them, and re-layouts  55.2 us (20%)
  waiting for transfers between devices  50 us (18%)
  starting transfers between devices  28.4 us (10%)
  other arithmetic  21.5 us (8%)
    ppermute x4, waiting for transfers between devices, passed_along(): return lax.ppermute(block, axis, route)  50 us
    dot_general x2, matrix products, swin_block(): reduced = jnp.dot(expanded, down_weight, preferred_element_type=jnp.float32)  32.3 us
    dot_general x2, matrix products, relative_position_bias(): logits = jnp.dot(hidden_units, second_layer, precision=finest)  30.6 us
    dot_general x2, matrix products, swin_block(): jnp.einsum('nqhd,nkhd->nhqk', queries, keys_now, precision=finest)  24.1 us
    dot_general x2, matrix products, relative_position_bias(): jnp.dot(coords.reshape(-1, 2), first_layer, precision=finest) + first_bias  15.7 us
    reshape x2, local copies, waits for them, and re-layouts, swin_block(): triple = triple.reshape(n_windows, n_places, 3, n_heads, n_feat // n_heads)  12.6 us
    all_to_all x1, starting transfers between devices, local(): lax.all_to_all(slots_out, ('row', 'col'), split_axis=0, concat_axis=0, ti...  11.7 us
    all_to_all x1, starting transfers between devices, local(): lax.all_to_all(padded_out[source], ('row', 'col'), split_axis=0, concat_a...  8.63 us
  transfers between devices with their start and end apart: 6, of which 3 were waited for; matrix products, arithmetic and copies ran while one was open for 66% of the time, Pallas kernels for 0%

commit v1 on v0

v1 whole, which is shorter than its diff:
```python
import functools
import math

import jax
import jax.numpy as jnp
import numpy as np
from jax import lax
from jax.experimental import pallas as pl
from jax.experimental.pallas import tpu as pltpu
from jax.sharding import PartitionSpec as P

WIN = 8
HALF = WIN // 2
CELLS = WIN * WIN
LOG2E = math.log2(math.e)
F32 = jnp.float32
BF16 = jnp.bfloat16
VMEM_BYTES = 60 * 2**20
SMEM = pl.BlockSpec(memory_space=pltpu.SMEM)
ANY = pl.BlockSpec(memory_space=pl.ANY)


def log_step(offset):
    scaled = np.abs(offset).astype(np.float32) * np.float32(8.0 / (WIN - 1))
    return np.sign(offset) * np.log2(scaled + 1.0) / 3.0


def offset_coords():
    lane = np.arange(128)
    across = np.maximum(WIN - 1 - lane // WIN, 1 - WIN)
    down = np.concatenate([-(lane % WIN), np.minimum(WIN - lane % WIN, WIN - 1)])
    return np.stack([log_step(down), log_step(np.tile(across, 2))], 1).astype(np.float32)


def head_blocks(rows, row_block, cols, col_block):
    same = (np.arange(rows) // row_block)[:, None] == (np.arange(cols) // col_block)[None, :]
    return same.astype(np.float32)


def constants(n_heads, n_feat):
    per_head = n_feat // n_heads
    return (
        jnp.asarray(offset_coords(), F32),
        jnp.asarray(head_blocks(n_feat, per_head, n_feat, per_head), BF16),
        jnp.asarray(head_blocks(n_heads * CELLS, CELLS, n_feat, per_head), BF16),
        jnp.asarray(head_blocks(n_heads, 1, n_feat, per_head), BF16),
    )


def dot(a, b):
    return jnp.dot(a, b, preferred_element_type=F32)


def dot_nt(a, b):
    return lax.dot_general(a, b, (((1,), (1,)), ((), ())), preferred_element_type=F32)


def bias_strips(coords_ref, net_in, net_first, net_out, strips_ref):
    coords = coords_ref[...]
    units = jnp.maximum(
        coords[:, 0:1] * net_in[0:1, :] + coords[:, 1:2] * net_in[1:2, :] + net_first[...], 0.0
    )
    logits = lax.dot_general(
        net_out[...], units, (((0,), (1,)), ((), ())),
        precision=lax.Precision.HIGHEST, preferred_element_type=F32,
    )
    n_heads = logits.shape[0]
    logits = jnp.concatenate([logits, jnp.zeros((8 - n_heads, 256), F32)], 0)
    table = 16.0 * LOG2E / (1.0 + jnp.exp(-logits))
    before, after = table[:, :128], table[:, 128:]
    cell = lax.broadcasted_iota(jnp.int32, (8, 128), 1) % WIN
    for u in range(WIN):
        strip = jnp.where(
            cell >= u,
            pltpu.roll(before, u, 1) if u else before,
            pltpu.roll(after, (u - WIN) % 128, 1),
        )
        strips_ref[:, u, :] = strip


def turned(strip):
    cell = lax.broadcasted_iota(jnp.int32, (WIN, 128), 1) % WIN
    strip = pltpu.roll(strip, HALF, 0)
    return jnp.where(cell < HALF, pltpu.roll(strip, 128 - HALF, 1), pltpu.roll(strip, HALF, 1))


def bias_rows(strips, w):
    lane = lax.broadcasted_iota(jnp.int32, (WIN, 128), 1)
    back = (WIN - 1 - w) * WIN
    parts = []
    for pair in range(len(strips) // 2):
        low = pltpu.roll(strips[2 * pair], (128 - back) % 128, 1)
        high = pltpu.roll(strips[2 * pair + 1], (192 - back) % 128, 1)
        parts.append(jnp.where(lane < CELLS, low, high))
    return jnp.concatenate(parts, 1)


def layer_norm(values, gain_row):
    row_mean = jnp.mean(values, -1, keepdims=True)
    centred = values - row_mean
    spread = jnp.mean(centred * centred, -1, keepdims=True)
    return centred * lax.rsqrt(spread + 1e-05) * gain_row


def unit_vectors(t, heads_ref):
    t = t.astype(BF16).astype(F32)
    squares = dot((t * t).astype(BF16), heads_ref[...])
    return t * lax.rsqrt(squares + 1e-06)


def temper_row(temper, layer, mask_ref):
    row = jnp.zeros((1, mask_ref.shape[1]), F32)
    for h in range(mask_ref.shape[0]):
        row = row + (temper[layer, h] * LOG2E) * mask_ref[h : h + 1, :].astype(F32)
    return row


def spread_heads(t, mask_ref):
    low = [t[:, :128] * mask_ref[h : h + 1, :128] for h in range(4)]
    high = [t[:, 128:] * mask_ref[h : h + 1, 128:] for h in range(4, 6)]
    return jnp.concatenate(low, 0), jnp.concatenate(high, 0)


def scores_of(q, k, mask_ref):
    low, high = spread_heads(k, mask_ref)
    return jnp.concatenate([dot_nt(q[:, :128], low), dot_nt(q[:, 128:], high)], 1)


def weighted(p, low, high):
    return jnp.concatenate([dot(p[:, :256], low), dot(p[:, 256:], high)], 1)


def totals_of(p, ones_ref):
    return weighted(p, ones_ref[:256, :128], ones_ref[256:, 128:])


def dense_tail(x, mixed, proj_ref, up_ref, down_ref, gain_ref):
    attended = dot(mixed.astype(BF16), proj_ref[...])
    hidden = (x + layer_norm(attended, gain_ref[0:1, :])).astype(BF16)
    raised = dot(hidden, up_ref[...])
    expanded = (0.5 * raised * (1.0 + lax.erf(raised * math.sqrt(0.5)))).astype(BF16)
    reduced = dot(expanded, down_ref[...])
    return (hidden.astype(F32) + layer_norm(reduced, gain_ref[1:2, :])).astype(BF16)


def split_weights(qkv_ref, q_w, k_w, v_w):
    n_feat = q_w.shape[0]
    q_w[...] = qkv_ref[:, :n_feat]
    k_w[...] = qkv_ref[:, n_feat : 2 * n_feat]
    v_w[...] = qkv_ref[:, 2 * n_feat :]


def first_kernel(
    groups,
    targets, temper, emb_ref, token_ref, coords_ref, heads_ref, ones_ref, mask_ref,
    net_in, net_first, net_out, qkv_ref, proj_ref, up_ref, down_ref, gain_ref,
    mid0_ref, mid1_ref, left_ref, right_ref, send_ref,
    bias_ref, strips_ref, q_w, k_w, v_w, p_ref, staging, sems,
):
    step = pl.program_id(0)
    n_heads, n_feat = mask_ref.shape

    @pl.when(step == 0)
    def _():
        bias_strips(coords_ref, net_in, net_first, net_out, strips_ref)
        strips = [strips_ref[h] for h in range(n_heads)]
        for w in range(WIN):
            bias_ref[w * WIN : (w + 1) * WIN, :] = bias_rows(strips, w)
        split_weights(qkv_ref, q_w, k_w, v_w)

    tiles = []
    for group in range(groups):
        slabs = []
        for w in range(WIN):
            at = (group * WIN + w) * n_feat
            slabs.append(emb_ref[:, at : at + n_feat].astype(F32))
        for i in range(2):
            tiles.append(jnp.concatenate([s[i * WIN : (i + 1) * WIN] for s in slabs], 0))
    x = jnp.concatenate(tiles, 0)
    xb = x.astype(BF16)
    q = (unit_vectors(dot(xb, q_w[...]), heads_ref) * temper_row(temper, 0, mask_ref)).astype(BF16)
    k = unit_vectors(dot(xb, k_w[...]), heads_ref).astype(BF16)
    v = dot(xb, v_w[...]).astype(BF16)
    bias = bias_ref[...]
    mixed = []
    for n in range(2 * groups):
        rows = slice(n * CELLS, (n + 1) * CELLS)
        p_ref[rows, :] = jnp.exp2(scores_of(q[rows], k[rows], mask_ref) + bias).astype(BF16)
    for n in range(2 * groups):
        rows = slice(n * CELLS, (n + 1) * CELLS)
        mixed.append(weighted(p_ref[rows, :], *spread_heads(v[rows], mask_ref)))
    mixed = jnp.concatenate(mixed, 0) / totals_of(p_ref[...], ones_ref)
    y = dense_tail(x, mixed, proj_ref, up_ref, down_ref, gain_ref).astype(F32)

    token = token_ref[...].astype(F32)
    for group in range(groups):
        for i in range(2):
            n = 2 * group + i
            j = step * groups + group
            target = targets[i, j]
            tile = y[n * CELLS : (n + 1) * CELLS]
            kept = jnp.where(target >= 0, tile, token).astype(BF16)
            mid = (mid0_ref, mid1_ref)[i]
            mid[2 * group] = kept[:32]
            mid[2 * group + 1] = kept[32:]
            if group == 0:

                @pl.when(step == 0)
                def _(i=i, kept=kept):
                    left_ref[i] = kept[:32]

            if group == groups - 1:

                @pl.when(step == pl.num_programs(0) - 1)
                def _(i=i, kept=kept):
                    right_ref[i] = kept[32:]

            slot = j * 2 + i
            staging[slot, :64] = tile[:, :128].astype(BF16)
            tails = tile[:, 128:].reshape(4, 2, WIN, 64)
            joined = jnp.concatenate([tails[:, 0], tails[:, 1]], -1)
            staging[slot, 64:] = joined.reshape(32, 128).astype(BF16)

            @pl.when(target >= 0)
            def _(slot=slot, target=target):
                pltpu.make_async_copy(staging.at[slot], send_ref.at[target], sems.at[slot]).start()

    @pl.when(step == pl.num_programs(0) - 1)
    def _():
        def finish(slot, carry):
            target = targets[lax.rem(slot, 2), slot // 2]

            @pl.when(target >= 0)
            def _():
                pltpu.make_async_copy(staging.at[slot], send_ref.at[target], sems.at[slot]).wait()

            return carry

        lax.fori_loop(0, staging.shape[0], finish, 0)


def whole(array):
    zeros = (0,) * array.ndim
    return pl.BlockSpec(array.shape, lambda *_: zeros)


def one_layer(array, layer):
    rest = array.shape[1:]
    at = (layer,) + (0,) * len(rest)
    return pl.BlockSpec((None,) + rest, lambda *_: at)


def layer_scratch(n_heads, n_feat):
    square = pltpu.VMEM((n_feat, n_feat), BF16)
    return [pltpu.VMEM((8, WIN, 128), F32), square, square, square]


def first_layer(embedded, targets, temper, token, consts, params, devices, groups=8):
    n_heads, n_feat = consts[3].shape
    columns = embedded.shape[1] // (WIN * n_feat)
    side = jax.ShapeDtypeStruct((2, 32, n_feat), BF16)
    mid = jax.ShapeDtypeStruct((2 * columns, 32, n_feat), BF16)
    mid_spec = pl.BlockSpec((2 * groups, 32, n_feat), lambda g: (g, 0, 0))
    return pl.pallas_call(
        functools.partial(first_kernel, groups),
        grid=(columns // groups,),
        out_shape=(mid, mid, side, side, jax.ShapeDtypeStruct((devices, 96, 128), BF16)),
        in_specs=[SMEM, SMEM, pl.BlockSpec((2 * WIN, groups * WIN * n_feat), lambda g: (0, g))]
        + [whole(a) for a in (token,) + consts]
        + [one_layer(a, 0) for a in params],
        out_specs=(mid_spec, mid_spec, whole(side), whole(side), ANY),
        scratch_shapes=[pltpu.VMEM((CELLS, n_heads * CELLS), F32)]
        + layer_scratch(n_heads, n_feat)
        + [
            pltpu.VMEM((groups * 2 * CELLS, n_heads * CELLS), BF16),
            pltpu.VMEM((2 * columns, 96, 128), BF16),
            pltpu.SemaphoreType.DMA((2 * columns,)),
        ],
        compiler_params=pltpu.CompilerParams(vmem_limit_bytes=VMEM_BYTES),
        cost_estimate=pl.CostEstimate(flops=2 * 10**9, bytes_accessed=6 * 10**6, transcendentals=10**6),
        name="first_layer",
    )(targets, temper, embedded, token, *consts, *params)


def second_kernel(
    groups,
    place, temper, mid0_ref, mid1_ref, above_ref, below_ref, left_ref, right_ref,
    nw_ref, ne_ref, sw_ref, se_ref, coords_ref, heads_ref, ones_ref, mask_ref,
    net_in, net_first, net_out, qkv_ref, proj_ref, up_ref, down_ref, gain_ref,
    out_ref,
    bias_ref, strips_ref, q_w, k_w, v_w, ext, p_ref, sems,
):
    step = pl.program_id(0)
    n_heads, n_feat = mask_ref.shape
    n_half = mid0_ref.shape[0]
    row, col, last_row, last_col = place[0], place[1], place[2], place[3]

    @pl.when(step == 0)
    def _():
        inner = pl.ds(1, n_half)
        end = n_half + 1
        copies = [
            pltpu.make_async_copy(src, dst, sems.at[n])
            for n, (src, dst) in enumerate(
                [
                    (above_ref, ext.at[0, inner]),
                    (mid0_ref, ext.at[1, inner]),
                    (mid1_ref, ext.at[2, inner]),
                    (below_ref, ext.at[3, inner]),
                    (left_ref, ext.at[pl.ds(1, 2), 0]),
                    (right_ref, ext.at[pl.ds(1, 2), end]),
                    (nw_ref.at[1], ext.at[0, 0]),
                    (ne_ref.at[1], ext.at[0, end]),
                    (sw_ref.at[0], ext.at[3, 0]),
                    (se_ref.at[0], ext.at[3, end]),
                ]
            )
        ]
        for copy in copies:
            copy.start()
        for spare in range(n_half + 2, ext.shape[1]):
            ext[:, spare] = jnp.zeros((4, 32, n_feat), BF16)
        split_weights(qkv_ref, q_w, k_w, v_w)
        bias_strips(coords_ref, net_in, net_first, net_out, strips_ref)
        strips = [turned(strips_ref[h]) for h in range(n_heads)]
        lane = lax.broadcasted_iota(jnp.int32, (WIN, n_heads * CELLS), 1)
        upper = lax.broadcasted_iota(jnp.int32, (WIN, n_heads * CELLS), 0) < HALF
        other_rows = upper != (lane % WIN < HALF)
        top, bottom = row == 0, row == last_row
        edge_rows = other_rows & ((upper & top) | (~upper & bottom))
        for w in range(WIN):
            other_cols = (lane % CELLS >= CELLS // 2) != (w >= HALF)
            rows = slice(w * WIN, (w + 1) * WIN)
            bias = bias_rows(strips, w)
            away = -100.0 * LOG2E
            bias_ref[0, rows, :] = bias
            bias_ref[1, rows, :] = bias + jnp.where(other_cols, away, 0.0)
            bias_ref[2, rows, :] = bias + jnp.where(edge_rows, away, 0.0)
            bias_ref[3, rows, :] = bias + jnp.where(edge_rows | other_cols, away, 0.0)
        for copy in copies:
            copy.wait()

    first_half = 2 * groups * step
    upper = lax.broadcasted_iota(jnp.int32, (CELLS, n_feat), 0) % WIN < HALF

    def tile_of(line, group):
        return jnp.concatenate(
            [ext[line, first_half + 2 * group], ext[line, first_half + 2 * group + 1]], 0
        )

    own, around = [], []
    for group in range(groups):
        own += [tile_of(1, group), tile_of(2, group)]
        around.append(jnp.where(upper, tile_of(3, group), tile_of(0, group)))
    xb = jnp.concatenate(own, 0)
    xa = jnp.concatenate(around, 0)
    q = (unit_vectors(dot(xb, q_w[...]), heads_ref) * temper_row(temper, 1, mask_ref)).astype(BF16)
    keys = [unit_vectors(dot(t, k_w[...]), heads_ref).astype(BF16) for t in (xb, xa)]
    values = [dot(t, v_w[...]).astype(BF16) for t in (xb, xa)]

    def tiles(t, group):
        low = 2 * group * CELLS
        return t[low : low + CELLS], t[low + CELLS : low + 2 * CELLS]

    def three(parts, group):
        zero, one = tiles(parts[0], group)
        ring = parts[1][group * CELLS : (group + 1) * CELLS]
        return (
            jnp.where(upper, one, zero),
            jnp.where(upper, zero, ring),
            jnp.where(upper, ring, one),
        )

    upper_wide = lax.broadcasted_iota(jnp.int32, (CELLS, n_heads * CELLS), 0) % WIN < HALF
    for group in range(groups):
        zero, one = tiles(q, group)
        inside, over, under = three(keys, group)
        column = step * groups + group
        cut = ((column == 0) & (col == 0)) | ((column == n_half // 2) & (col == last_col))
        cut = cut.astype(jnp.int32)
        rows = slice(2 * group * CELLS, (2 * group + 1) * CELLS)
        scores = scores_of(jnp.where(upper, one, zero), inside, mask_ref)
        p_ref[rows, :] = jnp.exp2(scores + bias_ref[cut]).astype(BF16)
        edge = jnp.where(upper, zero, one)
        scores = jnp.where(
            upper_wide, scores_of(edge, over, mask_ref), scores_of(edge, under, mask_ref)
        )
        rows = slice((2 * group + 1) * CELLS, (2 * group + 2) * CELLS)
        p_ref[rows, :] = jnp.exp2(scores + bias_ref[2 + cut]).astype(BF16)
    totals = totals_of(p_ref[...], ones_ref)
    mixed = []
    for group in range(groups):
        inside, over, under = three(values, group)
        rows = slice(2 * group * CELLS, (2 * group + 1) * CELLS)
        middle = weighted(p_ref[rows, :], *spread_heads(inside, mask_ref)) / totals[rows]
        rows = slice((2 * group + 1) * CELLS, (2 * group + 2) * CELLS)
        p = p_ref[rows, :]
        edge = jnp.where(
            upper,
            weighted(p, *spread_heads(over, mask_ref)),
            weighted(p, *spread_heads(under, mask_ref)),
        ) / totals[rows]
        mixed += [jnp.where(upper, edge, middle), jnp.where(upper, middle, edge)]
    mixed = jnp.concatenate(mixed, 0)
    y = dense_tail(xb.astype(F32), mixed, proj_ref, up_ref, down_ref, gain_ref).astype(F32)

    for group in range(groups):
        zero, one = tiles(y, group)
        for half in range(2):
            slabs = []
            for w in range(half * HALF, (half + 1) * HALF):
                rows = slice(w * WIN, (w + 1) * WIN)
                slabs.append(jnp.concatenate([zero[rows], one[rows]], 0))
            strip = jnp.concatenate(slabs, 1).astype(BF16)
            at = first_half + 2 * group + half - 1

            @pl.when((at >= 0) & (at < n_half))
            def _(at=at, strip=strip):
                width = HALF * n_feat
                out_ref[:, pl.ds(pl.multiple_of(at * width, 128), width)] = strip


def second_layer(place, temper, pieces, consts, params, groups=6):
    n_heads, n_feat = consts[3].shape
    n_half = pieces[0].shape[0]
    steps = -(-(n_half // 2 + 1) // groups)
    out = jax.ShapeDtypeStruct((2 * WIN, n_half * HALF * n_feat), BF16)
    return pl.pallas_call(
        functools.partial(second_kernel, groups),
        grid=(steps,),
        out_shape=out,
        in_specs=[SMEM, SMEM]
        + [ANY] * len(pieces)
        + [whole(a) for a in consts]
        + [one_layer(a, 1) for a in params],
        out_specs=whole(out),
        scratch_shapes=[pltpu.VMEM((4, CELLS, n_heads * CELLS), F32)]
        + layer_scratch(n_heads, n_feat)
        + [
            pltpu.VMEM((4, 2 * groups * steps, 32, n_feat), BF16),
            pltpu.VMEM((groups * 2 * CELLS, n_heads * CELLS), BF16),
            pltpu.SemaphoreType.DMA((len(pieces),)),
        ],
        compiler_params=pltpu.CompilerParams(vmem_limit_bytes=VMEM_BYTES),
        cost_estimate=pl.CostEstimate(flops=3 * 10**9, bytes_accessed=6 * 10**6, transcendentals=10**6),
        name="second_layer",
    )(place, temper, *pieces, *consts, *params)


def pack_kernel(me, codes_ref, arrived_ref, out_ref, held, sems):
    slots = out_ref.shape[0]
    codes = codes_ref[...]
    sender = lax.broadcasted_iota(jnp.int32, codes.shape, 0)
    copies = []
    for slot in range(slots):
        hit = jnp.where(codes == me[0] * slots + slot, sender, 0).astype(F32)
        source = jnp.sum(hit).astype(jnp.int32)
        copies.append(pltpu.make_async_copy(arrived_ref.at[source], held.at[slot], sems.at[slot]))
        copies[-1].start()
    for copy in copies:
        copy.wait()
    lane = lax.broadcasted_iota(jnp.int32, (slots, 128), 1)

    def rows_of(at):
        return jnp.swapaxes(held[:, at : at + WIN, :].astype(F32), 0, 1)

    for pair in range(WIN // 2):
        even = rows_of(2 * pair * WIN)
        odd = rows_of((2 * pair + 1) * WIN)
        tails = rows_of(CELLS + pair * WIN)
        for u in range(WIN):
            moved = pltpu.roll(odd[u], 64, 1)
            joined = [
                even[u],
                jnp.where(lane < 64, tails[u], moved),
                jnp.where(lane < 64, moved, tails[u]),
            ]
            at = (u * WIN + 2 * pair) * 192
            out_ref[:, at : at + 384] = jnp.concatenate(joined, 1).astype(BF16)


def pack_rows(me, codes, arrived, slots, width):
    return pl.pallas_call(
        pack_kernel,
        out_shape=jax.ShapeDtypeStruct((slots, width), BF16),
        in_specs=[SMEM, pl.BlockSpec(memory_space=pltpu.VMEM), ANY],
        out_specs=pl.BlockSpec(memory_space=pltpu.VMEM),
        scratch_shapes=[
            pltpu.VMEM((slots,) + arrived.shape[1:], BF16),
            pltpu.SemaphoreType.DMA((slots,)),
        ],
        compiler_params=pltpu.CompilerParams(vmem_limit_bytes=VMEM_BYTES),
        name="pack_rows",
    )(me, codes, arrived)


def moved(block, rows, cols):
    n_row, n_col = lax.axis_size("row"), lax.axis_size("col")
    route = [
        (r * n_col + c, (r + rows) % n_row * n_col + (c + cols) % n_col)
        for r in range(n_row)
        for c in range(n_col)
    ]
    return lax.ppermute(block, ("row", "col"), route)


def local(
    embedded,
    window_target_device,
    window_device_slot,
    cloud_mask_token,
    query_key_value_weight,
    projection_weight,
    up_weight,
    down_weight,
    bias_net_input_weight,
    bias_net_first_bias,
    bias_net_output_weight,
    temper,
    norm_gain_values,
):
    n_row, n_col = lax.axis_size("row"), lax.axis_size("col")
    n_heads, n_feat = temper.shape[1], cloud_mask_token.shape[0]
    slots = window_target_device.size // 2
    row, col = lax.axis_index("row"), lax.axis_index("col")
    place = jnp.stack([row, col, n_row - 1, n_col - 1]).astype(jnp.int32)
    me = (row * n_col + col).astype(jnp.int32).reshape(1)
    consts = constants(n_heads, n_feat)
    params = (
        bias_net_input_weight,
        bias_net_first_bias[:, None, :],
        bias_net_output_weight,
        query_key_value_weight,
        projection_weight,
        up_weight,
        down_weight,
        norm_gain_values,
    )
    code = jnp.where(
        window_target_device >= 0, window_target_device * slots + window_device_slot, -1
    )
    codes = lax.all_gather(code.reshape(1, -1), ("row", "col"), axis=0, tiled=True)
    mid0, mid1, left, right, send = first_layer(
        embedded, window_target_device, temper, cloud_mask_token[None, :], consts, params, n_row * n_col
    )
    pieces = (
        mid0,
        mid1,
        moved(mid1, 1, 0),
        moved(mid0, -1, 0),
        moved(right, 0, 1),
        moved(left, 0, -1),
        moved(right, 1, 1),
        moved(left, 1, -1),
        moved(right, -1, 1),
        moved(left, -1, -1),
    )
    arrived = lax.all_to_all(send, ("row", "col"), split_axis=0, concat_axis=0, tiled=True)
    features = second_layer(place, temper, pieces, consts, params)
    packed = pack_rows(me, codes, arrived, slots, CELLS * n_feat)
    return features, packed


def solution(mesh):
    in_specs = (P("row", "col"),) * 3 + (P(),) * 10
    out_specs = (P("row", "col"), P(("row", "col"), None))
    return jax.shard_map(local, mesh=mesh, in_specs=in_specs, out_specs=out_specs, check_vma=False)
```

time: 271 us -> 150 us (0.55)
  matrix products: 110 us -> 0 us
  local copies, waits for them, and re-layouts: 55.2 us -> 8.83 us
  blocking collectives: 0 us -> 43.9 us
  Pallas kernels: 0 us -> 34.9 us
  other arithmetic: 21.5 us -> 0.62 us
  waiting for transfers between devices: 50 us -> 32 us
    dot_general x14 -> x0, matrix products: 110 us -> none  [the longest x2 32.3 us: swin_block(): reduced = jnp.dot(expanded, down_weight, preferred_element_type=jnp.float32)]
    all_gather x0 -> x1, blocking collectives: none -> 43.9 us  [local(): lax.all_gather(code.reshape(1, -1), ('row', 'col'), axis=0, tiled=True)]
    pallas_call x0 -> x3, Pallas kernels: none -> 34.9 us  [the longest x1 18.5 us: second_layer(): pl.pallas_call(functools.partial(second_kernel, groups), grid=(steps,), o...]
    reshape x8 -> x0, local copies, waits for them, and re-layouts: 20.6 us -> none  [the longest x2 12.6 us: swin_block(): triple = triple.reshape(n_windows, n_places, 3, n_heads, n_feat // n_heads)]
    ppermute x4 -> x8, waiting for transfers between devices: 50 us -> 32 us  [moved(): return lax.ppermute(block, ('row', 'col'), route)]
    slice x9 -> x0, local copies, waits for them, and re-layouts: 12.8 us -> none  [the longest x2 7.78 us: swin_block(): values_now = triple[:, :, 2]]
    all_to_all x2 -> x1, starting transfers between devices: 20.3 us -> 11.3 us  [local(): lax.all_to_all(send, ('row', 'col'), split_axis=0, concat_axis=0, tiled=T...]
    ppermute x4 -> x8, starting transfers between devices: 8.05 us -> 15.6 us  [moved(): return lax.ppermute(block, ('row', 'col'), route)]
  transfers between devices with their start and end apart: 6 -> 9, of which waited for: 3 -> 1; matrix products, arithmetic and copies ran while one was open for 66% -> 0% of each run, Pallas kernels for 0% -> 12%
where the time goes in v1:
time: 150 us; the launch traced here: 148 us
  blocking collectives  43.9 us (29%)
  Pallas kernels  34.9 us (23%)
  waiting for transfers between devices  32 us (21%)
  starting transfers between devices  26.9 us (18%)
  local copies, waits for them, and re-layouts  8.83 us (6%)
    all_gather x1, blocking collectives, local(): lax.all_gather(code.reshape(1, -1), ('row', 'col'), axis=0, tiled=True)  43.9 us
    ppermute x8, waiting for transfers between devices, moved(): return lax.ppermute(block, ('row', 'col'), route)  32 us
    pallas_call x1, Pallas kernels, second_layer(): pl.pallas_call(functools.partial(second_kernel, groups), grid=(steps,), o...  18.5 us
    ppermute x8, starting transfers between devices, moved(): return lax.ppermute(block, ('row', 'col'), route)  15.6 us
    pallas_call x1, Pallas kernels, first_layer(): pl.pallas_call(functools.partial(first_kernel, groups), grid=(columns //...  13.3 us
    all_to_all x1, starting transfers between devices, local(): lax.all_to_all(send, ('row', 'col'), split_axis=0, concat_axis=0, tiled=T...  11.3 us
    unnamed x25, local copies, waits for them, and re-layouts  6.3 us
    pallas_call x1, Pallas kernels, pack_rows(): pl.pallas_call(pack_kernel, out_shape=jax.ShapeDtypeStruct((slots, width)...  3.08 us
  transfers between devices with their start and end apart: 9, of which 1 were waited for; matrix products, arithmetic and copies ran while one was open for 0% of the time, Pallas kernels for 12%

profile of v1, /device:TPU:0, one launch (start us, length us, event | category | flops | bytes accessed | tf_op | source)
XLA Modules:
  0.0 148.0 jit_solution(6385301098987892647)
XLA Ops:
  0.6 2.2 %copy.25.down_ref = bf16[2,768,192]{2,1,0:T(8,128)(2,1)} copy(bf16[2,768,192]{1,2,0:T(8,128)(2,1)} %param.24) | data formatting | bytes 1179648 | tf_op args[7]
  2.9 1.8 %copy.24.net_out = f32[2,512,6]{2,1,0:T(8,128)} copy(f32[2,512,6]{1,0,2:T(2,128)} %param.27) | data formatting | bytes 49152 | tf_op args[10]
  4.6 1.3 broadcast_in_dim.11.net_first
  5.9 1.2 broadcast_in_dim.10.token_ref
  7.2 13.3 %first_layer.1 = (bf16[32,32,192]{2,1,0:T(8,128)(2,1)}, bf16[32,32,192]{2,1,0:T(8,128)(2,1)}, bf16[2,32,192]{2,1,0:T(8,128)(2,1)}, bf16[2,32,192]{2,1,0:T(8,128)(2,1)}, bf16[128,96,128]{2,1,0:T(8,128)(2,1)}) custom-call(s32[2,16]{1,0:T(2,128)} %targets.1, f32[2,6]{1,0:T(2,128)} %temper.3, bf16[16,24576]{1,0:T(8,128)(2,1)} %emb_ref.1, ...), custom_call_target="tpu_custom_call" | custom-call | flops 2000000000 | bytes 6000000 | tf_op jit(solution)/shard_map/first_layer/pallas_call | solution.py:264
  20.5 0.0 copy-start.6
  20.5 0.0 copy-start.4
  20.5 0.0 copy-start.1
  20.5 0.0 copy-start.2
  20.5 11.3 %all-to-all-start = ((bf16[128,96,128]{2,1,0:T(8,128)(2,1)}), bf16[128,96,128]{2,1,0:T(8,128)(2,1)S(1)}, u32[]{:S(2)}, u32[]{:S(2)}) async-start(bf16[128,96,128]{2,1,0:T(8,128)(2,1)} %get-tuple-element.11), calls=%async_computation | async-start | bytes 6291456 | tf_op jit(solution)/shard_map/all_to_all | solution.py:558
  31.8 0.0 collective-permute-start
  31.8 2.9 %collective-permute-start.1 = (bf16[32,32,192]{2,1,0:T(8,128)(2,1)}, bf16[32,32,192]{2,1,0:T(8,128)(2,1)}, u32[]{:S(2)}, u32[]{:S(2)}) collective-permute-start(bf16[32,32,192]{2,1,0:T(8,128)(2,1)} %get-tuple-element.7.mid0_ref), channel_id=1, source_target_pairs={{0,112},{1,113},{2,114},{3,115},{4,116},{5,117},{6,118},{7,119},{8... | collective-permute-start | bytes 1179656 | tf_op jit(solution)/shard_map/ppermute | solution.py:504
  34.8 0.0 copy-done.6
  34.8 1.0 collective-permute-start.2
  35.7 0.0 collective-permute-start.4
  35.7 0.0 copy-done.4
  35.7 4.4 %collective-permute-start.3 = (bf16[2,32,192]{2,1,0:T(8,128)(2,1)S(1)}, bf16[2,32,192]{2,1,0:T(8,128)(2,1)S(1)}, u32[]{:S(2)}, u32[]{:S(2)}) collective-permute-start(bf16[2,32,192]{2,1,0:T(8,128)(2,1)S(1)} %copy-done.4), channel_id=1, source_target_pairs={{0,15},{1,0},{2,1},{3,2},{4,3},{5,4},{6,5},{7,6},{8,7},{9,8},{10,9... | collective-permute-start | bytes 73736 | tf_op jit(solution)/shard_map/ppermute | solution.py:504
  40.1 0.0 copy-done.1
  40.1 0.0 copy-done.2
  40.1 31.9 %collective-permute-done.2.left_ref = bf16[2,32,192]{2,1,0:T(8,128)(2,1)S(1)} collective-permute-done((bf16[2,32,192]{2,1,0:T(8,128)(2,1)S(1)}, bf16[2,32,192]{2,1,0:T(8,128)(2,1)S(1)}, u32[]{:S(2)}, u32[]{:S(2)}) %collective-permute-start.2) | collective-permute-done | bytes 24608 | tf_op jit(solution)/shard_map/ppermute | solution.py:504
  72.1 0.0 copy-start.3
  72.1 0.0 collective-permute-start.5
  72.1 0.0 collective-permute-done.3.right_ref
  72.1 0.0 copy-start.7
  72.1 3.8 %collective-permute-start.6 = (bf16[2,32,192]{2,1,0:T(8,128)(2,1)S(1)}, bf16[2,32,192]{2,1,0:T(8,128)(2,1)S(1)}, u32[]{:S(2)}, u32[]{:S(2)}) collective-permute-start(bf16[2,32,192]{2,1,0:T(8,128)(2,1)S(1)} %copy-done.6), channel_id=1, source_target_pairs={{0,113},{1,114},{2,115},{3,116},{4,117},{5,118},{6,119},{7,120},{8... | collective-permute-start | bytes 73736 | tf_op jit(solution)/shard_map/ppermute | solution.py:504
  75.9 0.0 collective-permute-done.4.nw_ref
  75.9 0.0 copy-start.5
  75.9 3.5 %collective-permute-start.7 = (bf16[2,32,192]{2,1,0:T(8,128)(2,1)S(1)}, bf16[2,32,192]{2,1,0:T(8,128)(2,1)S(1)}, u32[]{:S(2)}, u32[]{:S(2)}) collective-permute-start(bf16[2,32,192]{2,1,0:T(8,128)(2,1)S(1)} %copy-done.4), channel_id=1, source_target_pairs={{0,127},{1,112},{2,113},{3,114},{4,115},{5,116},{6,117},{7,118},{8... | collective-permute-start | bytes 73736 | tf_op jit(solution)/shard_map/ppermute | solution.py:504
  79.4 0.6 pad_add_fusion.place
  80.0 0.1 reshape.12
  80.1 43.9 %all-gather = s32[128,1,32]{2,1,0:T(1,128)} all-gather(s32[1,1,32]{2,1,0:T(1,128)S(1)} %reshape.12), channel_id=1, replica_groups=mesh['row'=8,'col'=16] {'row','col'}, dimensions={0}, use_global_device_ids=true | all-gather | bytes 16512 | tf_op jit(solution)/shard_map/all_gather | solution.py:542
  124.0 0.0 collective-permute-done.5.ne_ref
  124.0 0.0 copy-start.8
  124.0 0.0 collective-permute-done.6.sw_ref
  124.0 0.0 copy-start.9
  124.0 0.0 collective-permute-done.7.se_ref
  124.0 0.0 copy-start.10
  124.0 0.0 collective-permute-done.above_ref
  124.0 0.0 collective-permute-done.1.below_ref
  124.0 0.0 copy-done.3
  124.0 0.0 copy-done.7
  124.1 0.0 copy-done.5
  124.1 0.5 copy-done.8
  124.6 0.0 copy-done.9
  124.6 0.0 copy-done.10
  124.6 18.5 %second_layer.1 = bf16[16,24576]{1,0:T(8,128)(2,1)} custom-call(s32[4]{0:T(128)} %pad_add_fusion.place, f32[2,6]{1,0:T(2,128)} %temper.3, bf16[32,32,192]{2,1,0:T(8,128)(2,1)} %get-tuple-element.7.mid0_ref, bf16[32,32,192]{2,1,0:T(8,128)(2,1)} %get-tuple-element.8.mid1_ref, bf16[32,32,192]{2,1,0:T(8,128)(2,1)} %collective-permute-done.above_ref, ...), custom_call_target="tpu_custom_call" | custom-call | flops 3000000000 | bytes 6000000 | tf_op jit(solution)/shard_map/second_layer/pallas_call | solution.py:428
  143.1 0.0 all-to-all-done.arrived_ref
  143.1 0.0 copy-start
  143.1 1.6 %copy-done = bf16[128,96,128]{2,1,0:T(8,128)(2,1)} copy-done((bf16[128,96,128]{2,1,0:T(8,128)(2,1)}, bf16[128,96,128]{2,1,0:T(8,128)(2,1)S(1)}, u32[]{:S(2)}) %copy-start) | copy-done | bytes 3145752
  144.7 3.1 %pack_rows.1 = bf16[16,12288]{1,0:T(8,128)(2,1)} custom-call(s32[1]{0:T(128)} %bitcast.2.me, s32[128,32]{1,0:T(8,128)} %bitcast.4, bf16[128,96,128]{2,1,0:T(8,128)(2,1)} %copy-done), custom_call_target="tpu_custom_call" | custom-call | tf_op jit(solution)/shard_map/pack_rows/pallas_call | solution.py:483
  (1 shorter events, 0.0 us)
Async XLA Ops:
  20.5 14.3 %copy-start.6 = (bf16[2,32,192]{2,1,0:T(8,128)(2,1)S(1)}, bf16[2,32,192]{2,1,0:T(8,128)(2,1)}, u32[]{:S(2)}) copy-start(bf16[2,32,192]{2,1,0:T(8,128)(2,1)} %get-tuple-element.9) | copy-start | bytes 73732
  20.5 15.2 %copy-start.4 = (bf16[2,32,192]{2,1,0:T(8,128)(2,1)S(1)}, bf16[2,32,192]{2,1,0:T(8,128)(2,1)}, u32[]{:S(2)}) copy-start(bf16[2,32,192]{2,1,0:T(8,128)(2,1)} %get-tuple-element.10) | copy-start | bytes 73732
  20.5 19.6 %copy-start.1 = (s32[2,16]{1,0:T(2,128)S(1)}, s32[2,16]{1,0:T(2,128)}, u32[]{:S(2)}) copy-start(s32[2,16]{1,0:T(2,128)} %targets.1) | copy-start | bytes 388
  20.5 19.6 %copy-start.2 = (s32[2,16]{1,0:T(2,128)S(1)}, s32[2,16]{1,0:T(2,128)}, u32[]{:S(2)}) copy-start(s32[2,16]{1,0:T(2,128)} %param.19) | copy-start | bytes 388
  20.5 122.6 %all-to-all-start = ((bf16[128,96,128]{2,1,0:T(8,128)(2,1)}), bf16[128,96,128]{2,1,0:T(8,128)(2,1)S(1)}, u32[]{:S(2)}, u32[]{:S(2)}) async-start(bf16[128,96,128]{2,1,0:T(8,128)(2,1)} %get-tuple-element.11), calls=%async_computation | async-start | bytes 6291456 | tf_op jit(solution)/shard_map/all_to_all | solution.py:558
  31.8 92.2 %collective-permute-start = (bf16[32,32,192]{2,1,0:T(8,128)(2,1)}, bf16[32,32,192]{2,1,0:T(8,128)(2,1)}, u32[]{:S(2)}, u32[]{:S(2)}) collective-permute-start(bf16[32,32,192]{2,1,0:T(8,128)(2,1)} %get-tuple-element.8.mid1_ref), channel_id=1, source_target_pairs={{0,16},{1,17},{2,18},{3,19},{4,20},{5,21},{6,22},{7,23},{8,24},{9,... | collective-permute-start | bytes 1179656 | tf_op jit(solution)/shard_map/ppermute | solution.py:504
  31.8 92.2 %collective-permute-start.1 = (bf16[32,32,192]{2,1,0:T(8,128)(2,1)}, bf16[32,32,192]{2,1,0:T(8,128)(2,1)}, u32[]{:S(2)}, u32[]{:S(2)}) collective-permute-start(bf16[32,32,192]{2,1,0:T(8,128)(2,1)} %get-tuple-element.7.mid0_ref), channel_id=1, source_target_pairs={{0,112},{1,113},{2,114},{3,115},{4,116},{5,117},{6,118},{7,119},{8... | collective-permute-start | bytes 1179656 | tf_op jit(solution)/shard_map/ppermute | solution.py:504
  34.8 37.3 %collective-permute-start.2 = (bf16[2,32,192]{2,1,0:T(8,128)(2,1)S(1)}, bf16[2,32,192]{2,1,0:T(8,128)(2,1)S(1)}, u32[]{:S(2)}, u32[]{:S(2)}) collective-permute-start(bf16[2,32,192]{2,1,0:T(8,128)(2,1)S(1)} %copy-done.6), channel_id=1, source_target_pairs={{0,1},{1,2},{2,3},{3,4},{4,5},{5,6},{6,7},{7,8},{8,9},{9,10},{10,1... | collective-permute-start | bytes 73736 | tf_op jit(solution)/shard_map/ppermute | solution.py:504
  35.7 40.2 %collective-permute-start.4 = (bf16[2,32,192]{2,1,0:T(8,128)(2,1)S(1)}, bf16[2,32,192]{2,1,0:T(8,128)(2,1)S(1)}, u32[]{:S(2)}, u32[]{:S(2)}) collective-permute-start(bf16[2,32,192]{2,1,0:T(8,128)(2,1)S(1)} %copy-done.6), channel_id=1, source_target_pairs={{0,17},{1,18},{2,19},{3,20},{4,21},{5,22},{6,23},{7,24},{8,25},{9,... | collective-permute-start | bytes 73736 | tf_op jit(solution)/shard_map/ppermute | solution.py:504
  35.7 36.4 %collective-permute-start.3 = (bf16[2,32,192]{2,1,0:T(8,128)(2,1)S(1)}, bf16[2,32,192]{2,1,0:T(8,128)(2,1)S(1)}, u32[]{:S(2)}, u32[]{:S(2)}) collective-permute-start(bf16[2,32,192]{2,1,0:T(8,128)(2,1)S(1)} %copy-done.4), channel_id=1, source_target_pairs={{0,15},{1,0},{2,1},{3,2},{4,3},{5,4},{6,5},{7,6},{8,7},{9,8},{10,9... | collective-permute-start | bytes 73736 | tf_op jit(solution)/shard_map/ppermute | solution.py:504
  72.1 52.0 %copy-start.3 = (bf16[2,32,192]{2,1,0:T(8,128)(2,1)}, bf16[2,32,192]{2,1,0:T(8,128)(2,1)S(1)}, u32[]{:S(2)}) copy-start(bf16[2,32,192]{2,1,0:T(8,128)(2,1)S(1)} %collective-permute-done.2.left_ref) | copy-start | bytes 73732
  72.1 51.9 %collective-permute-start.5 = (bf16[2,32,192]{2,1,0:T(8,128)(2,1)S(1)}, bf16[2,32,192]{2,1,0:T(8,128)(2,1)S(1)}, u32[]{:S(2)}, u32[]{:S(2)}) collective-permute-start(bf16[2,32,192]{2,1,0:T(8,128)(2,1)S(1)} %copy-done.4), channel_id=1, source_target_pairs={{0,31},{1,16},{2,17},{3,18},{4,19},{5,20},{6,21},{7,22},{8,23},{9,... | collective-permute-start | bytes 73736 | tf_op jit(solution)/shard_map/ppermute | solution.py:504
  72.1 52.0 %copy-start.7 = (bf16[2,32,192]{2,1,0:T(8,128)(2,1)}, bf16[2,32,192]{2,1,0:T(8,128)(2,1)S(1)}, u32[]{:S(2)}) copy-start(bf16[2,32,192]{2,1,0:T(8,128)(2,1)S(1)} %collective-permute-done.3.right_ref) | copy-start | bytes 73732
  72.1 51.9 %collective-permute-start.6 = (bf16[2,32,192]{2,1,0:T(8,128)(2,1)S(1)}, bf16[2,32,192]{2,1,0:T(8,128)(2,1)S(1)}, u32[]{:S(2)}, u32[]{:S(2)}) collective-permute-start(bf16[2,32,192]{2,1,0:T(8,128)(2,1)S(1)} %copy-done.6), channel_id=1, source_target_pairs={{0,113},{1,114},{2,115},{3,116},{4,117},{5,118},{6,119},{7,120},{8... | collective-permute-start | bytes 73736 | tf_op jit(solution)/shard_map/ppermute | solution.py:504
  75.9 48.1 %copy-start.5 = (bf16[2,32,192]{2,1,0:T(8,128)(2,1)}, bf16[2,32,192]{2,1,0:T(8,128)(2,1)S(1)}, u32[]{:S(2)}) copy-start(bf16[2,32,192]{2,1,0:T(8,128)(2,1)S(1)} %collective-permute-done.4.nw_ref) | copy-start | bytes 73732
  75.9 48.1 %collective-permute-start.7 = (bf16[2,32,192]{2,1,0:T(8,128)(2,1)S(1)}, bf16[2,32,192]{2,1,0:T(8,128)(2,1)S(1)}, u32[]{:S(2)}, u32[]{:S(2)}) collective-permute-start(bf16[2,32,192]{2,1,0:T(8,128)(2,1)S(1)} %copy-done.4), channel_id=1, source_target_pairs={{0,127},{1,112},{2,113},{3,114},{4,115},{5,116},{6,117},{7,118},{8... | collective-permute-start | bytes 73736 | tf_op jit(solution)/shard_map/ppermute | solution.py:504
  124.0 0.6 copy-start.8
  124.0 0.6 copy-start.9
  124.0 0.6 copy-start.10
  143.1 1.7 %copy-start = (bf16[128,96,128]{2,1,0:T(8,128)(2,1)}, bf16[128,96,128]{2,1,0:T(8,128)(2,1)S(1)}, u32[]{:S(2)}) copy-start(bf16[128,96,128]{2,1,0:T(8,128)(2,1)S(1)} %all-to-all-done.arrived_ref) | copy-start | bytes 9437188

commit v2 on v1

--- a/solution.py
+++ b/solution.py
@@ -58,10 +58,10 @@
 def bias_strips(coords_ref, net_in, net_first, net_out, strips_ref):
     coords = coords_ref[...]
     units = jnp.maximum(
-        coords[:, 0:1] * net_in[0:1, :] + coords[:, 1:2] * net_in[1:2, :] + net_first[...], 0.0
+        coords[:, 0:1] * net_in[0:1, :] + coords[:, 1:2] * net_in[1:2, :] + net_first, 0.0
     )
     logits = lax.dot_general(
-        net_out[...], units, (((0,), (1,)), ((), ())),
+        net_out, units, (((1,), (1,)), ((), ())),
         precision=lax.Precision.HIGHEST, preferred_element_type=F32,
     )
     n_heads = logits.shape[0]
@@ -139,7 +139,7 @@
     hidden = (x + layer_norm(attended, gain_ref[0:1, :])).astype(BF16)
     raised = dot(hidden, up_ref[...])
     expanded = (0.5 * raised * (1.0 + lax.erf(raised * math.sqrt(0.5)))).astype(BF16)
-    reduced = dot(expanded, down_ref[...])
+    reduced = dot_nt(expanded, down_ref[...])
     return (hidden.astype(F32) + layer_norm(reduced, gain_ref[1:2, :])).astype(BF16)
 
 
@@ -150,19 +150,52 @@
     v_w[...] = qkv_ref[:, 2 * n_feat :]
 
 
+def half_rows(tile, lower):
+    first = lax.broadcasted_iota(jnp.int32, (WIN, tile.shape[1]), 0) < HALF
+    pairs = []
+    for pair in range(2):
+        even = tile[2 * pair * WIN : (2 * pair + 1) * WIN]
+        odd = tile[(2 * pair + 1) * WIN : (2 * pair + 2) * WIN]
+        if lower:
+            pairs.append(jnp.where(first, pltpu.roll(even, HALF, 0), odd))
+        else:
+            pairs.append(jnp.where(first, even, pltpu.roll(odd, HALF, 0)))
+    return jnp.concatenate(pairs, 0)
+
+
+def ring_tile(upper, lower):
+    first = lax.broadcasted_iota(jnp.int32, (WIN, upper.shape[1]), 0) < HALF
+    tiles = []
+    for pair in range(2):
+        rows = slice(pair * WIN, (pair + 1) * WIN)
+        up, low = upper[rows], lower[rows]
+        tiles.append(jnp.where(first, up, pltpu.roll(low, HALF, 0)))
+        tiles.append(jnp.where(first, pltpu.roll(up, HALF, 0), low))
+    return jnp.concatenate(tiles, 0)
+
+
 def first_kernel(
     groups,
-    targets, temper, emb_ref, token_ref, coords_ref, heads_ref, ones_ref, mask_ref,
+    targets, slots, temper, emb_ref, token_ref, coords_ref, heads_ref, ones_ref, mask_ref,
     net_in, net_first, net_out, qkv_ref, proj_ref, up_ref, down_ref, gain_ref,
-    mid0_ref, mid1_ref, left_ref, right_ref, send_ref,
-    bias_ref, strips_ref, q_w, k_w, v_w, p_ref, staging, sems,
+    mid0_ref, mid1_ref, upper_ref, lower_ref, left_ref, right_ref, send_ref,
+    bias_ref, strips_ref, q_w, k_w, v_w, p_ref, staging, blank, sems, blank_sems,
 ):
     step = pl.program_id(0)
     n_heads, n_feat = mask_ref.shape
 
+    n_blank = blank.shape[0]
+    blanks = [
+        pltpu.make_async_copy(blank, send_ref.at[pl.ds(n * n_blank, n_blank)], blank_sems.at[n])
+        for n in range(send_ref.shape[0] // n_blank)
+    ]
+
     @pl.when(step == 0)
     def _():
-        bias_strips(coords_ref, net_in, net_first, net_out, strips_ref)
+        blank[...] = jnp.full(blank.shape, -1.0, BF16)
+        for copy in blanks:
+            copy.start()
+        bias_strips(coords_ref, net_in, net_first[0:1, :], net_out[:, 0, :], strips_ref)
         strips = [strips_ref[h] for h in range(n_heads)]
         for w in range(WIN):
             bias_ref[w * WIN : (w + 1) * WIN, :] = bias_rows(strips, w)
@@ -190,36 +223,50 @@
         rows = slice(n * CELLS, (n + 1) * CELLS)
         mixed.append(weighted(p_ref[rows, :], *spread_heads(v[rows], mask_ref)))
     mixed = jnp.concatenate(mixed, 0) / totals_of(p_ref[...], ones_ref)
+
+    @pl.when(step == 0)
+    def _():
+        for copy in blanks:
+            copy.wait()
+
     y = dense_tail(x, mixed, proj_ref, up_ref, down_ref, gain_ref).astype(F32)
 
-    token = token_ref[...].astype(F32)
+    token = token_ref[...].astype(F32).reshape(1, n_feat)
     for group in range(groups):
         for i in range(2):
             n = 2 * group + i
             j = step * groups + group
             target = targets[i, j]
             tile = y[n * CELLS : (n + 1) * CELLS]
-            kept = jnp.where(target >= 0, tile, token).astype(BF16)
+            kept = jnp.where(target >= 0, tile, token)
+            rows = kept.astype(BF16)
             mid = (mid0_ref, mid1_ref)[i]
-            mid[2 * group] = kept[:32]
-            mid[2 * group + 1] = kept[32:]
+            mid[2 * group] = rows[:32]
+            mid[2 * group + 1] = rows[32:]
+            halves = [half_rows(kept[half * 32 : (half + 1) * 32], i).astype(BF16) for half in range(2)]
+            outward = (upper_ref, lower_ref)[i]
+            outward[1 + 2 * j] = halves[0]
+            outward[2 + 2 * j] = halves[1]
             if group == 0:
 
                 @pl.when(step == 0)
-                def _(i=i, kept=kept):
-                    left_ref[i] = kept[:32]
+                def _(i=i, rows=rows, halves=halves):
+                    left_ref[i * 32 : (i + 1) * 32] = rows[:32]
+                    left_ref[64 + i * 16 : 80 + i * 16] = halves[0]
 
             if group == groups - 1:
 
                 @pl.when(step == pl.num_programs(0) - 1)
-                def _(i=i, kept=kept):
-                    right_ref[i] = kept[32:]
+                def _(i=i, rows=rows, halves=halves):
+                    right_ref[i * 32 : (i + 1) * 32] = rows[32:]
+                    right_ref[64 + i * 16 : 80 + i * 16] = halves[1]
 
             slot = j * 2 + i
             staging[slot, :64] = tile[:, :128].astype(BF16)
             tails = tile[:, 128:].reshape(4, 2, WIN, 64)
             joined = jnp.concatenate([tails[:, 0], tails[:, 1]], -1)
-            staging[slot, 64:] = joined.reshape(32, 128).astype(BF16)
+            staging[slot, 64:96] = joined.reshape(32, 128).astype(BF16)
+            staging[slot, 96:] = jnp.full((8, 128), slots[i, j].astype(F32)).astype(BF16)
 
             @pl.when(target >= 0)
             def _(slot=slot, target=target):
@@ -244,7 +291,9 @@
     return pl.BlockSpec(array.shape, lambda *_: zeros)
 
 
-def one_layer(array, layer):
+def layer_spec(array, position, layer):
+    if position in (1, 2):
+        return whole(array)
     rest = array.shape[1:]
     at = (layer,) + (0,) * len(rest)
     return pl.BlockSpec((None,) + rest, lambda *_: at)
@@ -255,40 +304,71 @@
     return [pltpu.VMEM((8, WIN, 128), F32), square, square, square]
 
 
-def first_layer(embedded, targets, temper, token, consts, params, devices, groups=8):
+def first_layer(embedded, targets, slots, temper, token, consts, params, devices, groups=8):
     n_heads, n_feat = consts[3].shape
     columns = embedded.shape[1] // (WIN * n_feat)
-    side = jax.ShapeDtypeStruct((2, 32, n_feat), BF16)
+    side = jax.ShapeDtypeStruct((96, n_feat), BF16)
+    outward = jax.ShapeDtypeStruct((2 * columns + 2, 16, n_feat), BF16)
     mid = jax.ShapeDtypeStruct((2 * columns, 32, n_feat), BF16)
     mid_spec = pl.BlockSpec((2 * groups, 32, n_feat), lambda g: (g, 0, 0))
     return pl.pallas_call(
         functools.partial(first_kernel, groups),
         grid=(columns // groups,),
-        out_shape=(mid, mid, side, side, jax.ShapeDtypeStruct((devices, 96, 128), BF16)),
-        in_specs=[SMEM, SMEM, pl.BlockSpec((2 * WIN, groups * WIN * n_feat), lambda g: (0, g))]
+        out_shape=(mid, mid, outward, outward, side, side, jax.ShapeDtypeStruct((devices, 104, 128), BF16)),
+        in_specs=[SMEM, SMEM, SMEM, pl.BlockSpec((2 * WIN, groups * WIN * n_feat), lambda g: (0, g))]
         + [whole(a) for a in (token,) + consts]
-        + [one_layer(a, 0) for a in params],
-        out_specs=(mid_spec, mid_spec, whole(side), whole(side), ANY),
+        + [layer_spec(a, n, 0) for n, a in enumerate(params)],
+        out_specs=(mid_spec, mid_spec, whole(outward), whole(outward), whole(side), whole(side), ANY),
         scratch_shapes=[pltpu.VMEM((CELLS, n_heads * CELLS), F32)]
         + layer_scratch(n_heads, n_feat)
         + [
             pltpu.VMEM((groups * 2 * CELLS, n_heads * CELLS), BF16),
-            pltpu.VMEM((2 * columns, 96, 128), BF16),
+            pltpu.VMEM((2 * columns, 104, 128), BF16),
+            pltpu.VMEM((devices // 8, 104, 128), BF16),
             pltpu.SemaphoreType.DMA((2 * columns,)),
+            pltpu.SemaphoreType.DMA((8,)),
         ],
         compiler_params=pltpu.CompilerParams(vmem_limit_bytes=VMEM_BYTES),
         cost_estimate=pl.CostEstimate(flops=2 * 10**9, bytes_accessed=6 * 10**6, transcendentals=10**6),
         name="first_layer",
-    )(targets, temper, embedded, token, *consts, *params)
+    )(targets, slots, temper, embedded, token, *consts, *params)
+
+
+def corner_kernel(left_ref, right_ref, up_in, low_in, up_ref, low_ref, sems):
+    del up_in, low_in
+    end = up_ref.shape[0] - 1
+    copies = [
+        pltpu.make_async_copy(left_ref.at[pl.ds(64, 16)], up_ref.at[0], sems.at[0]),
+        pltpu.make_async_copy(right_ref.at[pl.ds(64, 16)], up_ref.at[end], sems.at[1]),
+        pltpu.make_async_copy(left_ref.at[pl.ds(80, 16)], low_ref.at[0], sems.at[2]),
+        pltpu.make_async_copy(right_ref.at[pl.ds(80, 16)], low_ref.at[end], sems.at[3]),
+    ]
+    for copy in copies:
+        copy.start()
+    for copy in copies:
+        copy.wait()
+
+
+def add_corners(left, right, upper, lower):
+    shape = jax.ShapeDtypeStruct(upper.shape, upper.dtype)
+    return pl.pallas_call(
+        corner_kernel,
+        out_shape=(shape, shape),
+        in_specs=[ANY] * 4,
+        out_specs=(ANY, ANY),
+        scratch_shapes=[pltpu.SemaphoreType.DMA((4,))],
+        input_output_aliases={2: 0, 3: 1},
+        name="add_corners",
+    )(left, right, upper, lower)
 
 
 def second_kernel(
     groups,
     place, temper, mid0_ref, mid1_ref, above_ref, below_ref, left_ref, right_ref,
-    nw_ref, ne_ref, sw_ref, se_ref, coords_ref, heads_ref, ones_ref, mask_ref,
+    coords_ref, heads_ref, ones_ref, mask_ref,
     net_in, net_first, net_out, qkv_ref, proj_ref, up_ref, down_ref, gain_ref,
     out_ref,
-    bias_ref, strips_ref, q_w, k_w, v_w, ext, p_ref, sems,
+    bias_ref, strips_ref, q_w, k_w, v_w, ext, upper_ring, lower_ring, p_ref, sems,
 ):
     step = pl.program_id(0)
     n_heads, n_feat = mask_ref.shape
@@ -297,31 +377,31 @@
 
     @pl.when(step == 0)
     def _():
-        inner = pl.ds(1, n_half)
+        inner, every = pl.ds(1, n_half), pl.ds(0, n_half + 2)
         end = n_half + 1
         copies = [
             pltpu.make_async_copy(src, dst, sems.at[n])
             for n, (src, dst) in enumerate(
                 [
-                    (above_ref, ext.at[0, inner]),
-                    (mid0_ref, ext.at[1, inner]),
-                    (mid1_ref, ext.at[2, inner]),
-                    (below_ref, ext.at[3, inner]),
-                    (left_ref, ext.at[pl.ds(1, 2), 0]),
-                    (right_ref, ext.at[pl.ds(1, 2), end]),
-                    (nw_ref.at[1], ext.at[0, 0]),
-                    (ne_ref.at[1], ext.at[0, end]),
-                    (sw_ref.at[0], ext.at[3, 0]),
-                    (se_ref.at[0], ext.at[3, end]),
+                    (mid0_ref, ext.at[0, inner]),
+                    (mid1_ref, ext.at[1, inner]),
+                    (left_ref.at[pl.ds(0, 32)], ext.at[0, 0]),
+                    (left_ref.at[pl.ds(32, 32)], ext.at[1, 0]),
+                    (right_ref.at[pl.ds(0, 32)], ext.at[0, end]),
+                    (right_ref.at[pl.ds(32, 32)], ext.at[1, end]),
+                    (above_ref, lower_ring.at[every]),
+                    (below_ref, upper_ring.at[every]),
                 ]
             )
         ]
         for copy in copies:
             copy.start()
         for spare in range(n_half + 2, ext.shape[1]):
-            ext[:, spare] = jnp.zeros((4, 32, n_feat), BF16)
+            ext[:, spare] = jnp.zeros((2, 32, n_feat), BF16)
+            upper_ring[spare] = jnp.zeros((16, n_feat), BF16)
+            lower_ring[spare] = jnp.zeros((16, n_feat), BF16)
         split_weights(qkv_ref, q_w, k_w, v_w)
-        bias_strips(coords_ref, net_in, net_first, net_out, strips_ref)
+        bias_strips(coords_ref, net_in, net_first[1:2, :], net_out[:, 1, :], strips_ref)
         strips = [turned(strips_ref[h]) for h in range(n_heads)]
         lane = lax.broadcasted_iota(jnp.int32, (WIN, n_heads * CELLS), 1)
         upper = lax.broadcasted_iota(jnp.int32, (WIN, n_heads * CELLS), 0) < HALF
@@ -350,8 +430,12 @@
 
     own, around = [], []
     for group in range(groups):
-        own += [tile_of(1, group), tile_of(2, group)]
-        around.append(jnp.where(upper, tile_of(3, group), tile_of(0, group)))
+        own += [tile_of(0, group), tile_of(1, group)]
+        for half in range(2):
+            at = first_half + 2 * group + half
+            around.append(
+                ring_tile(upper_ring[at].astype(F32), lower_ring[at].astype(F32)).astype(BF16)
+            )
     xb = jnp.concatenate(own, 0)
     xa = jnp.concatenate(around, 0)
     q = (unit_vectors(dot(xb, q_w[...]), heads_ref) * temper_row(temper, 1, mask_ref)).astype(BF16)
@@ -432,37 +516,46 @@
         in_specs=[SMEM, SMEM]
         + [ANY] * len(pieces)
         + [whole(a) for a in consts]
-        + [one_layer(a, 1) for a in params],
+        + [layer_spec(a, n, 1) for n, a in enumerate(params)],
         out_specs=whole(out),
         scratch_shapes=[pltpu.VMEM((4, CELLS, n_heads * CELLS), F32)]
         + layer_scratch(n_heads, n_feat)
         + [
-            pltpu.VMEM((4, 2 * groups * steps, 32, n_feat), BF16),
+            pltpu.VMEM((2, 2 * groups * steps, 32, n_feat), BF16),
+            pltpu.VMEM((2 * groups * steps, 16, n_feat), BF16),
+            pltpu.VMEM((2 * groups * steps, 16, n_feat), BF16),
             pltpu.VMEM((groups * 2 * CELLS, n_heads * CELLS), BF16),
-            pltpu.SemaphoreType.DMA((len(pieces),)),
+            pltpu.SemaphoreType.DMA((8,)),
         ],
         compiler_params=pltpu.CompilerParams(vmem_limit_bytes=VMEM_BYTES),
-        cost_estimate=pl.CostEstimate(flops=3 * 10**9, bytes_accessed=6 * 10**6, transcendentals=10**6),
+        cost_estimate=pl.CostEstimate(flops=10**11, bytes_accessed=10**7, transcendentals=10**6),
         name="second_layer",
     )(place, temper, *pieces, *consts, *params)
 
 
-def pack_kernel(me, codes_ref, arrived_ref, out_ref, held, sems):
+def pack_kernel(entries_ref, out_ref, arrived_ref, sems):
     slots = out_ref.shape[0]
-    codes = codes_ref[...]
-    sender = lax.broadcasted_iota(jnp.int32, codes.shape, 0)
-    copies = []
-    for slot in range(slots):
-        hit = jnp.where(codes == me[0] * slots + slot, sender, 0).astype(F32)
-        source = jnp.sum(hit).astype(jnp.int32)
-        copies.append(pltpu.make_async_copy(arrived_ref.at[source], held.at[slot], sems.at[slot]))
-        copies[-1].start()
+    part = arrived_ref.shape[0] // 8
+    copies = [
+        pltpu.make_async_copy(
+            entries_ref.at[pl.ds(n * part, part)], arrived_ref.at[pl.ds(n * part, part)], sems.at[n]
+        )
+        for n in range(8)
+    ]
+    for copy in copies:
+        copy.start()
     for copy in copies:
         copy.wait()
+    marks = arrived_ref[:, 96:, :].astype(F32)
+    lane = lax.broadcasted_iota(jnp.int32, marks.shape, 2).astype(F32)
+    sender = lax.broadcasted_iota(jnp.int32, marks.shape, 0).astype(F32)
+    found = jnp.max(jnp.where(marks == lane, sender, 0.0), 0).astype(jnp.int32)
+    sources = [found[0, slot] for slot in range(slots)]
     lane = lax.broadcasted_iota(jnp.int32, (slots, 128), 1)
 
     def rows_of(at):
-        return jnp.swapaxes(held[:, at : at + WIN, :].astype(F32), 0, 1)
+        rows = [arrived_ref[source, at : at + WIN, :].astype(F32) for source in sources]
+        return jnp.swapaxes(jnp.stack(rows, 0), 0, 1)
 
     for pair in range(WIN // 2):
         even = rows_of(2 * pair * WIN)
@@ -479,19 +572,16 @@
             out_ref[:, at : at + 384] = jnp.concatenate(joined, 1).astype(BF16)
 
 
-def pack_rows(me, codes, arrived, slots, width):
+def pack_rows(arrived, slots, width):
     return pl.pallas_call(
         pack_kernel,
         out_shape=jax.ShapeDtypeStruct((slots, width), BF16),
-        in_specs=[SMEM, pl.BlockSpec(memory_space=pltpu.VMEM), ANY],
+        in_specs=[ANY],
         out_specs=pl.BlockSpec(memory_space=pltpu.VMEM),
-        scratch_shapes=[
-            pltpu.VMEM((slots,) + arrived.shape[1:], BF16),
-            pltpu.SemaphoreType.DMA((slots,)),
-        ],
+        scratch_shapes=[pltpu.VMEM(arrived.shape, BF16), pltpu.SemaphoreType.DMA((8,))],
         compiler_params=pltpu.CompilerParams(vmem_limit_bytes=VMEM_BYTES),
         name="pack_rows",
-    )(me, codes, arrived)
+    )(arrived)
 
 
 def moved(block, rows, cols):
@@ -524,40 +614,28 @@
     slots = window_target_device.size // 2
     row, col = lax.axis_index("row"), lax.axis_index("col")
     place = jnp.stack([row, col, n_row - 1, n_col - 1]).astype(jnp.int32)
-    me = (row * n_col + col).astype(jnp.int32).reshape(1)
     consts = constants(n_heads, n_feat)
     params = (
         bias_net_input_weight,
-        bias_net_first_bias[:, None, :],
-        bias_net_output_weight,
+        bias_net_first_bias,
+        jnp.transpose(bias_net_output_weight, (2, 0, 1)),
         query_key_value_weight,
         projection_weight,
         up_weight,
-        down_weight,
+        jnp.swapaxes(down_weight, 1, 2),
         norm_gain_values,
     )
-    code = jnp.where(
-        window_target_device >= 0, window_target_device * slots + window_device_slot, -1
+    mid0, mid1, upper, lower, left, right, send = first_layer(
+        embedded, window_target_device, window_device_slot, temper, cloud_mask_token, consts, params,
+        n_row * n_col,
     )
-    codes = lax.all_gather(code.reshape(1, -1), ("row", "col"), axis=0, tiled=True)
-    mid0, mid1, left, right, send = first_layer(
-        embedded, window_target_device, temper, cloud_mask_token[None, :], consts, params, n_row * n_col
-    )
-    pieces = (
-        mid0,
-        mid1,
-        moved(mid1, 1, 0),
-        moved(mid0, -1, 0),
-        moved(right, 0, 1),
-        moved(left, 0, -1),
-        moved(right, 1, 1),
-        moved(left, 1, -1),
-        moved(right, -1, 1),
-        moved(left, -1, -1),
-    )
+    left, right = moved(right, 0, 1), moved(left, 0, -1)
+    upper, lower = add_corners(left, right, upper, lower)
+    send, upper, lower = lax.optimization_barrier((send, upper, lower))
+    pieces = (mid0, mid1, moved(lower, 1, 0), moved(upper, -1, 0), left, right)
     arrived = lax.all_to_all(send, ("row", "col"), split_axis=0, concat_axis=0, tiled=True)
     features = second_layer(place, temper, pieces, consts, params)
-    packed = pack_rows(me, codes, arrived, slots, CELLS * n_feat)
+    packed = pack_rows(arrived, slots, CELLS * n_feat)
     return features, packed
 
 

time: 150 us -> 87.4 us (0.58)
  blocking collectives: 43.9 us -> 0 us
  starting transfers between devices: 26.9 us -> 18.1 us
  local copies, waits for them, and re-layouts: 8.83 us -> 2.33 us
  waiting for transfers between devices: 32 us -> 27 us
  Pallas kernels: 34.9 us -> 37.7 us
    all_gather x1 -> x0, blocking collectives: 43.9 us -> none  [local(): lax.all_gather(code.reshape(1, -1), ('row', 'col'), axis=0, tiled=True)]
    ppermute x8 -> x4, waiting for transfers between devices: 32 us -> 2.21 us  [moved(): return lax.ppermute(block, ('row', 'col'), route)]
    all_to_all x1, waiting for transfers between devices: 0.01 us -> 24.8 us  [local(): lax.all_to_all(send, ('row', 'col'), split_axis=0, concat_axis=0, tiled=T...]
    ppermute x8 -> x4, starting transfers between devices: 15.6 us -> 9.31 us  [moved(): return lax.ppermute(block, ('row', 'col'), route)]
    unnamed x25 -> x6, local copies, waits for them, and re-layouts: 6.3 us -> 2.33 us
    broadcast_in_dim x2 -> x0, local copies, waits for them, and re-layouts: 2.53 us -> none  [the longest x1 1.28 us: local(): bias_net_first_bias[:, None, :]]
    all_to_all x1, starting transfers between devices: 11.3 us -> 8.84 us  [local(): lax.all_to_all(send, ('row', 'col'), split_axis=0, concat_axis=0, tiled=T...]
    pallas_call x0 -> x1, Pallas kernels: none -> 2.13 us  [add_corners(): pl.pallas_call(corner_kernel, out_shape=(shape, shape), in_specs=[ANY] *...]
  transfers between devices with their start and end apart: 9 -> 5, of which waited for: 1 -> 2; matrix products, arithmetic and copies ran while one was open for 0% -> 1% of each run, Pallas kernels for 12% -> 21%
where the time goes in v2:
time: 87.4 us; the launch traced here: 86.5 us
  Pallas kernels  37.7 us (43%)
  waiting for transfers between devices  27 us (31%)
  starting transfers between devices  18.1 us (21%)
  local copies, waits for them, and re-layouts  2.33 us (3%)
    all_to_all x1, waiting for transfers between devices, local(): lax.all_to_all(send, ('row', 'col'), split_axis=0, concat_axis=0, tiled=T...  24.8 us
    pallas_call x1, Pallas kernels, second_layer(): pl.pallas_call(functools.partial(second_kernel, groups), grid=(steps,), o...  18.3 us
    pallas_call x1, Pallas kernels, first_layer(): pl.pallas_call(functools.partial(first_kernel, groups), grid=(columns //...  14.2 us
    ppermute x4, starting transfers between devices, moved(): return lax.ppermute(block, ('row', 'col'), route)  9.31 us
    all_to_all x1, starting transfers between devices, local(): lax.all_to_all(send, ('row', 'col'), split_axis=0, concat_axis=0, tiled=T...  8.84 us
    pallas_call x1, Pallas kernels, pack_rows(): pl.pallas_call(pack_kernel, out_shape=jax.ShapeDtypeStruct((slots, width)...  3.16 us
    unnamed x6, local copies, waits for them, and re-layouts  2.33 us
    ppermute x4, waiting for transfers between devices, moved(): return lax.ppermute(block, ('row', 'col'), route)  2.21 us
  transfers between devices with their start and end apart: 5, of which 2 were waited for; matrix products, arithmetic and copies ran while one was open for 1% of the time, Pallas kernels for 21%

profile of v2, /device:TPU:0, one launch (start us, length us, event | category | flops | bytes accessed | tf_op | source)
XLA Modules:
  0.0 86.5 jit_solution(7086607380983980753)
XLA Ops:
  0.6 14.2 %first_layer.1 = (bf16[32,32,192]{2,1,0:T(8,128)(2,1)}, bf16[32,32,192]{2,1,0:T(8,128)(2,1)}, bf16[34,16,192]{2,1,0:T(8,128)(2,1)}, bf16[34,16,192]{2,1,0:T(8,12...) custom-call(s32[2,16]{1,0:T(2,128)} %targets.1, s32[2,16]{1,0:T(2,128)} %slots.1, ...), custom_call_target="tpu_custom_call" | custom-call | flops 2000000000 | bytes 6000000 | tf_op jit(solution)/shard_map/first_layer/pallas_call | solution.py:314
  14.8 1.5 %collective-permute-start = (bf16[96,192]{1,0:T(8,128)(2,1)}, bf16[96,192]{1,0:T(8,128)(2,1)S(1)}, u32[]{:S(2)}, u32[]{:S(2)}) collective-permute-start(bf16[96,192]{1,0:T(8,128)(2,1)} %get-tuple-element.17), channel_id=1, source_target_pairs={{0,1},{1,2},{2,3},{3,4},{4,5},{5,6},{6,7},{7,8},{8,9},{9,10},{10,1... | collective-permute-start | bytes 110600 | tf_op jit(solution)/shard_map/ppermute | solution.py:594
  16.3 4.8 %collective-permute-start.1 = (bf16[96,192]{1,0:T(8,128)(2,1)}, bf16[96,192]{1,0:T(8,128)(2,1)S(1)}, u32[]{:S(2)}, u32[]{:S(2)}) collective-permute-start(bf16[96,192]{1,0:T(8,128)(2,1)} %get-tuple-element.18), channel_id=1, source_target_pairs={{0,15},{1,0},{2,1},{3,2},{4,3},{5,4},{6,5},{7,6},{8,7},{9,8},{10,9... | collective-permute-start | bytes 110600 | tf_op jit(solution)/shard_map/ppermute | solution.py:594
  21.2 2.2 %collective-permute-done.left_ref = bf16[96,192]{1,0:T(8,128)(2,1)S(1)} collective-permute-done((bf16[96,192]{1,0:T(8,128)(2,1)}, bf16[96,192]{1,0:T(8,128)(2,1)S(1)}, u32[]{:S(2)}, u32[]{:S(2)}) %collective-permute-start) | collective-permute-done | bytes 36896 | tf_op jit(solution)/shard_map/ppermute | solution.py:594
  23.4 0.0 copy-start.1
  23.4 0.0 collective-permute-done.1.right_ref
  23.4 0.0 copy-start.2
  23.4 0.6 copy-done.1
  24.0 0.0 copy-done.2
  24.0 2.1 %add_corners.1 = (bf16[34,16,192]{2,1,0:T(8,128)(2,1)}, bf16[34,16,192]{2,1,0:T(8,128)(2,1)}) custom-call(bf16[96,192]{1,0:T(8,128)(2,1)} %copy-done.1, bf16[96,192]{1,0:T(8,128)(2,1)} %copy-done.2, bf16[34,16,192]{2,1,0:T(8,128)(2,1)} %get-tuple-element.19.up_in, ...), custom_call_target="tpu_custom_call", output_to_operand_aliasing={{0}: (2, {}), {1}: (3, {})} | custom-call | tf_op jit(solution)/shard_map/add_corners/pallas_call | solution.py:354
  26.1 0.0 collective-permute-start.2
  26.1 2.9 %collective-permute-start.3 = (bf16[34,16,192]{2,1,0:T(8,128)(2,1)}, bf16[34,16,192]{2,1,0:T(8,128)(2,1)}, u32[]{:S(2)}, u32[]{:S(2)}) collective-permute-start(bf16[34,16,192]{2,1,0:T(8,128)(2,1)} %get-tuple-element.24), channel_id=1, source_target_pairs={{0,112},{1,113},{2,114},{3,115},{4,116},{5,117},{6,118},{7,119},{8... | collective-permute-start | bytes 626696 | tf_op jit(solution)/shard_map/ppermute | solution.py:594
  29.1 0.6 pad_add_fusion.place
  29.7 8.8 %all-to-all-start = ((bf16[128,104,128]{2,1,0:T(8,128)(2,1)}), bf16[128,104,128]{2,1,0:T(8,128)(2,1)S(1)}, u32[]{:S(2)}, u32[]{:S(2)}) async-start(bf16[128,104,128]{2,1,0:T(8,128)(2,1)} %get-tuple-element.25), calls=%async_computation | async-start | bytes 6815744 | tf_op jit(solution)/shard_map/all_to_all | solution.py:636
  38.5 0.0 collective-permute-done.2.above_ref
  38.5 0.0 collective-permute-done.3.below_ref
  38.5 18.3 %second_layer.1 = bf16[16,24576]{1,0:T(8,128)(2,1)} custom-call(s32[4]{0:T(128)} %pad_add_fusion.place, f32[2,6]{1,0:T(2,128)} %temper.3, bf16[32,32,192]{2,1,0:T(8,128)(2,1)} %get-tuple-element.14.mid0_ref, bf16[32,32,192]{2,1,0:T(8,128)(2,1)} %get-tuple-element.15.mid1_ref, bf16[34,16,192]{2,1,0:T(8,128)(2,1)} %collective-permute-done.2.above_ref, ...), custom_call_target="tpu_custom_call" | custom-call | flops 99999997952 | bytes 10000000 | tf_op jit(solution)/shard_map/second_layer/pallas_call | solution.py:512
  56.8 24.8 %all-to-all-done.entries_ref = bf16[128,104,128]{2,1,0:T(8,128)(2,1)S(1)} async-done(((bf16[128,104,128]{2,1,0:T(8,128)(2,1)}), bf16[128,104,128]{2,1,0:T(8,128)(2,1)S(1)}, u32[]{:S(2)}, u32[]{:S(2)}) %all-to-all-start) | async-done | bytes 3407904 | tf_op jit(solution)/shard_map/all_to_all | solution.py:636
  81.6 0.0 copy-start
  81.6 1.7 %copy-done = bf16[128,104,128]{2,1,0:T(8,128)(2,1)} copy-done((bf16[128,104,128]{2,1,0:T(8,128)(2,1)}, bf16[128,104,128]{2,1,0:T(8,128)(2,1)S(1)}, u32[]{:S(2)}) %copy-start) | copy-done | bytes 3407896
  83.3 3.2 %pack_rows.1 = bf16[16,12288]{1,0:T(8,128)(2,1)} custom-call(bf16[128,104,128]{2,1,0:T(8,128)(2,1)} %copy-done), custom_call_target="tpu_custom_call" | custom-call | tf_op jit(solution)/shard_map/pack_rows/pallas_call | solution.py:576
Async XLA Ops:
  14.8 8.5 %collective-permute-start = (bf16[96,192]{1,0:T(8,128)(2,1)}, bf16[96,192]{1,0:T(8,128)(2,1)S(1)}, u32[]{:S(2)}, u32[]{:S(2)}) collective-permute-start(bf16[96,192]{1,0:T(8,128)(2,1)} %get-tuple-element.17), channel_id=1, source_target_pairs={{0,1},{1,2},{2,3},{3,4},{4,5},{5,6},{6,7},{7,8},{8,9},{9,10},{10,1... | collective-permute-start | bytes 110600 | tf_op jit(solution)/shard_map/ppermute | solution.py:594
  16.3 7.0 %collective-permute-start.1 = (bf16[96,192]{1,0:T(8,128)(2,1)}, bf16[96,192]{1,0:T(8,128)(2,1)S(1)}, u32[]{:S(2)}, u32[]{:S(2)}) collective-permute-start(bf16[96,192]{1,0:T(8,128)(2,1)} %get-tuple-element.18), channel_id=1, source_target_pairs={{0,15},{1,0},{2,1},{3,2},{4,3},{5,4},{6,5},{7,6},{8,7},{9,8},{10,9... | collective-permute-start | bytes 110600 | tf_op jit(solution)/shard_map/ppermute | solution.py:594
  23.4 0.6 copy-start.1
  23.4 0.6 copy-start.2
  26.1 12.4 %collective-permute-start.2 = (bf16[34,16,192]{2,1,0:T(8,128)(2,1)}, bf16[34,16,192]{2,1,0:T(8,128)(2,1)}, u32[]{:S(2)}, u32[]{:S(2)}) collective-permute-start(bf16[34,16,192]{2,1,0:T(8,128)(2,1)} %get-tuple-element.23), channel_id=1, source_target_pairs={{0,16},{1,17},{2,18},{3,19},{4,20},{5,21},{6,22},{7,23},{8,24},{9,... | collective-permute-start | bytes 626696 | tf_op jit(solution)/shard_map/ppermute | solution.py:594
  26.1 12.4 %collective-permute-start.3 = (bf16[34,16,192]{2,1,0:T(8,128)(2,1)}, bf16[34,16,192]{2,1,0:T(8,128)(2,1)}, u32[]{:S(2)}, u32[]{:S(2)}) collective-permute-start(bf16[34,16,192]{2,1,0:T(8,128)(2,1)} %get-tuple-element.24), channel_id=1, source_target_pairs={{0,112},{1,113},{2,114},{3,115},{4,116},{5,117},{6,118},{7,119},{8... | collective-permute-start | bytes 626696 | tf_op jit(solution)/shard_map/ppermute | solution.py:594
  29.7 52.0 %all-to-all-start = ((bf16[128,104,128]{2,1,0:T(8,128)(2,1)}), bf16[128,104,128]{2,1,0:T(8,128)(2,1)S(1)}, u32[]{:S(2)}, u32[]{:S(2)}) async-start(bf16[128,104,128]{2,1,0:T(8,128)(2,1)} %get-tuple-element.25), calls=%async_computation | async-start | bytes 6815744 | tf_op jit(solution)/shard_map/all_to_all | solution.py:636
  81.6 1.7 %copy-start = (bf16[128,104,128]{2,1,0:T(8,128)(2,1)}, bf16[128,104,128]{2,1,0:T(8,128)(2,1)S(1)}, u32[]{:S(2)}) copy-start(bf16[128,104,128]{2,1,0:T(8,128)(2,1)S(1)} %all-to-all-done.entries_ref) | copy-start | bytes 10223620

commit v3 on v2

--- a/solution.py
+++ b/solution.py
@@ -18,6 +18,7 @@
 VMEM_BYTES = 60 * 2**20
 SMEM = pl.BlockSpec(memory_space=pltpu.SMEM)
 ANY = pl.BlockSpec(memory_space=pl.ANY)
+HBM = pl.BlockSpec(memory_space=pltpu.HBM)
 
 
 def log_step(offset):
@@ -143,6 +144,21 @@
     return (hidden.astype(F32) + layer_norm(reduced, gain_ref[1:2, :])).astype(BF16)
 
 
+def attend(x, q_w, k_w, v_w, temper, heads_ref, ones_ref, mask_ref, bias_of, p_ref):
+    n_windows = x.shape[0] // CELLS
+    q = (unit_vectors(dot(x, q_w[...]), heads_ref) * temper).astype(BF16)
+    k = unit_vectors(dot(x, k_w[...]), heads_ref).astype(BF16)
+    v = dot(x, v_w[...]).astype(BF16)
+    mixed = []
+    for n in range(n_windows):
+        rows = slice(n * CELLS, (n + 1) * CELLS)
+        p_ref[rows, :] = jnp.exp2(scores_of(q[rows], k[rows], mask_ref) + bias_of(n)).astype(BF16)
+    for n in range(n_windows):
+        rows = slice(n * CELLS, (n + 1) * CELLS)
+        mixed.append(weighted(p_ref[rows, :], *spread_heads(v[rows], mask_ref)))
+    return jnp.concatenate(mixed, 0) / totals_of(p_ref[...], ones_ref)
+
+
 def split_weights(qkv_ref, q_w, k_w, v_w):
     n_feat = q_w.shape[0]
     q_w[...] = qkv_ref[:, :n_feat]
@@ -150,27 +166,21 @@
     v_w[...] = qkv_ref[:, 2 * n_feat :]
 
 
-def half_rows(tile, lower):
+def half_rows(tile):
     first = lax.broadcasted_iota(jnp.int32, (WIN, tile.shape[1]), 0) < HALF
     pairs = []
     for pair in range(2):
         even = tile[2 * pair * WIN : (2 * pair + 1) * WIN]
         odd = tile[(2 * pair + 1) * WIN : (2 * pair + 2) * WIN]
-        if lower:
-            pairs.append(jnp.where(first, pltpu.roll(even, HALF, 0), odd))
-        else:
-            pairs.append(jnp.where(first, even, pltpu.roll(odd, HALF, 0)))
+        pairs.append(jnp.where(first, even, pltpu.roll(odd, HALF, 0)))
     return jnp.concatenate(pairs, 0)
 
 
-def ring_tile(upper, lower):
-    first = lax.broadcasted_iota(jnp.int32, (WIN, upper.shape[1]), 0) < HALF
+def whole_rows(halves):
     tiles = []
     for pair in range(2):
-        rows = slice(pair * WIN, (pair + 1) * WIN)
-        up, low = upper[rows], lower[rows]
-        tiles.append(jnp.where(first, up, pltpu.roll(low, HALF, 0)))
-        tiles.append(jnp.where(first, pltpu.roll(up, HALF, 0), low))
+        rows = halves[pair * WIN : (pair + 1) * WIN]
+        tiles += [rows, pltpu.roll(rows, HALF, 0)]
     return jnp.concatenate(tiles, 0)
 
 
@@ -178,7 +188,7 @@
     groups,
     targets, slots, temper, emb_ref, token_ref, coords_ref, heads_ref, ones_ref, mask_ref,
     net_in, net_first, net_out, qkv_ref, proj_ref, up_ref, down_ref, gain_ref,
-    mid0_ref, mid1_ref, upper_ref, lower_ref, left_ref, right_ref, send_ref,
+    mid0_ref, mid1_ref, upper_ref, left_ref, send_ref,
     bias_ref, strips_ref, q_w, k_w, v_w, p_ref, staging, blank, sems, blank_sems,
 ):
     step = pl.program_id(0)
@@ -210,19 +220,10 @@
         for i in range(2):
             tiles.append(jnp.concatenate([s[i * WIN : (i + 1) * WIN] for s in slabs], 0))
     x = jnp.concatenate(tiles, 0)
-    xb = x.astype(BF16)
-    q = (unit_vectors(dot(xb, q_w[...]), heads_ref) * temper_row(temper, 0, mask_ref)).astype(BF16)
-    k = unit_vectors(dot(xb, k_w[...]), heads_ref).astype(BF16)
-    v = dot(xb, v_w[...]).astype(BF16)
-    bias = bias_ref[...]
-    mixed = []
-    for n in range(2 * groups):
-        rows = slice(n * CELLS, (n + 1) * CELLS)
-        p_ref[rows, :] = jnp.exp2(scores_of(q[rows], k[rows], mask_ref) + bias).astype(BF16)
-    for n in range(2 * groups):
-        rows = slice(n * CELLS, (n + 1) * CELLS)
-        mixed.append(weighted(p_ref[rows, :], *spread_heads(v[rows], mask_ref)))
-    mixed = jnp.concatenate(mixed, 0) / totals_of(p_ref[...], ones_ref)
+    mixed = attend(
+        x.astype(BF16), q_w, k_w, v_w, temper_row(temper, 0, mask_ref), heads_ref, ones_ref, mask_ref,
+        lambda n: bias_ref[...], p_ref,
+    )
 
     @pl.when(step == 0)
     def _():
@@ -243,23 +244,17 @@
             mid = (mid0_ref, mid1_ref)[i]
             mid[2 * group] = rows[:32]
             mid[2 * group + 1] = rows[32:]
-            halves = [half_rows(kept[half * 32 : (half + 1) * 32], i).astype(BF16) for half in range(2)]
-            outward = (upper_ref, lower_ref)[i]
-            outward[1 + 2 * j] = halves[0]
-            outward[2 + 2 * j] = halves[1]
+            if i == 0:
+                halves = [half_rows(kept[half * 32 : (half + 1) * 32]).astype(BF16) for half in range(2)]
+                upper_ref[2 * group] = halves[0]
+                upper_ref[2 * group + 1] = halves[1]
             if group == 0:
 
                 @pl.when(step == 0)
                 def _(i=i, rows=rows, halves=halves):
                     left_ref[i * 32 : (i + 1) * 32] = rows[:32]
-                    left_ref[64 + i * 16 : 80 + i * 16] = halves[0]
-
-            if group == groups - 1:
-
-                @pl.when(step == pl.num_programs(0) - 1)
-                def _(i=i, rows=rows, halves=halves):
-                    right_ref[i * 32 : (i + 1) * 32] = rows[32:]
-                    right_ref[64 + i * 16 : 80 + i * 16] = halves[1]
+                    if i == 0:
+                        left_ref[64:] = halves[0]
 
             slot = j * 2 + i
             staging[slot, :64] = tile[:, :128].astype(BF16)
@@ -307,18 +302,18 @@
 def first_layer(embedded, targets, slots, temper, token, consts, params, devices, groups=8):
     n_heads, n_feat = consts[3].shape
     columns = embedded.shape[1] // (WIN * n_feat)
-    side = jax.ShapeDtypeStruct((96, n_feat), BF16)
-    outward = jax.ShapeDtypeStruct((2 * columns + 2, 16, n_feat), BF16)
+    side = jax.ShapeDtypeStruct((80, n_feat), BF16)
+    upper = jax.ShapeDtypeStruct((2 * columns, 16, n_feat), BF16)
     mid = jax.ShapeDtypeStruct((2 * columns, 32, n_feat), BF16)
     mid_spec = pl.BlockSpec((2 * groups, 32, n_feat), lambda g: (g, 0, 0))
     return pl.pallas_call(
         functools.partial(first_kernel, groups),
         grid=(columns // groups,),
-        out_shape=(mid, mid, outward, outward, side, side, jax.ShapeDtypeStruct((devices, 104, 128), BF16)),
+        out_shape=(mid, mid, upper, side, jax.ShapeDtypeStruct((devices, 104, 128), BF16)),
         in_specs=[SMEM, SMEM, SMEM, pl.BlockSpec((2 * WIN, groups * WIN * n_feat), lambda g: (0, g))]
         + [whole(a) for a in (token,) + consts]
         + [layer_spec(a, n, 0) for n, a in enumerate(params)],
-        out_specs=(mid_spec, mid_spec, whole(outward), whole(outward), whole(side), whole(side), ANY),
+        out_specs=(mid_spec, mid_spec, pl.BlockSpec((2 * groups, 16, n_feat), lambda g: (g, 0, 0)), whole(side), ANY),
         scratch_shapes=[pltpu.VMEM((CELLS, n_heads * CELLS), F32)]
         + layer_scratch(n_heads, n_feat)
         + [
@@ -334,80 +329,45 @@
     )(targets, slots, temper, embedded, token, *consts, *params)
 
 
-def corner_kernel(left_ref, right_ref, up_in, low_in, up_ref, low_ref, sems):
-    del up_in, low_in
-    end = up_ref.shape[0] - 1
-    copies = [
-        pltpu.make_async_copy(left_ref.at[pl.ds(64, 16)], up_ref.at[0], sems.at[0]),
-        pltpu.make_async_copy(right_ref.at[pl.ds(64, 16)], up_ref.at[end], sems.at[1]),
-        pltpu.make_async_copy(left_ref.at[pl.ds(80, 16)], low_ref.at[0], sems.at[2]),
-        pltpu.make_async_copy(right_ref.at[pl.ds(80, 16)], low_ref.at[end], sems.at[3]),
-    ]
-    for copy in copies:
-        copy.start()
-    for copy in copies:
-        copy.wait()
-
-
-def add_corners(left, right, upper, lower):
-    shape = jax.ShapeDtypeStruct(upper.shape, upper.dtype)
-    return pl.pallas_call(
-        corner_kernel,
-        out_shape=(shape, shape),
-        in_specs=[ANY] * 4,
-        out_specs=(ANY, ANY),
-        scratch_shapes=[pltpu.SemaphoreType.DMA((4,))],
-        input_output_aliases={2: 0, 3: 1},
-        name="add_corners",
-    )(left, right, upper, lower)
-
-
 def second_kernel(
     groups,
-    place, temper, mid0_ref, mid1_ref, above_ref, below_ref, left_ref, right_ref,
+    place, temper, mid0_ref, mid1_ref, below_ref, right_ref, corner_ref,
     coords_ref, heads_ref, ones_ref, mask_ref,
     net_in, net_first, net_out, qkv_ref, proj_ref, up_ref, down_ref, gain_ref,
-    out_ref,
-    bias_ref, strips_ref, q_w, k_w, v_w, ext, upper_ring, lower_ring, p_ref, sems,
+    out_ref, rows_ref, side_ref,
+    bias_ref, strips_ref, q_w, k_w, v_w, ext, ring, p_ref, sems,
 ):
     step = pl.program_id(0)
     n_heads, n_feat = mask_ref.shape
     n_half = mid0_ref.shape[0]
     row, col, last_row, last_col = place[0], place[1], place[2], place[3]
+    width = HALF * n_feat
 
     @pl.when(step == 0)
     def _():
-        inner, every = pl.ds(1, n_half), pl.ds(0, n_half + 2)
-        end = n_half + 1
+        own = pl.ds(0, n_half)
         copies = [
             pltpu.make_async_copy(src, dst, sems.at[n])
             for n, (src, dst) in enumerate(
                 [
-                    (mid0_ref, ext.at[0, inner]),
-                    (mid1_ref, ext.at[1, inner]),
-                    (left_ref.at[pl.ds(0, 32)], ext.at[0, 0]),
-                    (left_ref.at[pl.ds(32, 32)], ext.at[1, 0]),
-                    (right_ref.at[pl.ds(0, 32)], ext.at[0, end]),
-                    (right_ref.at[pl.ds(32, 32)], ext.at[1, end]),
-                    (above_ref, lower_ring.at[every]),
-                    (below_ref, upper_ring.at[every]),
+                    (mid0_ref, ext.at[0, own]),
+                    (mid1_ref, ext.at[1, own]),
+                    (right_ref.at[pl.ds(0, 32)], ext.at[0, n_half]),
+                    (right_ref.at[pl.ds(32, 32)], ext.at[1, n_half]),
+                    (below_ref, ring.at[own]),
+                    (corner_ref.at[pl.ds(64, 16)], ring.at[n_half]),
                 ]
             )
         ]
         for copy in copies:
             copy.start()
-        for spare in range(n_half + 2, ext.shape[1]):
-            ext[:, spare] = jnp.zeros((2, 32, n_feat), BF16)
-            upper_ring[spare] = jnp.zeros((16, n_feat), BF16)
-            lower_ring[spare] = jnp.zeros((16, n_feat), BF16)
+        out_ref[:, :width] = jnp.zeros((2 * WIN, width), BF16)
         split_weights(qkv_ref, q_w, k_w, v_w)
         bias_strips(coords_ref, net_in, net_first[1:2, :], net_out[:, 1, :], strips_ref)
         strips = [turned(strips_ref[h]) for h in range(n_heads)]
         lane = lax.broadcasted_iota(jnp.int32, (WIN, n_heads * CELLS), 1)
         upper = lax.broadcasted_iota(jnp.int32, (WIN, n_heads * CELLS), 0) < HALF
         other_rows = upper != (lane % WIN < HALF)
-        top, bottom = row == 0, row == last_row
-        edge_rows = other_rows & ((upper & top) | (~upper & bottom))
         for w in range(WIN):
             other_cols = (lane % CELLS >= CELLS // 2) != (w >= HALF)
             rows = slice(w * WIN, (w + 1) * WIN)
@@ -415,117 +375,89 @@
             away = -100.0 * LOG2E
             bias_ref[0, rows, :] = bias
             bias_ref[1, rows, :] = bias + jnp.where(other_cols, away, 0.0)
-            bias_ref[2, rows, :] = bias + jnp.where(edge_rows, away, 0.0)
-            bias_ref[3, rows, :] = bias + jnp.where(edge_rows | other_cols, away, 0.0)
+            bias_ref[2, rows, :] = bias + jnp.where(other_rows, away, 0.0)
+            bias_ref[3, rows, :] = bias + jnp.where(other_rows | other_cols, away, 0.0)
         for copy in copies:
             copy.wait()
 
-    first_half = 2 * groups * step
     upper = lax.broadcasted_iota(jnp.int32, (CELLS, n_feat), 0) % WIN < HALF
-
-    def tile_of(line, group):
-        return jnp.concatenate(
-            [ext[line, first_half + 2 * group], ext[line, first_half + 2 * group + 1]], 0
-        )
-
-    own, around = [], []
+    tiles = []
     for group in range(groups):
-        own += [tile_of(0, group), tile_of(1, group)]
-        for half in range(2):
-            at = first_half + 2 * group + half
-            around.append(
-                ring_tile(upper_ring[at].astype(F32), lower_ring[at].astype(F32)).astype(BF16)
-            )
-    xb = jnp.concatenate(own, 0)
-    xa = jnp.concatenate(around, 0)
-    q = (unit_vectors(dot(xb, q_w[...]), heads_ref) * temper_row(temper, 1, mask_ref)).astype(BF16)
-    keys = [unit_vectors(dot(t, k_w[...]), heads_ref).astype(BF16) for t in (xb, xa)]
-    values = [dot(t, v_w[...]).astype(BF16) for t in (xb, xa)]
-
-    def tiles(t, group):
-        low = 2 * group * CELLS
-        return t[low : low + CELLS], t[low + CELLS : low + 2 * CELLS]
-
-    def three(parts, group):
-        zero, one = tiles(parts[0], group)
-        ring = parts[1][group * CELLS : (group + 1) * CELLS]
-        return (
-            jnp.where(upper, one, zero),
-            jnp.where(upper, zero, ring),
-            jnp.where(upper, ring, one),
-        )
-
-    upper_wide = lax.broadcasted_iota(jnp.int32, (CELLS, n_heads * CELLS), 0) % WIN < HALF
+        at = 2 * (step * groups + group) + 1
+        zero = jnp.concatenate([ext[0, at], ext[0, at + 1]], 0)
+        one = jnp.concatenate([ext[1, at], ext[1, at + 1]], 0)
+        two = jnp.concatenate([whole_rows(ring[at + half].astype(F32)) for half in range(2)], 0)
+        tiles += [jnp.where(upper, one, zero), jnp.where(upper, two.astype(BF16), one)]
+    x = jnp.concatenate(tiles, 0)
+    low_cut = (row == last_row).astype(jnp.int32)
+
+    def bias_of(n):
+        column = step * groups + n // 2
+        cut = ((col == last_col) & (column == n_half // 2 - 1)).astype(jnp.int32)
+        return bias_ref[cut + 2 * low_cut * (n % 2)]
+
+    mixed = attend(
+        x, q_w, k_w, v_w, temper_row(temper, 1, mask_ref), heads_ref, ones_ref, mask_ref, bias_of, p_ref
+    )
+    y = dense_tail(x.astype(F32), mixed, proj_ref, up_ref, down_ref, gain_ref).astype(F32)
+
     for group in range(groups):
-        zero, one = tiles(q, group)
-        inside, over, under = three(keys, group)
-        column = step * groups + group
-        cut = ((column == 0) & (col == 0)) | ((column == n_half // 2) & (col == last_col))
-        cut = cut.astype(jnp.int32)
-        rows = slice(2 * group * CELLS, (2 * group + 1) * CELLS)
-        scores = scores_of(jnp.where(upper, one, zero), inside, mask_ref)
-        p_ref[rows, :] = jnp.exp2(scores + bias_ref[cut]).astype(BF16)
-        edge = jnp.where(upper, zero, one)
-        scores = jnp.where(
-            upper_wide, scores_of(edge, over, mask_ref), scores_of(edge, under, mask_ref)
-        )
-        rows = slice((2 * group + 1) * CELLS, (2 * group + 2) * CELLS)
-        p_ref[rows, :] = jnp.exp2(scores + bias_ref[2 + cut]).astype(BF16)
-    totals = totals_of(p_ref[...], ones_ref)
-    mixed = []
-    for group in range(groups):
-        inside, over, under = three(values, group)
-        rows = slice(2 * group * CELLS, (2 * group + 1) * CELLS)
-        middle = weighted(p_ref[rows, :], *spread_heads(inside, mask_ref)) / totals[rows]
-        rows = slice((2 * group + 1) * CELLS, (2 * group + 2) * CELLS)
-        p = p_ref[rows, :]
-        edge = jnp.where(
-            upper,
-            weighted(p, *spread_heads(over, mask_ref)),
-            weighted(p, *spread_heads(under, mask_ref)),
-        ) / totals[rows]
-        mixed += [jnp.where(upper, edge, middle), jnp.where(upper, middle, edge)]
-    mixed = jnp.concatenate(mixed, 0)
-    y = dense_tail(xb.astype(F32), mixed, proj_ref, up_ref, down_ref, gain_ref).astype(F32)
-
-    for group in range(groups):
-        zero, one = tiles(y, group)
+        first = y[2 * group * CELLS : (2 * group + 1) * CELLS]
+        second = y[(2 * group + 1) * CELLS : (2 * group + 2) * CELLS]
+        zero = jnp.where(upper, second, first)
+        one = jnp.where(upper, first, second)
         for half in range(2):
             slabs = []
             for w in range(half * HALF, (half + 1) * HALF):
                 rows = slice(w * WIN, (w + 1) * WIN)
                 slabs.append(jnp.concatenate([zero[rows], one[rows]], 0))
             strip = jnp.concatenate(slabs, 1).astype(BF16)
-            at = first_half + 2 * group + half - 1
-
-            @pl.when((at >= 0) & (at < n_half))
-            def _(at=at, strip=strip):
-                width = HALF * n_feat
+            at = 2 * (step * groups + group) + 1 + half
+            if half == 0 or group < groups - 1:
                 out_ref[:, pl.ds(pl.multiple_of(at * width, 128), width)] = strip
-
-
-def second_layer(place, temper, pieces, consts, params, groups=6):
+            else:
+
+                @pl.when(at < n_half)
+                def _(at=at, strip=strip):
+                    out_ref[:, pl.ds(pl.multiple_of(at * width, 128), width)] = strip
+
+                @pl.when(at == n_half)
+                def _(strip=strip):
+                    side_ref[...] = strip
+
+    @pl.when(step == pl.num_programs(0) - 1)
+    def _():
+        quarter = rows_ref.shape[1]
+        first = lax.broadcasted_iota(jnp.int32, (WIN, quarter), 0) < HALF
+        tops = [out_ref[:, n * quarter : (n + 1) * quarter][:WIN].astype(F32) for n in range(4)]
+        pairs = [
+            jnp.where(first, tops[2 * n], pltpu.roll(tops[2 * n + 1], HALF, 0)) for n in range(2)
+        ]
+        rows_ref[...] = jnp.concatenate(pairs, 0).astype(BF16)
+
+
+def second_layer(place, temper, pieces, consts, params, groups=8):
     n_heads, n_feat = consts[3].shape
     n_half = pieces[0].shape[0]
-    steps = -(-(n_half // 2 + 1) // groups)
     out = jax.ShapeDtypeStruct((2 * WIN, n_half * HALF * n_feat), BF16)
+    rows = jax.ShapeDtypeStruct((2 * WIN, n_half * n_feat), BF16)
+    side = jax.ShapeDtypeStruct((2 * WIN, HALF * n_feat), BF16)
     return pl.pallas_call(
         functools.partial(second_kernel, groups),
-        grid=(steps,),
-        out_shape=out,
+        grid=(n_half // 2 // groups,),
+        out_shape=(out, rows, side),
         in_specs=[SMEM, SMEM]
         + [ANY] * len(pieces)
         + [whole(a) for a in consts]
         + [layer_spec(a, n, 1) for n, a in enumerate(params)],
-        out_specs=whole(out),
+        out_specs=(whole(out), whole(rows), whole(side)),
         scratch_shapes=[pltpu.VMEM((4, CELLS, n_heads * CELLS), F32)]
         + layer_scratch(n_heads, n_feat)
         + [
-            pltpu.VMEM((2, 2 * groups * steps, 32, n_feat), BF16),
-            pltpu.VMEM((2 * groups * steps, 16, n_feat), BF16),
-            pltpu.VMEM((2 * groups * steps, 16, n_feat), BF16),
+            pltpu.VMEM((2, n_half + 1, 32, n_feat), BF16),
+            pltpu.VMEM((n_half + 1, 16, n_feat), BF16),
             pltpu.VMEM((groups * 2 * CELLS, n_heads * CELLS), BF16),
-            pltpu.SemaphoreType.DMA((8,)),
+            pltpu.SemaphoreType.DMA((6,)),
         ],
         compiler_params=pltpu.CompilerParams(vmem_limit_bytes=VMEM_BYTES),
         cost_estimate=pl.CostEstimate(flops=10**11, bytes_accessed=10**7, transcendentals=10**6),
@@ -533,8 +465,25 @@
     )(place, temper, *pieces, *consts, *params)
 
 
-def pack_kernel(entries_ref, out_ref, arrived_ref, sems):
-    slots = out_ref.shape[0]
+def merge_features(own_ref, rows_ref, side_ref, corner_ref, out_ref):
+    quarter, width = rows_ref.shape[1], side_ref.shape[1]
+    first = lax.broadcasted_iota(jnp.int32, (WIN, quarter), 0) < HALF
+    for n in range(4):
+        lanes = slice(n * quarter, (n + 1) * quarter)
+        own = own_ref[:, lanes].astype(F32)
+        top = rows_ref[...].astype(F32)[n // 2 * WIN : (n // 2 + 1) * WIN]
+        top = pltpu.roll(top, HALF, 0) if n % 2 else top
+        merged = jnp.concatenate([jnp.where(first, top, own[:WIN]), own[WIN:]], 0)
+        out_ref[:, lanes] = merged.astype(BF16)
+    corner = lax.broadcasted_iota(jnp.int32, (2 * WIN, width), 0) < HALF
+    merged = jnp.where(corner, corner_ref[...].astype(F32), side_ref[...].astype(F32))
+    out_ref[:, :width] = merged.astype(BF16)
+
+
+def last_kernel(
+    entries_ref, own_ref, rows_ref, side_ref, corner_ref, features_ref, packed_ref, arrived_ref, sems
+):
+    slots = packed_ref.shape[0]
     part = arrived_ref.shape[0] // 8
     copies = [
         pltpu.make_async_copy(
@@ -544,6 +493,7 @@
     ]
     for copy in copies:
         copy.start()
+    merge_features(own_ref, rows_ref, side_ref, corner_ref, features_ref)
     for copy in copies:
         copy.wait()
     marks = arrived_ref[:, 96:, :].astype(F32)
@@ -569,19 +519,19 @@
                 jnp.where(lane < 64, moved, tails[u]),
             ]
             at = (u * WIN + 2 * pair) * 192
-            out_ref[:, at : at + 384] = jnp.concatenate(joined, 1).astype(BF16)
-
-
-def pack_rows(arrived, slots, width):
+            packed_ref[:, at : at + 384] = jnp.concatenate(joined, 1).astype(BF16)
+
+
+def last_steps(arrived, own, rows, side, corner, slots, width):
     return pl.pallas_call(
-        pack_kernel,
-        out_shape=jax.ShapeDtypeStruct((slots, width), BF16),
-        in_specs=[ANY],
-        out_specs=pl.BlockSpec(memory_space=pltpu.VMEM),
+        last_kernel,
+        out_shape=(jax.ShapeDtypeStruct(own.shape, BF16), jax.ShapeDtypeStruct((slots, width), BF16)),
+        in_specs=[HBM] + [pl.BlockSpec(memory_space=pltpu.VMEM)] * 4,
+        out_specs=(pl.BlockSpec(memory_space=pltpu.VMEM),) * 2,
         scratch_shapes=[pltpu.VMEM(arrived.shape, BF16), pltpu.SemaphoreType.DMA((8,))],
         compiler_params=pltpu.CompilerParams(vmem_limit_bytes=VMEM_BYTES),
-        name="pack_rows",
-    )(arrived)
+        name="last_steps",
+    )(arrived, own, rows, side, corner)
 
 
 def moved(block, rows, cols):
@@ -625,18 +575,16 @@
         jnp.swapaxes(down_weight, 1, 2),
         norm_gain_values,
     )
-    mid0, mid1, upper, lower, left, right, send = first_layer(
+    mid0, mid1, upper, left, send = first_layer(
         embedded, window_target_device, window_device_slot, temper, cloud_mask_token, consts, params,
         n_row * n_col,
     )
-    left, right = moved(right, 0, 1), moved(left, 0, -1)
-    upper, lower = add_corners(left, right, upper, lower)
-    send, upper, lower = lax.optimization_barrier((send, upper, lower))
-    pieces = (mid0, mid1, moved(lower, 1, 0), moved(upper, -1, 0), left, right)
+    pieces = (mid0, mid1, moved(upper, -1, 0), moved(left, 0, -1), moved(left, -1, -1))
     arrived = lax.all_to_all(send, ("row", "col"), split_axis=0, concat_axis=0, tiled=True)
-    features = second_layer(place, temper, pieces, consts, params)
-    packed = pack_rows(arrived, slots, CELLS * n_feat)
-    return features, packed
+    own, rows, side = second_layer(place, temper, pieces, consts, params)
+    return last_steps(
+        arrived, own, moved(rows, 1, 0), moved(side, 0, 1), moved(side, 1, 1), slots, CELLS * n_feat
+    )
 
 
 def solution(mesh):

time: 87.4 us -> 79.6 us (0.911)
  Pallas kernels: 37.7 us -> 32.2 us
  waiting for transfers between devices: 27 us -> 25.9 us
    all_to_all x1, waiting for transfers between devices: 24.8 us -> 0.01 us  [local(): lax.all_to_all(send, ('row', 'col'), split_axis=0, concat_axis=0, tiled=T...]
    ppermute x4 -> x6, waiting for transfers between devices: 2.21 us -> 25.9 us  [moved(): return lax.ppermute(block, ('row', 'col'), route)]
    pallas_call x3 -> x2, Pallas kernels: 23.6 us -> 18.5 us  [the longest x1 14 us: second_layer(): pl.pallas_call(functools.partial(second_kernel, groups), grid=(n_half //...]
    all_to_all x1, starting transfers between devices: 8.84 us -> 4.67 us  [local(): lax.all_to_all(send, ('row', 'col'), split_axis=0, concat_axis=0, tiled=T...]
    ppermute x4 -> x6, starting transfers between devices: 9.31 us -> 12.9 us  [moved(): return lax.ppermute(block, ('row', 'col'), route)]
    unnamed x6 -> x10, local copies, waits for them, and re-layouts: 2.33 us -> 2.33 us
  transfers between devices with their start and end apart: 5 -> 7, of which waited for: 2 -> 2; matrix products, arithmetic and copies ran while one was open for 1% -> 1% of each run, Pallas kernels for 21% -> 18%
where the time goes in v3:
time: 79.6 us; the launch traced here: 79.4 us
  Pallas kernels  32.2 us (40%)
  waiting for transfers between devices  25.9 us (33%)
  starting transfers between devices  17.5 us (22%)
  local copies, waits for them, and re-layouts  2.33 us (3%)
    ppermute x6, waiting for transfers between devices, moved(): return lax.ppermute(block, ('row', 'col'), route)  25.9 us
    pallas_call x1, Pallas kernels, second_layer(): pl.pallas_call(functools.partial(second_kernel, groups), grid=(n_half //...  14 us
    pallas_call x1, Pallas kernels, first_layer(): pl.pallas_call(functools.partial(first_kernel, groups), grid=(columns //...  13.7 us
    ppermute x6, starting transfers between devices, moved(): return lax.ppermute(block, ('row', 'col'), route)  12.9 us
    all_to_all x1, starting transfers between devices, local(): lax.all_to_all(send, ('row', 'col'), split_axis=0, concat_axis=0, tiled=T...  4.67 us
    pallas_call x1, Pallas kernels, last_steps(): pl.pallas_call(last_kernel, out_shape=(jax.ShapeDtypeStruct(own.shape, BF...  4.48 us
    unnamed x10, local copies, waits for them, and re-layouts  2.33 us
  transfers between devices with their start and end apart: 7, of which 2 were waited for; matrix products, arithmetic and copies ran while one was open for 1% of the time, Pallas kernels for 18%

profile of v3, /device:TPU:0, one launch (start us, length us, event | category | flops | bytes accessed | tf_op | source)
XLA Modules:
  0.0 79.4 jit_solution(6277612938493069064)
XLA Ops:
  0.6 13.7 %first_layer.1 = (bf16[32,32,192]{2,1,0:T(8,128)(2,1)}, bf16[32,32,192]{2,1,0:T(8,128)(2,1)}, bf16[32,16,192]{2,1,0:T(8,128)(2,1)}, bf16[80,192]{1,0:T(8,128)(2,1)}, bf16[128,104,128]{2,1,0:T(8,128)(2,1)}) custom-call(s32[2,16]{1,0:T(2,128)} %targets.1, s32[2,16]{1,0:T(2,128)} %slots.1, f32[2,6]{1,0:T(2,128)} %temper.3, bf16[16,24576]{1,0:T(8,128)(2,1)} %emb_ref.1, ...), custom_call_target="tpu_custom_call" | custom-call | flops 2000000000 | bytes 6000000 | tf_op jit(solution)/shard_map/first_layer/pallas_call | solution.py:309
  14.4 2.7 %collective-permute-start = (bf16[32,16,192]{2,1,0:T(8,128)(2,1)}, bf16[32,16,192]{2,1,0:T(8,128)(2,1)}, u32[]{:S(2)}, u32[]{:S(2)}) collective-permute-start(bf16[32,16,192]{2,1,0:T(8,128)(2,1)} %get-tuple-element.13), channel_id=1, source_target_pairs={{0,112},{1,113},{2,114},{3,115},{4,116},{5,117},{6,118},{7,119},{8... | collective-permute-start | bytes 589832 | tf_op jit(solution)/shard_map/ppermute | solution.py:544
  17.0 6.2 %collective-permute-start.1 = (bf16[80,192]{1,0:T(8,128)(2,1)}, bf16[80,192]{1,0:T(8,128)(2,1)S(1)}, u32[]{:S(2)}, u32[]{:S(2)}) collective-permute-start(bf16[80,192]{1,0:T(8,128)(2,1)} %get-tuple-element.14), channel_id=1, source_target_pairs={{0,15},{1,0},{2,1},{3,2},{4,3},{5,4},{6,5},{7,6},{8,7},{9,8},{10,9... | collective-permute-start | bytes 92168 | tf_op jit(solution)/shard_map/ppermute | solution.py:544
  23.3 0.7 collective-permute-start.2
  24.0 4.7 %all-to-all-start = ((bf16[128,104,128]{2,1,0:T(8,128)(2,1)}), bf16[128,104,128]{2,1,0:T(8,128)(2,1)S(1)}, u32[]{:S(2)}, u32[]{:S(2)}) async-start(bf16[128,104,128]{2,1,0:T(8,128)(2,1)} %get-tuple-element.10), calls=%async_computation | async-start | bytes 6815744 | tf_op jit(solution)/shard_map/all_to_all | solution.py:583
  28.6 0.7 pad_add_fusion.place
  29.3 0.0 collective-permute-done.1.right_ref
  29.3 0.0 copy-start.3
  29.3 0.0 collective-permute-done.2.corner_ref
  29.3 0.0 copy-start.4
  29.3 0.0 collective-permute-done.below_ref
  29.3 0.6 copy-done.3
  29.9 0.1 copy-done.4
  30.0 14.0 %second_layer.1 = (bf16[16,24576]{1,0:T(8,128)(2,1)}, bf16[16,6144]{1,0:T(8,128)(2,1)}, bf16[16,768]{1,0:T(8,128)(2,1)}) custom-call(s32[4]{0:T(128)} %pad_add_fusion.place, f32[2,6]{1,0:T(2,128)} %temper.3, bf16[32,32,192]{2,1,0:T(8,128)(2,1)} %get-tuple-element.11.mid0_ref, bf16[32,32,192]{2,1,0:T(8,128)(2,1)} %get-tuple-element.12.mid1_ref, ...), custom_call_target="tpu_custom_call" | custom-call | flops 99999997952 | bytes 10000000 | tf_op jit(solution)/shard_map/second_layer/pallas_call | solution.py:445
  44.0 0.0 collective-permute-start.3
  44.0 1.0 %collective-permute-start.4 = (bf16[16,768]{1,0:T(8,128)(2,1)}, bf16[16,768]{1,0:T(8,128)(2,1)S(1)}, u32[]{:S(2)}, u32[]{:S(2)}) collective-permute-start(bf16[16,768]{1,0:T(8,128)(2,1)} %get-tuple-element.17), channel_id=1, source_target_pairs={{0,1},{1,2},{2,3},{3,4},{4,5},{5,6},{6,7},{7,8},{8,9},{9,10},{10,1... | collective-permute-start | bytes 73736 | tf_op jit(solution)/shard_map/ppermute | solution.py:544
  45.0 2.3 %collective-permute-start.5 = (bf16[16,768]{1,0:T(8,128)(2,1)}, bf16[16,768]{1,0:T(8,128)(2,1)S(1)}, u32[]{:S(2)}, u32[]{:S(2)}) collective-permute-start(bf16[16,768]{1,0:T(8,128)(2,1)} %get-tuple-element.17), channel_id=1, source_target_pairs={{0,17},{1,18},{2,19},{3,20},{4,21},{5,22},{6,23},{7,24},{8,25},{9,... | collective-permute-start | bytes 73736 | tf_op jit(solution)/shard_map/ppermute | solution.py:544
  47.3 24.2 %collective-permute-done.4.side_ref = bf16[16,768]{1,0:T(8,128)(2,1)S(1)} collective-permute-done((bf16[16,768]{1,0:T(8,128)(2,1)}, bf16[16,768]{1,0:T(8,128)(2,1)S(1)}, u32[]{:S(2)}, u32[]{:S(2)}) %collective-permute-start.4) | collective-permute-done | bytes 24608 | tf_op jit(solution)/shard_map/ppermute | solution.py:544
  71.4 0.0 copy-start.1
  71.4 1.7 %collective-permute-done.5.corner_ref = bf16[16,768]{1,0:T(8,128)(2,1)S(1)} collective-permute-done((bf16[16,768]{1,0:T(8,128)(2,1)}, bf16[16,768]{1,0:T(8,128)(2,1)S(1)}, u32[]{:S(2)}, u32[]{:S(2)}) %collective-permute-start.5) | collective-permute-done | bytes 24608 | tf_op jit(solution)/shard_map/ppermute | solution.py:544
  73.2 0.0 copy-start.2
  73.2 0.0 collective-permute-done.3.rows_ref
  73.2 0.0 all-to-all-done.entries_ref
  73.2 0.0 copy-start
  73.2 0.0 copy-done.1
  73.2 0.6 copy-done.2
  73.8 1.1 %copy-done = bf16[128,104,128]{2,1,0:T(8,128)(2,1)} copy-done((bf16[128,104,128]{2,1,0:T(8,128)(2,1)}, bf16[128,104,128]{2,1,0:T(8,128)(2,1)S(1)}, u32[]{:S(2)}) %copy-start) | copy-done | bytes 3407896
  74.9 4.5 %last_steps.1 = (bf16[16,24576]{1,0:T(8,128)(2,1)}, bf16[16,12288]{1,0:T(8,128)(2,1)}) custom-call(bf16[128,104,128]{2,1,0:T(8,128)(2,1)} %copy-done, bf16[16,24576]{1,0:T(8,128)(2,1)} %get-tuple-element.15.own_ref, bf16[16,6144]{1,0:T(8,128)(2,1)} %collective-permute-done.3.rows_ref, bf16[16,768]{1,0:T(8,128)(2,1)} %copy-done.1, bf16[16,768]{1,0:T(8,128)(2,1)} %copy-done.2), custom_call_target="tpu_custom_call" | custom-call | tf_op jit(solution)/shard_map/last_steps/pallas_call | solution.py:526
Async XLA Ops:
  14.4 15.0 %collective-permute-start = (bf16[32,16,192]{2,1,0:T(8,128)(2,1)}, bf16[32,16,192]{2,1,0:T(8,128)(2,1)}, u32[]{:S(2)}, u32[]{:S(2)}) collective-permute-start(bf16[32,16,192]{2,1,0:T(8,128)(2,1)} %get-tuple-element.13), channel_id=1, source_target_pairs={{0,112},{1,113},{2,114},{3,115},{4,116},{5,117},{6,118},{7,119},{8... | collective-permute-start | bytes 589832 | tf_op jit(solution)/shard_map/ppermute | solution.py:544
  17.0 12.3 %collective-permute-start.1 = (bf16[80,192]{1,0:T(8,128)(2,1)}, bf16[80,192]{1,0:T(8,128)(2,1)S(1)}, u32[]{:S(2)}, u32[]{:S(2)}) collective-permute-start(bf16[80,192]{1,0:T(8,128)(2,1)} %get-tuple-element.14), channel_id=1, source_target_pairs={{0,15},{1,0},{2,1},{3,2},{4,3},{5,4},{6,5},{7,6},{8,7},{9,8},{10,9... | collective-permute-start | bytes 92168 | tf_op jit(solution)/shard_map/ppermute | solution.py:544
  23.3 6.1 %collective-permute-start.2 = (bf16[80,192]{1,0:T(8,128)(2,1)}, bf16[80,192]{1,0:T(8,128)(2,1)S(1)}, u32[]{:S(2)}, u32[]{:S(2)}) collective-permute-start(bf16[80,192]{1,0:T(8,128)(2,1)} %get-tuple-element.14), channel_id=1, source_target_pairs={{0,127},{1,112},{2,113},{3,114},{4,115},{5,116},{6,117},{7,118},{8... | collective-permute-start | bytes 92168 | tf_op jit(solution)/shard_map/ppermute | solution.py:544
  24.0 49.2 %all-to-all-start = ((bf16[128,104,128]{2,1,0:T(8,128)(2,1)}), bf16[128,104,128]{2,1,0:T(8,128)(2,1)S(1)}, u32[]{:S(2)}, u32[]{:S(2)}) async-start(bf16[128,104,128]{2,1,0:T(8,128)(2,1)} %get-tuple-element.10), calls=%async_computation | async-start | bytes 6815744 | tf_op jit(solution)/shard_map/all_to_all | solution.py:583
  29.3 0.6 copy-start.3
  29.3 0.7 copy-start.4
  44.0 29.2 %collective-permute-start.3 = (bf16[16,6144]{1,0:T(8,128)(2,1)}, bf16[16,6144]{1,0:T(8,128)(2,1)}, u32[]{:S(2)}, u32[]{:S(2)}) collective-permute-start(bf16[16,6144]{1,0:T(8,128)(2,1)} %get-tuple-element.16), channel_id=1, source_target_pairs={{0,16},{1,17},{2,18},{3,19},{4,20},{5,21},{6,22},{7,23},{8,24},{9,... | collective-permute-start | bytes 589832 | tf_op jit(solution)/shard_map/ppermute | solution.py:544
  44.0 27.4 %collective-permute-start.4 = (bf16[16,768]{1,0:T(8,128)(2,1)}, bf16[16,768]{1,0:T(8,128)(2,1)S(1)}, u32[]{:S(2)}, u32[]{:S(2)}) collective-permute-start(bf16[16,768]{1,0:T(8,128)(2,1)} %get-tuple-element.17), channel_id=1, source_target_pairs={{0,1},{1,2},{2,3},{3,4},{4,5},{5,6},{6,7},{7,8},{8,9},{9,10},{10,1... | collective-permute-start | bytes 73736 | tf_op jit(solution)/shard_map/ppermute | solution.py:544
  45.0 28.2 %collective-permute-start.5 = (bf16[16,768]{1,0:T(8,128)(2,1)}, bf16[16,768]{1,0:T(8,128)(2,1)S(1)}, u32[]{:S(2)}, u32[]{:S(2)}) collective-permute-start(bf16[16,768]{1,0:T(8,128)(2,1)} %get-tuple-element.17), channel_id=1, source_target_pairs={{0,17},{1,18},{2,19},{3,20},{4,21},{5,22},{6,23},{7,24},{8,25},{9,... | collective-permute-start | bytes 73736 | tf_op jit(solution)/shard_map/ppermute | solution.py:544
  71.4 1.8 %copy-start.1 = (bf16[16,768]{1,0:T(8,128)(2,1)}, bf16[16,768]{1,0:T(8,128)(2,1)S(1)}, u32[]{:S(2)}) copy-start(bf16[16,768]{1,0:T(8,128)(2,1)S(1)} %collective-permute-done.4.side_ref) | copy-start | bytes 73732
  73.2 0.6 copy-start.2
  73.2 1.7 %copy-start = (bf16[128,104,128]{2,1,0:T(8,128)(2,1)}, bf16[128,104,128]{2,1,0:T(8,128)(2,1)S(1)}, u32[]{:S(2)}) copy-start(bf16[128,104,128]{2,1,0:T(8,128)(2,1)S(1)} %all-to-all-done.entries_ref) | copy-start | bytes 10223620

commit v4 on v3

--- a/solution.py
+++ b/solution.py
@@ -16,9 +16,9 @@
 F32 = jnp.float32
 BF16 = jnp.bfloat16
 VMEM_BYTES = 60 * 2**20
+LAST_BYTES = 62 * 2**20
 SMEM = pl.BlockSpec(memory_space=pltpu.SMEM)
 ANY = pl.BlockSpec(memory_space=pl.ANY)
-HBM = pl.BlockSpec(memory_space=pltpu.HBM)
 
 
 def log_step(offset):
@@ -189,22 +189,17 @@
     targets, slots, temper, emb_ref, token_ref, coords_ref, heads_ref, ones_ref, mask_ref,
     net_in, net_first, net_out, qkv_ref, proj_ref, up_ref, down_ref, gain_ref,
     mid0_ref, mid1_ref, upper_ref, left_ref, send_ref,
-    bias_ref, strips_ref, q_w, k_w, v_w, p_ref, staging, blank, sems, blank_sems,
+    bias_ref, strips_ref, q_w, k_w, v_w, p_ref, staging, blank, sems, blank_sem,
 ):
     step = pl.program_id(0)
     n_heads, n_feat = mask_ref.shape
 
-    n_blank = blank.shape[0]
-    blanks = [
-        pltpu.make_async_copy(blank, send_ref.at[pl.ds(n * n_blank, n_blank)], blank_sems.at[n])
-        for n in range(send_ref.shape[0] // n_blank)
-    ]
+    no_slots = pltpu.make_async_copy(blank, send_ref.at[:, pl.ds(96, 8)], blank_sem)
 
     @pl.when(step == 0)
     def _():
         blank[...] = jnp.full(blank.shape, -1.0, BF16)
-        for copy in blanks:
-            copy.start()
+        no_slots.start()
         bias_strips(coords_ref, net_in, net_first[0:1, :], net_out[:, 0, :], strips_ref)
         strips = [strips_ref[h] for h in range(n_heads)]
         for w in range(WIN):
@@ -227,10 +222,15 @@
 
     @pl.when(step == 0)
     def _():
-        for copy in blanks:
-            copy.wait()
-
-    y = dense_tail(x, mixed, proj_ref, up_ref, down_ref, gain_ref).astype(F32)
+        no_slots.wait()
+
+    y = jnp.concatenate(
+        [
+            dense_tail(x[n : n + 256], mixed[n : n + 256], proj_ref, up_ref, down_ref, gain_ref)
+            for n in range(0, x.shape[0], 256)
+        ],
+        0,
+    ).astype(F32)
 
     token = token_ref[...].astype(F32).reshape(1, n_feat)
     for group in range(groups):
@@ -299,7 +299,7 @@
     return [pltpu.VMEM((8, WIN, 128), F32), square, square, square]
 
 
-def first_layer(embedded, targets, slots, temper, token, consts, params, devices, groups=8):
+def first_layer(embedded, targets, slots, temper, token, consts, params, devices, groups=16):
     n_heads, n_feat = consts[3].shape
     columns = embedded.shape[1] // (WIN * n_feat)
     side = jax.ShapeDtypeStruct((80, n_feat), BF16)
@@ -319,9 +319,9 @@
         + [
             pltpu.VMEM((groups * 2 * CELLS, n_heads * CELLS), BF16),
             pltpu.VMEM((2 * columns, 104, 128), BF16),
-            pltpu.VMEM((devices // 8, 104, 128), BF16),
+            pltpu.VMEM((devices, 8, 128), BF16),
             pltpu.SemaphoreType.DMA((2 * columns,)),
-            pltpu.SemaphoreType.DMA((8,)),
+            pltpu.SemaphoreType.DMA,
         ],
         compiler_params=pltpu.CompilerParams(vmem_limit_bytes=VMEM_BYTES),
         cost_estimate=pl.CostEstimate(flops=2 * 10**9, bytes_accessed=6 * 10**6, transcendentals=10**6),
@@ -481,31 +481,33 @@
 
 
 def last_kernel(
-    entries_ref, own_ref, rows_ref, side_ref, corner_ref, features_ref, packed_ref, arrived_ref, sems
+    entries_ref, own_hbm, rows_ref, side_ref, corner_ref, features_ref, packed_ref,
+    marks_ref, held, own_ref, sems, slot_sems,
 ):
     slots = packed_ref.shape[0]
-    part = arrived_ref.shape[0] // 8
-    copies = [
-        pltpu.make_async_copy(
-            entries_ref.at[pl.ds(n * part, part)], arrived_ref.at[pl.ds(n * part, part)], sems.at[n]
-        )
-        for n in range(8)
-    ]
-    for copy in copies:
-        copy.start()
-    merge_features(own_ref, rows_ref, side_ref, corner_ref, features_ref)
-    for copy in copies:
-        copy.wait()
-    marks = arrived_ref[:, 96:, :].astype(F32)
+    marks_copy = pltpu.make_async_copy(entries_ref.at[:, pl.ds(96, 8)], marks_ref, sems.at[0])
+    own_copy = pltpu.make_async_copy(own_hbm, own_ref, sems.at[1])
+    marks_copy.start()
+    own_copy.start()
+    marks_copy.wait()
+    marks = marks_ref[...].astype(F32)
     lane = lax.broadcasted_iota(jnp.int32, marks.shape, 2).astype(F32)
     sender = lax.broadcasted_iota(jnp.int32, marks.shape, 0).astype(F32)
     found = jnp.max(jnp.where(marks == lane, sender, 0.0), 0).astype(jnp.int32)
-    sources = [found[0, slot] for slot in range(slots)]
+    windows = [
+        pltpu.make_async_copy(entries_ref.at[found[0, slot]], held.at[slot], slot_sems.at[slot])
+        for slot in range(slots)
+    ]
+    for copy in windows:
+        copy.start()
+    own_copy.wait()
+    merge_features(own_ref, rows_ref, side_ref, corner_ref, features_ref)
+    for copy in windows:
+        copy.wait()
     lane = lax.broadcasted_iota(jnp.int32, (slots, 128), 1)
 
     def rows_of(at):
-        rows = [arrived_ref[source, at : at + WIN, :].astype(F32) for source in sources]
-        return jnp.swapaxes(jnp.stack(rows, 0), 0, 1)
+        return jnp.swapaxes(held[:, at : at + WIN, :].astype(F32), 0, 1)
 
     for pair in range(WIN // 2):
         even = rows_of(2 * pair * WIN)
@@ -526,10 +528,14 @@
     return pl.pallas_call(
         last_kernel,
         out_shape=(jax.ShapeDtypeStruct(own.shape, BF16), jax.ShapeDtypeStruct((slots, width), BF16)),
-        in_specs=[HBM] + [pl.BlockSpec(memory_space=pltpu.VMEM)] * 4,
+        in_specs=[ANY, ANY] + [pl.BlockSpec(memory_space=pltpu.VMEM)] * 3,
         out_specs=(pl.BlockSpec(memory_space=pltpu.VMEM),) * 2,
-        scratch_shapes=[pltpu.VMEM(arrived.shape, BF16), pltpu.SemaphoreType.DMA((8,))],
-        compiler_params=pltpu.CompilerParams(vmem_limit_bytes=VMEM_BYTES),
+        scratch_shapes=[
+            pltpu.VMEM((arrived.shape[0], 8, 128), BF16),
+            pltpu.VMEM((slots,) + arrived.shape[1:], BF16),
+        ]
+        + [pltpu.VMEM(own.shape, BF16), pltpu.SemaphoreType.DMA((2,)), pltpu.SemaphoreType.DMA((slots,))],
+        compiler_params=pltpu.CompilerParams(vmem_limit_bytes=LAST_BYTES),
         name="last_steps",
     )(arrived, own, rows, side, corner)
 

time: 79.6 us -> 78.4 us (0.985)
  local copies, waits for them, and re-layouts: 2.33 us -> 1.36 us
  Pallas kernels: 32.2 us -> 31.3 us
  starting transfers between devices: 17.5 us -> 18.4 us
    all_to_all x1, starting transfers between devices: 4.67 us -> 5.92 us  [local(): lax.all_to_all(send, ('row', 'col'), split_axis=0, concat_axis=0, tiled=T...]
    unnamed x10 -> x12, local copies, waits for them, and re-layouts: 2.33 us -> 1.36 us
where the time goes in v4:
time: 78.4 us; the launch traced here: 78.1 us
  Pallas kernels  31.3 us (40%)
  waiting for transfers between devices  25.5 us (33%)
  starting transfers between devices  18.4 us (23%)
  local copies, waits for them, and re-layouts  1.36 us (2%)
  between operations  0.88 us (1%)
    ppermute x6, waiting for transfers between devices, moved(): return lax.ppermute(block, ('row', 'col'), route)  25.5 us
    pallas_call x1, Pallas kernels, second_layer(): pl.pallas_call(functools.partial(second_kernel, groups), grid=(n_half //...  14 us
    pallas_call x1, Pallas kernels, first_layer(): pl.pallas_call(functools.partial(first_kernel, groups), grid=(columns //...  13.1 us
    ppermute x6, starting transfers between devices, moved(): return lax.ppermute(block, ('row', 'col'), route)  12.5 us
    all_to_all x1, starting transfers between devices, local(): lax.all_to_all(send, ('row', 'col'), split_axis=0, concat_axis=0, tiled=T...  5.92 us
    pallas_call x1, Pallas kernels, last_steps(): pl.pallas_call(last_kernel, out_shape=(jax.ShapeDtypeStruct(own.shape, BF...  4.23 us
  transfers between devices with their start and end apart: 7, of which 2 were waited for; matrix products, arithmetic and copies ran while one was open for 1% of the time, Pallas kernels for 18%

profile of v4, /device:TPU:0, one launch (start us, length us, event | category | flops | bytes accessed | tf_op | source)
XLA Modules:
  0.0 78.1 jit_solution(5068947246828177966)
XLA Ops:
  0.6 13.1 %first_layer.1 = (bf16[32,32,192]{2,1,0:T(8,128)(2,1)}, bf16[32,32,192]{2,1,0:T(8,128)(2,1)}, bf16[32,16,192]{2,1,0:T(8,128)(2,1)}, bf16[80,192]{1,0:T(8,128)(2,1)}, bf16[128,104,128]{2,1,0:T(8,128)(2,1)}) custom-call(s32[2,16]{1,0:T(2,128)} %targets.1, s32[2,16]{1,0:T(2,128)} %slots.1, f32[2,6]{1,0:T(2,128)} %temper.3, bf16[16,24576]{1,0:T(8,128)(2,1)} %emb_ref.1, ...), custom_call_target="tpu_custom_call" | custom-call | flops 2000000000 | bytes 6000000 | tf_op jit(solution)/shard_map/first_layer/pallas_call | solution.py:309
  13.7 2.5 %collective-permute-start = (bf16[32,16,192]{2,1,0:T(8,128)(2,1)}, bf16[32,16,192]{2,1,0:T(8,128)(2,1)S(1)}, u32[]{:S(2)}, u32[]{:S(2)}) collective-permute-start(bf16[32,16,192]{2,1,0:T(8,128)(2,1)} %get-tuple-element.13), channel_id=1, source_target_pairs={{0,112},{1,113},{2,114},{3,115},{4,116},{5,117},{6,118},{7,119},{8... | collective-permute-start | bytes 589832 | tf_op jit(solution)/shard_map/ppermute | solution.py:550
  16.2 6.2 %collective-permute-start.1 = (bf16[80,192]{1,0:T(8,128)(2,1)}, bf16[80,192]{1,0:T(8,128)(2,1)S(1)}, u32[]{:S(2)}, u32[]{:S(2)}) collective-permute-start(bf16[80,192]{1,0:T(8,128)(2,1)} %get-tuple-element.14), channel_id=1, source_target_pairs={{0,15},{1,0},{2,1},{3,2},{4,3},{5,4},{6,5},{7,6},{8,7},{9,8},{10,9... | collective-permute-start | bytes 92168 | tf_op jit(solution)/shard_map/ppermute | solution.py:550
  22.4 0.7 collective-permute-start.2
  23.2 5.9 %all-to-all-start = ((bf16[128,104,128]{2,1,0:T(8,128)(2,1)}), bf16[128,104,128]{2,1,0:T(8,128)(2,1)}, u32[]{:S(2)}, u32[]{:S(2)}) async-start(bf16[128,104,128]{2,1,0:T(8,128)(2,1)} %get-tuple-element.10), calls=%async_computation | async-start | bytes 6815744 | tf_op jit(solution)/shard_map/all_to_all | solution.py:589
  29.1 0.6 pad_add_fusion.place
  29.7 0.0 collective-permute-done.1.right_ref
  29.7 0.0 copy-start.4
  29.7 0.0 collective-permute-done.2.corner_ref
  29.7 0.0 copy-start.5
  29.7 0.0 collective-permute-done.below_ref
  29.7 0.0 copy-start.3
  29.8 0.6 copy-done.4
  30.3 0.0 copy-done.5
  30.4 0.1 copy-done.3
  30.4 14.0 %second_layer.1 = (bf16[16,24576]{1,0:T(8,128)(2,1)}, bf16[16,6144]{1,0:T(8,128)(2,1)}, bf16[16,768]{1,0:T(8,128)(2,1)}) custom-call(s32[4]{0:T(128)} %pad_add_fusion.place, f32[2,6]{1,0:T(2,128)} %temper.3, bf16[32,32,192]{2,1,0:T(8,128)(2,1)} %get-tuple-element.11.mid0_ref, bf16[32,32,192]{2,1,0:T(8,128)(2,1)} %get-tuple-element.12.mid1_ref, ...), custom_call_target="tpu_custom_call" | custom-call | flops 99999997952 | bytes 10000000 | tf_op jit(solution)/shard_map/second_layer/pallas_call | solution.py:445
  44.5 0.0 collective-permute-start.3
  44.5 0.7 collective-permute-start.4
  45.2 2.3 %collective-permute-start.5 = (bf16[16,768]{1,0:T(8,128)(2,1)}, bf16[16,768]{1,0:T(8,128)(2,1)S(1)}, u32[]{:S(2)}, u32[]{:S(2)}) collective-permute-start(bf16[16,768]{1,0:T(8,128)(2,1)} %get-tuple-element.17), channel_id=1, source_target_pairs={{0,17},{1,18},{2,19},{3,20},{4,21},{5,22},{6,23},{7,24},{8,25},{9,... | collective-permute-start | bytes 73736 | tf_op jit(solution)/shard_map/ppermute | solution.py:550
  47.5 23.7 %collective-permute-done.4.side_ref = bf16[16,768]{1,0:T(8,128)(2,1)S(1)} collective-permute-done((bf16[16,768]{1,0:T(8,128)(2,1)}, bf16[16,768]{1,0:T(8,128)(2,1)S(1)}, u32[]{:S(2)}, u32[]{:S(2)}) %collective-permute-start.4) | collective-permute-done | bytes 24608 | tf_op jit(solution)/shard_map/ppermute | solution.py:550
  71.2 0.0 copy-start.1
  71.3 1.7 %collective-permute-done.5.corner_ref = bf16[16,768]{1,0:T(8,128)(2,1)S(1)} collective-permute-done((bf16[16,768]{1,0:T(8,128)(2,1)}, bf16[16,768]{1,0:T(8,128)(2,1)S(1)}, u32[]{:S(2)}, u32[]{:S(2)}) %collective-permute-start.5) | collective-permute-done | bytes 24608 | tf_op jit(solution)/shard_map/ppermute | solution.py:550
  73.0 0.0 copy-start.2
  73.0 0.0 collective-permute-done.3.rows_ref
  73.0 0.0 copy-start
  73.0 0.0 all-to-all-done.entries_ref
  73.0 0.0 copy-done.1
  73.0 0.6 copy-done.2
  73.6 0.1 copy-done
  73.7 4.2 %last_steps.1 = (bf16[16,24576]{1,0:T(8,128)(2,1)}, bf16[16,12288]{1,0:T(8,128)(2,1)}) custom-call(bf16[128,104,128]{2,1,0:T(8,128)(2,1)} %all-to-all-done.entries_ref, bf16[16,24576]{1,0:T(8,128)(2,1)} %get-tuple-element.15.own_hbm, bf16[16,6144]{1,0:T(8,128)(2,1)} %copy-done, bf16[16,768]{1,0:T(8,128)(2,1)} %copy-done.1, bf16[16,768]{1,0:T(8,128)(2,1)} %copy-done.2), custom_call_target="tpu_custom_call" | custom-call | tf_op jit(solution)/shard_map/last_steps/pallas_call | solution.py:528
Async XLA Ops:
  13.7 16.0 %collective-permute-start = (bf16[32,16,192]{2,1,0:T(8,128)(2,1)}, bf16[32,16,192]{2,1,0:T(8,128)(2,1)S(1)}, u32[]{:S(2)}, u32[]{:S(2)}) collective-permute-start(bf16[32,16,192]{2,1,0:T(8,128)(2,1)} %get-tuple-element.13), channel_id=1, source_target_pairs={{0,112},{1,113},{2,114},{3,115},{4,116},{5,117},{6,118},{7,119},{8... | collective-permute-start | bytes 589832 | tf_op jit(solution)/shard_map/ppermute | solution.py:550
  16.2 13.5 %collective-permute-start.1 = (bf16[80,192]{1,0:T(8,128)(2,1)}, bf16[80,192]{1,0:T(8,128)(2,1)S(1)}, u32[]{:S(2)}, u32[]{:S(2)}) collective-permute-start(bf16[80,192]{1,0:T(8,128)(2,1)} %get-tuple-element.14), channel_id=1, source_target_pairs={{0,15},{1,0},{2,1},{3,2},{4,3},{5,4},{6,5},{7,6},{8,7},{9,8},{10,9... | collective-permute-start | bytes 92168 | tf_op jit(solution)/shard_map/ppermute | solution.py:550
  22.4 7.3 %collective-permute-start.2 = (bf16[80,192]{1,0:T(8,128)(2,1)}, bf16[80,192]{1,0:T(8,128)(2,1)S(1)}, u32[]{:S(2)}, u32[]{:S(2)}) collective-permute-start(bf16[80,192]{1,0:T(8,128)(2,1)} %get-tuple-element.14), channel_id=1, source_target_pairs={{0,127},{1,112},{2,113},{3,114},{4,115},{5,116},{6,117},{7,118},{8... | collective-permute-start | bytes 92168 | tf_op jit(solution)/shard_map/ppermute | solution.py:550
  23.2 49.8 %all-to-all-start = ((bf16[128,104,128]{2,1,0:T(8,128)(2,1)}), bf16[128,104,128]{2,1,0:T(8,128)(2,1)}, u32[]{:S(2)}, u32[]{:S(2)}) async-start(bf16[128,104,128]{2,1,0:T(8,128)(2,1)} %get-tuple-element.10), calls=%async_computation | async-start | bytes 6815744 | tf_op jit(solution)/shard_map/all_to_all | solution.py:589
  29.7 0.6 copy-start.4
  29.7 0.6 copy-start.5
  29.7 0.7 copy-start.3
  44.5 28.5 %collective-permute-start.3 = (bf16[16,6144]{1,0:T(8,128)(2,1)}, bf16[16,6144]{1,0:T(8,128)(2,1)S(1)}, u32[]{:S(2)}, u32[]{:S(2)}) collective-permute-start(bf16[16,6144]{1,0:T(8,128)(2,1)} %get-tuple-element.16), channel_id=1, source_target_pairs={{0,16},{1,17},{2,18},{3,19},{4,20},{5,21},{6,22},{7,23},{8,24},{9,... | collective-permute-start | bytes 589832 | tf_op jit(solution)/shard_map/ppermute | solution.py:550
  44.5 26.8 %collective-permute-start.4 = (bf16[16,768]{1,0:T(8,128)(2,1)}, bf16[16,768]{1,0:T(8,128)(2,1)S(1)}, u32[]{:S(2)}, u32[]{:S(2)}) collective-permute-start(bf16[16,768]{1,0:T(8,128)(2,1)} %get-tuple-element.17), channel_id=1, source_target_pairs={{0,1},{1,2},{2,3},{3,4},{4,5},{5,6},{6,7},{7,8},{8,9},{9,10},{10,1... | collective-permute-start | bytes 73736 | tf_op jit(solution)/shard_map/ppermute | solution.py:550
  45.2 27.8 %collective-permute-start.5 = (bf16[16,768]{1,0:T(8,128)(2,1)}, bf16[16,768]{1,0:T(8,128)(2,1)S(1)}, u32[]{:S(2)}, u32[]{:S(2)}) collective-permute-start(bf16[16,768]{1,0:T(8,128)(2,1)} %get-tuple-element.17), channel_id=1, source_target_pairs={{0,17},{1,18},{2,19},{3,20},{4,21},{5,22},{6,23},{7,24},{8,25},{9,... | collective-permute-start | bytes 73736 | tf_op jit(solution)/shard_map/ppermute | solution.py:550
  71.2 1.8 %copy-start.1 = (bf16[16,768]{1,0:T(8,128)(2,1)}, bf16[16,768]{1,0:T(8,128)(2,1)S(1)}, u32[]{:S(2)}) copy-start(bf16[16,768]{1,0:T(8,128)(2,1)S(1)} %collective-permute-done.4.side_ref) | copy-start | bytes 73732
  73.0 0.6 copy-start.2
  73.0 0.7 copy-start

commit v5 on v4

--- a/solution.py
+++ b/solution.py
@@ -226,8 +226,8 @@
 
     y = jnp.concatenate(
         [
-            dense_tail(x[n : n + 256], mixed[n : n + 256], proj_ref, up_ref, down_ref, gain_ref)
-            for n in range(0, x.shape[0], 256)
+            dense_tail(x[n : n + 512], mixed[n : n + 512], proj_ref, up_ref, down_ref, gain_ref)
+            for n in range(0, x.shape[0], 512)
         ],
         0,
     ).astype(F32)
@@ -481,8 +481,8 @@
 
 
 def last_kernel(
-    entries_ref, own_hbm, rows_ref, side_ref, corner_ref, features_ref, packed_ref,
-    marks_ref, held, own_ref, sems, slot_sems,
+    entries_ref, own_hbm, rows_ref, side_ref, corner_ref, features_hbm, packed_ref,
+    marks_ref, held, own_ref, features_ref, sems, slot_sems,
 ):
     slots = packed_ref.shape[0]
     marks_copy = pltpu.make_async_copy(entries_ref.at[:, pl.ds(96, 8)], marks_ref, sems.at[0])
@@ -502,6 +502,8 @@
         copy.start()
     own_copy.wait()
     merge_features(own_ref, rows_ref, side_ref, corner_ref, features_ref)
+    leave = pltpu.make_async_copy(features_ref, features_hbm, sems.at[2])
+    leave.start()
     for copy in windows:
         copy.wait()
     lane = lax.broadcasted_iota(jnp.int32, (slots, 128), 1)
@@ -522,6 +524,7 @@
             ]
             at = (u * WIN + 2 * pair) * 192
             packed_ref[:, at : at + 384] = jnp.concatenate(joined, 1).astype(BF16)
+    leave.wait()
 
 
 def last_steps(arrived, own, rows, side, corner, slots, width):
@@ -529,12 +532,13 @@
         last_kernel,
         out_shape=(jax.ShapeDtypeStruct(own.shape, BF16), jax.ShapeDtypeStruct((slots, width), BF16)),
         in_specs=[ANY, ANY] + [pl.BlockSpec(memory_space=pltpu.VMEM)] * 3,
-        out_specs=(pl.BlockSpec(memory_space=pltpu.VMEM),) * 2,
+        out_specs=(ANY, pl.BlockSpec(memory_space=pltpu.VMEM)),
         scratch_shapes=[
             pltpu.VMEM((arrived.shape[0], 8, 128), BF16),
             pltpu.VMEM((slots,) + arrived.shape[1:], BF16),
         ]
-        + [pltpu.VMEM(own.shape, BF16), pltpu.SemaphoreType.DMA((2,)), pltpu.SemaphoreType.DMA((slots,))],
+        + [pltpu.VMEM(own.shape, BF16)] * 2
+        + [pltpu.SemaphoreType.DMA((3,)), pltpu.SemaphoreType.DMA((slots,))],
         compiler_params=pltpu.CompilerParams(vmem_limit_bytes=LAST_BYTES),
         name="last_steps",
     )(arrived, own, rows, side, corner)

time: 78.4 us -> 77.8 us (level)
  no operation moved by 1% of the time
where the time goes in v5:
time: 77.8 us; the launch traced here: 77.4 us
  Pallas kernels  30.7 us (39%)
  waiting for transfers between devices  25.5 us (33%)
  starting transfers between devices  18.4 us (24%)
  local copies, waits for them, and re-layouts  1.36 us (2%)
  between operations  0.88 us (1%)
    ppermute x6, waiting for transfers between devices, moved(): return lax.ppermute(block, ('row', 'col'), route)  25.5 us
    pallas_call x1, Pallas kernels, second_layer(): pl.pallas_call(functools.partial(second_kernel, groups), grid=(n_half //...  14 us
    ppermute x6, starting transfers between devices, moved(): return lax.ppermute(block, ('row', 'col'), route)  12.5 us
    pallas_call x1, Pallas kernels, first_layer(): pl.pallas_call(functools.partial(first_kernel, groups), grid=(columns //...  12.4 us
    all_to_all x1, starting transfers between devices, local(): lax.all_to_all(send, ('row', 'col'), split_axis=0, concat_axis=0, tiled=T...  5.92 us
    pallas_call x1, Pallas kernels, last_steps(): pl.pallas_call(last_kernel, out_shape=(jax.ShapeDtypeStruct(own.shape, BF...  4.25 us
  transfers between devices with their start and end apart: 7, of which 2 were waited for; matrix products, arithmetic and copies ran while one was open for 1% of the time, Pallas kernels for 18%

profile of v5, /device:TPU:0, one launch (start us, length us, event | category | flops | bytes accessed | tf_op | source)
XLA Modules:
  0.0 77.4 jit_solution(10397238568182871922)
XLA Ops:
  0.6 12.4 %first_layer.1 = (bf16[32,32,192]{2,1,0:T(8,128)(2,1)}, bf16[32,32,192]{2,1,0:T(8,128)(2,1)}, bf16[32,16,192]{2,1,0:T(8,128)(2,1)}, bf16[80,192]{1,0:T(8,128)(2,1)}, bf16[128,104,128]{2,1,0:T(8,128)(2,1)}) custom-call(s32[2,16]{1,0:T(2,128)} %targets.1, s32[2,16]{1,0:T(2,128)} %slots.1, f32[2,6]{1,0:T(2,128)} %temper.3, bf16[16,24576]{1,0:T(8,128)(2,1)} %emb_ref.1, ...), custom_call_target="tpu_custom_call" | custom-call | flops 2000000000 | bytes 6000000 | tf_op jit(solution)/shard_map/first_layer/pallas_call | solution.py:309
  13.1 2.5 %collective-permute-start = (bf16[32,16,192]{2,1,0:T(8,128)(2,1)}, bf16[32,16,192]{2,1,0:T(8,128)(2,1)S(1)}, u32[]{:S(2)}, u32[]{:S(2)}) collective-permute-start(bf16[32,16,192]{2,1,0:T(8,128)(2,1)} %get-tuple-element.13), channel_id=1, source_target_pairs={{0,112},{1,113},{2,114},{3,115},{4,116},{5,117},{6,118},{7,119},{8... | collective-permute-start | bytes 589832 | tf_op jit(solution)/shard_map/ppermute | solution.py:554
  15.6 6.2 %collective-permute-start.1 = (bf16[80,192]{1,0:T(8,128)(2,1)}, bf16[80,192]{1,0:T(8,128)(2,1)S(1)}, u32[]{:S(2)}, u32[]{:S(2)}) collective-permute-start(bf16[80,192]{1,0:T(8,128)(2,1)} %get-tuple-element.14), channel_id=1, source_target_pairs={{0,15},{1,0},{2,1},{3,2},{4,3},{5,4},{6,5},{7,6},{8,7},{9,8},{10,9... | collective-permute-start | bytes 92168 | tf_op jit(solution)/shard_map/ppermute | solution.py:554
  21.8 0.8 collective-permute-start.2
  22.5 5.9 %all-to-all-start = ((bf16[128,104,128]{2,1,0:T(8,128)(2,1)}), bf16[128,104,128]{2,1,0:T(8,128)(2,1)}, u32[]{:S(2)}, u32[]{:S(2)}) async-start(bf16[128,104,128]{2,1,0:T(8,128)(2,1)} %get-tuple-element.10), calls=%async_computation | async-start | bytes 6815744 | tf_op jit(solution)/shard_map/all_to_all | solution.py:593
  28.4 0.6 pad_add_fusion.place
  29.1 0.0 collective-permute-done.1.right_ref
  29.1 0.0 copy-start.4
  29.1 0.0 collective-permute-done.2.corner_ref
  29.1 0.0 copy-start.5
  29.1 0.0 collective-permute-done.below_ref
  29.1 0.0 copy-start.3
  29.1 0.6 copy-done.4
  29.7 0.0 copy-done.5
  29.7 0.1 copy-done.3
  29.8 14.0 %second_layer.1 = (bf16[16,24576]{1,0:T(8,128)(2,1)}, bf16[16,6144]{1,0:T(8,128)(2,1)}, bf16[16,768]{1,0:T(8,128)(2,1)}) custom-call(s32[4]{0:T(128)} %pad_add_fusion.place, f32[2,6]{1,0:T(2,128)} %temper.3, bf16[32,32,192]{2,1,0:T(8,128)(2,1)} %get-tuple-element.11.mid0_ref, bf16[32,32,192]{2,1,0:T(8,128)(2,1)} %get-tuple-element.12.mid1_ref, ...), custom_call_target="tpu_custom_call" | custom-call | flops 99999997952 | bytes 10000000 | tf_op jit(solution)/shard_map/second_layer/pallas_call | solution.py:445
  43.8 0.0 collective-permute-start.3
  43.8 0.7 collective-permute-start.4
  44.6 2.3 %collective-permute-start.5 = (bf16[16,768]{1,0:T(8,128)(2,1)}, bf16[16,768]{1,0:T(8,128)(2,1)S(1)}, u32[]{:S(2)}, u32[]{:S(2)}) collective-permute-start(bf16[16,768]{1,0:T(8,128)(2,1)} %get-tuple-element.17), channel_id=1, source_target_pairs={{0,17},{1,18},{2,19},{3,20},{4,21},{5,22},{6,23},{7,24},{8,25},{9,... | collective-permute-start | bytes 73736 | tf_op jit(solution)/shard_map/ppermute | solution.py:554
  46.9 23.7 %collective-permute-done.4.side_ref = bf16[16,768]{1,0:T(8,128)(2,1)S(1)} collective-permute-done((bf16[16,768]{1,0:T(8,128)(2,1)}, bf16[16,768]{1,0:T(8,128)(2,1)S(1)}, u32[]{:S(2)}, u32[]{:S(2)}) %collective-permute-start.4) | collective-permute-done | bytes 24608 | tf_op jit(solution)/shard_map/ppermute | solution.py:554
  70.6 0.0 copy-start.1
  70.6 1.7 %collective-permute-done.5.corner_ref = bf16[16,768]{1,0:T(8,128)(2,1)S(1)} collective-permute-done((bf16[16,768]{1,0:T(8,128)(2,1)}, bf16[16,768]{1,0:T(8,128)(2,1)S(1)}, u32[]{:S(2)}, u32[]{:S(2)}) %collective-permute-start.5) | collective-permute-done | bytes 24608 | tf_op jit(solution)/shard_map/ppermute | solution.py:554
  72.3 0.0 copy-start.2
  72.3 0.0 collective-permute-done.3.rows_ref
  72.3 0.0 copy-start
  72.4 0.0 all-to-all-done.entries_ref
  72.4 0.0 copy-done.1
  72.4 0.6 copy-done.2
  72.9 0.1 copy-done
  73.0 4.2 %last_steps.1 = (bf16[16,24576]{1,0:T(8,128)(2,1)}, bf16[16,12288]{1,0:T(8,128)(2,1)}) custom-call(bf16[128,104,128]{2,1,0:T(8,128)(2,1)} %all-to-all-done.entries_ref, bf16[16,24576]{1,0:T(8,128)(2,1)} %get-tuple-element.15.own_hbm, bf16[16,6144]{1,0:T(8,128)(2,1)} %copy-done, bf16[16,768]{1,0:T(8,128)(2,1)} %copy-done.1, bf16[16,768]{1,0:T(8,128)(2,1)} %copy-done.2), custom_call_target="tpu_custom_call" | custom-call | tf_op jit(solution)/shard_map/last_steps/pallas_call | solution.py:531
Async XLA Ops:
  13.1 16.0 %collective-permute-start = (bf16[32,16,192]{2,1,0:T(8,128)(2,1)}, bf16[32,16,192]{2,1,0:T(8,128)(2,1)S(1)}, u32[]{:S(2)}, u32[]{:S(2)}) collective-permute-start(bf16[32,16,192]{2,1,0:T(8,128)(2,1)} %get-tuple-element.13), channel_id=1, source_target_pairs={{0,112},{1,113},{2,114},{3,115},{4,116},{5,117},{6,118},{7,119},{8... | collective-permute-start | bytes 589832 | tf_op jit(solution)/shard_map/ppermute | solution.py:554
  15.6 13.5 %collective-permute-start.1 = (bf16[80,192]{1,0:T(8,128)(2,1)}, bf16[80,192]{1,0:T(8,128)(2,1)S(1)}, u32[]{:S(2)}, u32[]{:S(2)}) collective-permute-start(bf16[80,192]{1,0:T(8,128)(2,1)} %get-tuple-element.14), channel_id=1, source_target_pairs={{0,15},{1,0},{2,1},{3,2},{4,3},{5,4},{6,5},{7,6},{8,7},{9,8},{10,9... | collective-permute-start | bytes 92168 | tf_op jit(solution)/shard_map/ppermute | solution.py:554
  21.8 7.3 %collective-permute-start.2 = (bf16[80,192]{1,0:T(8,128)(2,1)}, bf16[80,192]{1,0:T(8,128)(2,1)S(1)}, u32[]{:S(2)}, u32[]{:S(2)}) collective-permute-start(bf16[80,192]{1,0:T(8,128)(2,1)} %get-tuple-element.14), channel_id=1, source_target_pairs={{0,127},{1,112},{2,113},{3,114},{4,115},{5,116},{6,117},{7,118},{8... | collective-permute-start | bytes 92168 | tf_op jit(solution)/shard_map/ppermute | solution.py:554
  22.5 49.8 %all-to-all-start = ((bf16[128,104,128]{2,1,0:T(8,128)(2,1)}), bf16[128,104,128]{2,1,0:T(8,128)(2,1)}, u32[]{:S(2)}, u32[]{:S(2)}) async-start(bf16[128,104,128]{2,1,0:T(8,128)(2,1)} %get-tuple-element.10), calls=%async_computation | async-start | bytes 6815744 | tf_op jit(solution)/shard_map/all_to_all | solution.py:593
  29.1 0.6 copy-start.4
  29.1 0.6 copy-start.5
  29.1 0.7 copy-start.3
  43.8 28.5 %collective-permute-start.3 = (bf16[16,6144]{1,0:T(8,128)(2,1)}, bf16[16,6144]{1,0:T(8,128)(2,1)S(1)}, u32[]{:S(2)}, u32[]{:S(2)}) collective-permute-start(bf16[16,6144]{1,0:T(8,128)(2,1)} %get-tuple-element.16), channel_id=1, source_target_pairs={{0,16},{1,17},{2,18},{3,19},{4,20},{5,21},{6,22},{7,23},{8,24},{9,... | collective-permute-start | bytes 589832 | tf_op jit(solution)/shard_map/ppermute | solution.py:554
  43.8 26.8 %collective-permute-start.4 = (bf16[16,768]{1,0:T(8,128)(2,1)}, bf16[16,768]{1,0:T(8,128)(2,1)S(1)}, u32[]{:S(2)}, u32[]{:S(2)}) collective-permute-start(bf16[16,768]{1,0:T(8,128)(2,1)} %get-tuple-element.17), channel_id=1, source_target_pairs={{0,1},{1,2},{2,3},{3,4},{4,5},{5,6},{6,7},{7,8},{8,9},{9,10},{10,1... | collective-permute-start | bytes 73736 | tf_op jit(solution)/shard_map/ppermute | solution.py:554
  44.6 27.8 %collective-permute-start.5 = (bf16[16,768]{1,0:T(8,128)(2,1)}, bf16[16,768]{1,0:T(8,128)(2,1)S(1)}, u32[]{:S(2)}, u32[]{:S(2)}) collective-permute-start(bf16[16,768]{1,0:T(8,128)(2,1)} %get-tuple-element.17), channel_id=1, source_target_pairs={{0,17},{1,18},{2,19},{3,20},{4,21},{5,22},{6,23},{7,24},{8,25},{9,... | collective-permute-start | bytes 73736 | tf_op jit(solution)/shard_map/ppermute | solution.py:554
  70.6 1.8 %copy-start.1 = (bf16[16,768]{1,0:T(8,128)(2,1)}, bf16[16,768]{1,0:T(8,128)(2,1)S(1)}, u32[]{:S(2)}) copy-start(bf16[16,768]{1,0:T(8,128)(2,1)S(1)} %collective-permute-done.4.side_ref) | copy-start | bytes 73732
  72.3 0.6 copy-start.2
  72.3 0.7 copy-start

commit v6 on v5

--- a/solution.py
+++ b/solution.py
@@ -194,7 +194,7 @@
     step = pl.program_id(0)
     n_heads, n_feat = mask_ref.shape
 
-    no_slots = pltpu.make_async_copy(blank, send_ref.at[:, pl.ds(96, 8)], blank_sem)
+    no_slots = pltpu.make_async_copy(blank, send_ref.at[:, pl.ds(24, 1)], blank_sem)
 
     @pl.when(step == 0)
     def _():
@@ -257,11 +257,11 @@
                         left_ref[64:] = halves[0]
 
             slot = j * 2 + i
-            staging[slot, :64] = tile[:, :128].astype(BF16)
+            staging[slot, :16] = tile[:, :128].reshape(16, 4, 128).astype(BF16)
             tails = tile[:, 128:].reshape(4, 2, WIN, 64)
             joined = jnp.concatenate([tails[:, 0], tails[:, 1]], -1)
-            staging[slot, 64:96] = joined.reshape(32, 128).astype(BF16)
-            staging[slot, 96:] = jnp.full((8, 128), slots[i, j].astype(F32)).astype(BF16)
+            staging[slot, 16:24] = joined.reshape(8, 4, 128).astype(BF16)
+            staging[slot, 24:] = jnp.full((1, 4, 128), slots[i, j].astype(F32)).astype(BF16)
 
             @pl.when(target >= 0)
             def _(slot=slot, target=target):
@@ -309,7 +309,7 @@
     return pl.pallas_call(
         functools.partial(first_kernel, groups),
         grid=(columns // groups,),
-        out_shape=(mid, mid, upper, side, jax.ShapeDtypeStruct((devices, 104, 128), BF16)),
+        out_shape=(mid, mid, upper, side, jax.ShapeDtypeStruct((devices, 25, 4, 128), BF16)),
         in_specs=[SMEM, SMEM, SMEM, pl.BlockSpec((2 * WIN, groups * WIN * n_feat), lambda g: (0, g))]
         + [whole(a) for a in (token,) + consts]
         + [layer_spec(a, n, 0) for n, a in enumerate(params)],
@@ -318,8 +318,8 @@
         + layer_scratch(n_heads, n_feat)
         + [
             pltpu.VMEM((groups * 2 * CELLS, n_heads * CELLS), BF16),
-            pltpu.VMEM((2 * columns, 104, 128), BF16),
-            pltpu.VMEM((devices, 8, 128), BF16),
+            pltpu.VMEM((2 * columns, 25, 4, 128), BF16),
+            pltpu.VMEM((devices, 1, 4, 128), BF16),
             pltpu.SemaphoreType.DMA((2 * columns,)),
             pltpu.SemaphoreType.DMA,
         ],
@@ -485,12 +485,12 @@
     marks_ref, held, own_ref, features_ref, sems, slot_sems,
 ):
     slots = packed_ref.shape[0]
-    marks_copy = pltpu.make_async_copy(entries_ref.at[:, pl.ds(96, 8)], marks_ref, sems.at[0])
+    marks_copy = pltpu.make_async_copy(entries_ref.at[:, pl.ds(24, 1)], marks_ref, sems.at[0])
     own_copy = pltpu.make_async_copy(own_hbm, own_ref, sems.at[1])
     marks_copy.start()
     own_copy.start()
     marks_copy.wait()
-    marks = marks_ref[...].astype(F32)
+    marks = marks_ref[...][:, 0].astype(F32)
     lane = lax.broadcasted_iota(jnp.int32, marks.shape, 2).astype(F32)
     sender = lax.broadcasted_iota(jnp.int32, marks.shape, 0).astype(F32)
     found = jnp.max(jnp.where(marks == lane, sender, 0.0), 0).astype(jnp.int32)
@@ -509,7 +509,8 @@
     lane = lax.broadcasted_iota(jnp.int32, (slots, 128), 1)
 
     def rows_of(at):
-        return jnp.swapaxes(held[:, at : at + WIN, :].astype(F32), 0, 1)
+        rows = held[:, at // 4 : at // 4 + 2].astype(F32).reshape(slots, WIN, 128)
+        return jnp.swapaxes(rows, 0, 1)
 
     for pair in range(WIN // 2):
         even = rows_of(2 * pair * WIN)
@@ -534,7 +535,7 @@
         in_specs=[ANY, ANY] + [pl.BlockSpec(memory_space=pltpu.VMEM)] * 3,
         out_specs=(ANY, pl.BlockSpec(memory_space=pltpu.VMEM)),
         scratch_shapes=[
-            pltpu.VMEM((arrived.shape[0], 8, 128), BF16),
+            pltpu.VMEM((arrived.shape[0], 1, 4, 128), BF16),
             pltpu.VMEM((slots,) + arrived.shape[1:], BF16),
         ]
         + [pltpu.VMEM(own.shape, BF16)] * 2

time: 77.8 us -> 76.3 us (0.981)
  waiting for transfers between devices: 25.5 us -> 24.1 us
    ppermute x6, waiting for transfers between devices: 25.5 us -> 24.1 us  [moved(): return lax.ppermute(block, ('row', 'col'), route)]
  transfers between devices with their start and end apart: 7 -> 7, of which waited for: 2 -> 2; matrix products, arithmetic and copies ran while one was open for 1% -> 1% of each run, Pallas kernels for 18% -> 19%
where the time goes in v6:
time: 76.3 us; the launch traced here: 75.9 us
  Pallas kernels  30.7 us (40%)
  waiting for transfers between devices  24.1 us (32%)
  starting transfers between devices  18.3 us (24%)
  local copies, waits for them, and re-layouts  1.36 us (2%)
  between operations  0.88 us (1%)
    ppermute x6, waiting for transfers between devices, moved(): return lax.ppermute(block, ('row', 'col'), route)  24.1 us
    pallas_call x1, Pallas kernels, second_layer(): pl.pallas_call(functools.partial(second_kernel, groups), grid=(n_half //...  14 us
    pallas_call x1, Pallas kernels, first_layer(): pl.pallas_call(functools.partial(first_kernel, groups), grid=(columns //...  12.5 us
    ppermute x6, starting transfers between devices, moved(): return lax.ppermute(block, ('row', 'col'), route)  12.4 us
    all_to_all x1, starting transfers between devices, local(): lax.all_to_all(send, ('row', 'col'), split_axis=0, concat_axis=0, tiled=T...  5.92 us
    pallas_call x1, Pallas kernels, last_steps(): pl.pallas_call(last_kernel, out_shape=(jax.ShapeDtypeStruct(own.shape, BF...  4.16 us
  transfers between devices with their start and end apart: 7, of which 2 were waited for; matrix products, arithmetic and copies ran while one was open for 1% of the time, Pallas kernels for 19%

profile of v6, /device:TPU:0, one launch (start us, length us, event | category | flops | bytes accessed | tf_op | source)
XLA Modules:
  0.0 75.9 jit_solution(8147887490530521758)
XLA Ops:
  0.6 12.5 %first_layer.1 = (bf16[32,32,192]{2,1,0:T(8,128)(2,1)}, bf16[32,32,192]{2,1,0:T(8,128)(2,1)}, bf16[32,16,192]{2,1,0:T(8,128)(2,1)}, bf16[80,192]{1,0:T(8,128)(2,1)}, bf16[128,25,4,128]{3,2,1,0:T(4,128)(2,1)}) custom-call(s32[2,16]{1,0:T(2,128)} %targets.1, s32[2,16]{1,0:T(2,128)} %slots.1, f32[2,6]{1,0:T(2,128)} %temper.3, bf16[16,24576]{1,0:T(8,128)(2,1)} %emb_ref.1, ...), custom_call_target="tpu_custom_call" | custom-call | flops 2000000000 | bytes 6000000 | tf_op jit(solution)/shard_map/first_layer/pallas_call | solution.py:309
  13.1 2.6 %collective-permute-start = (bf16[32,16,192]{2,1,0:T(8,128)(2,1)}, bf16[32,16,192]{2,1,0:T(8,128)(2,1)S(1)}, u32[]{:S(2)}, u32[]{:S(2)}) collective-permute-start(bf16[32,16,192]{2,1,0:T(8,128)(2,1)} %get-tuple-element.13), channel_id=1, source_target_pairs={{0,112},{1,113},{2,114},{3,115},{4,116},{5,117},{6,118},{7,119},{8... | collective-permute-start | bytes 589832 | tf_op jit(solution)/shard_map/ppermute | solution.py:555
  15.7 6.2 %collective-permute-start.1 = (bf16[80,192]{1,0:T(8,128)(2,1)}, bf16[80,192]{1,0:T(8,128)(2,1)S(1)}, u32[]{:S(2)}, u32[]{:S(2)}) collective-permute-start(bf16[80,192]{1,0:T(8,128)(2,1)} %get-tuple-element.14), channel_id=1, source_target_pairs={{0,15},{1,0},{2,1},{3,2},{4,3},{5,4},{6,5},{7,6},{8,7},{9,8},{10,9... | collective-permute-start | bytes 92168 | tf_op jit(solution)/shard_map/ppermute | solution.py:555
  21.9 0.6 collective-permute-start.2
  22.5 5.9 %all-to-all-start = ((bf16[128,25,4,128]{3,2,1,0:T(4,128)(2,1)}), bf16[128,25,4,128]{3,2,1,0:T(4,128)(2,1)}, u32[]{:S(2)}, u32[]{:S(2)}) async-start(bf16[128,25,4,128]{3,2,1,0:T(4,128)(2,1)} %get-tuple-element.10), calls=%async_computation | async-start | bytes 6553600 | tf_op jit(solution)/shard_map/all_to_all | solution.py:594
  28.5 0.6 pad_add_fusion.place
  29.0 0.0 collective-permute-done.1.right_ref
  29.0 0.0 copy-start.4
  29.0 0.0 collective-permute-done.2.corner_ref
  29.0 0.0 copy-start.5
  29.0 0.0 collective-permute-done.below_ref
  29.0 0.0 copy-start.3
  29.1 0.6 copy-done.4
  29.6 0.0 copy-done.5
  29.7 0.1 copy-done.3
  29.7 14.0 %second_layer.1 = (bf16[16,24576]{1,0:T(8,128)(2,1)}, bf16[16,6144]{1,0:T(8,128)(2,1)}, bf16[16,768]{1,0:T(8,128)(2,1)}) custom-call(s32[4]{0:T(128)} %pad_add_fusion.place, f32[2,6]{1,0:T(2,128)} %temper.3, bf16[32,32,192]{2,1,0:T(8,128)(2,1)} %get-tuple-element.11.mid0_ref, bf16[32,32,192]{2,1,0:T(8,128)(2,1)} %get-tuple-element.12.mid1_ref, ...), custom_call_target="tpu_custom_call" | custom-call | flops 99999997952 | bytes 10000000 | tf_op jit(solution)/shard_map/second_layer/pallas_call | solution.py:445
  43.8 0.0 collective-permute-start.3
  43.8 0.7 collective-permute-start.4
  44.6 2.3 %collective-permute-start.5 = (bf16[16,768]{1,0:T(8,128)(2,1)}, bf16[16,768]{1,0:T(8,128)(2,1)S(1)}, u32[]{:S(2)}, u32[]{:S(2)}) collective-permute-start(bf16[16,768]{1,0:T(8,128)(2,1)} %get-tuple-element.17), channel_id=1, source_target_pairs={{0,17},{1,18},{2,19},{3,20},{4,21},{5,22},{6,23},{7,24},{8,25},{9,... | collective-permute-start | bytes 73736 | tf_op jit(solution)/shard_map/ppermute | solution.py:555
  46.9 22.4 %collective-permute-done.4.side_ref = bf16[16,768]{1,0:T(8,128)(2,1)S(1)} collective-permute-done((bf16[16,768]{1,0:T(8,128)(2,1)}, bf16[16,768]{1,0:T(8,128)(2,1)S(1)}, u32[]{:S(2)}, u32[]{:S(2)}) %collective-permute-start.4) | collective-permute-done | bytes 24608 | tf_op jit(solution)/shard_map/ppermute | solution.py:555
  69.2 0.0 copy-start.1
  69.2 1.7 %collective-permute-done.5.corner_ref = bf16[16,768]{1,0:T(8,128)(2,1)S(1)} collective-permute-done((bf16[16,768]{1,0:T(8,128)(2,1)}, bf16[16,768]{1,0:T(8,128)(2,1)S(1)}, u32[]{:S(2)}, u32[]{:S(2)}) %collective-permute-start.5) | collective-permute-done | bytes 24608 | tf_op jit(solution)/shard_map/ppermute | solution.py:555
  70.9 0.0 copy-start.2
  70.9 0.0 collective-permute-done.3.rows_ref
  70.9 0.0 copy-start
  70.9 0.0 all-to-all-done.entries_ref
  71.0 0.0 copy-done.1
  71.0 0.6 copy-done.2
  71.5 0.1 copy-done
  71.6 4.2 %last_steps.1 = (bf16[16,24576]{1,0:T(8,128)(2,1)}, bf16[16,12288]{1,0:T(8,128)(2,1)}) custom-call(bf16[128,25,4,128]{3,2,1,0:T(4,128)(2,1)} %all-to-all-done.entries_ref, bf16[16,24576]{1,0:T(8,128)(2,1)} %get-tuple-element.15.own_hbm, bf16[16,6144]{1,0:T(8,128)(2,1)} %copy-done, bf16[16,768]{1,0:T(8,128)(2,1)} %copy-done.1, bf16[16,768]{1,0:T(8,128)(2,1)} %copy-done.2), custom_call_target="tpu_custom_call" | custom-call | tf_op jit(solution)/shard_map/last_steps/pallas_call | solution.py:532
Async XLA Ops:
  13.1 15.9 %collective-permute-start = (bf16[32,16,192]{2,1,0:T(8,128)(2,1)}, bf16[32,16,192]{2,1,0:T(8,128)(2,1)S(1)}, u32[]{:S(2)}, u32[]{:S(2)}) collective-permute-start(bf16[32,16,192]{2,1,0:T(8,128)(2,1)} %get-tuple-element.13), channel_id=1, source_target_pairs={{0,112},{1,113},{2,114},{3,115},{4,116},{5,117},{6,118},{7,119},{8... | collective-permute-start | bytes 589832 | tf_op jit(solution)/shard_map/ppermute | solution.py:555
  15.7 13.3 %collective-permute-start.1 = (bf16[80,192]{1,0:T(8,128)(2,1)}, bf16[80,192]{1,0:T(8,128)(2,1)S(1)}, u32[]{:S(2)}, u32[]{:S(2)}) collective-permute-start(bf16[80,192]{1,0:T(8,128)(2,1)} %get-tuple-element.14), channel_id=1, source_target_pairs={{0,15},{1,0},{2,1},{3,2},{4,3},{5,4},{6,5},{7,6},{8,7},{9,8},{10,9... | collective-permute-start | bytes 92168 | tf_op jit(solution)/shard_map/ppermute | solution.py:555
  21.9 7.1 %collective-permute-start.2 = (bf16[80,192]{1,0:T(8,128)(2,1)}, bf16[80,192]{1,0:T(8,128)(2,1)S(1)}, u32[]{:S(2)}, u32[]{:S(2)}) collective-permute-start(bf16[80,192]{1,0:T(8,128)(2,1)} %get-tuple-element.14), channel_id=1, source_target_pairs={{0,127},{1,112},{2,113},{3,114},{4,115},{5,116},{6,117},{7,118},{8... | collective-permute-start | bytes 92168 | tf_op jit(solution)/shard_map/ppermute | solution.py:555
  22.5 48.4 %all-to-all-start = ((bf16[128,25,4,128]{3,2,1,0:T(4,128)(2,1)}), bf16[128,25,4,128]{3,2,1,0:T(4,128)(2,1)}, u32[]{:S(2)}, u32[]{:S(2)}) async-start(bf16[128,25,4,128]{3,2,1,0:T(4,128)(2,1)} %get-tuple-element.10), calls=%async_computation | async-start | bytes 6553600 | tf_op jit(solution)/shard_map/all_to_all | solution.py:594
  29.0 0.6 copy-start.4
  29.0 0.6 copy-start.5
  29.0 0.7 copy-start.3
  43.8 27.1 %collective-permute-start.3 = (bf16[16,6144]{1,0:T(8,128)(2,1)}, bf16[16,6144]{1,0:T(8,128)(2,1)S(1)}, u32[]{:S(2)}, u32[]{:S(2)}) collective-permute-start(bf16[16,6144]{1,0:T(8,128)(2,1)} %get-tuple-element.16), channel_id=1, source_target_pairs={{0,16},{1,17},{2,18},{3,19},{4,20},{5,21},{6,22},{7,23},{8,24},{9,... | collective-permute-start | bytes 589832 | tf_op jit(solution)/shard_map/ppermute | solution.py:555
  43.8 25.4 %collective-permute-start.4 = (bf16[16,768]{1,0:T(8,128)(2,1)}, bf16[16,768]{1,0:T(8,128)(2,1)S(1)}, u32[]{:S(2)}, u32[]{:S(2)}) collective-permute-start(bf16[16,768]{1,0:T(8,128)(2,1)} %get-tuple-element.17), channel_id=1, source_target_pairs={{0,1},{1,2},{2,3},{3,4},{4,5},{5,6},{6,7},{7,8},{8,9},{9,10},{10,1... | collective-permute-start | bytes 73736 | tf_op jit(solution)/shard_map/ppermute | solution.py:555
  44.6 26.4 %collective-permute-start.5 = (bf16[16,768]{1,0:T(8,128)(2,1)}, bf16[16,768]{1,0:T(8,128)(2,1)S(1)}, u32[]{:S(2)}, u32[]{:S(2)}) collective-permute-start(bf16[16,768]{1,0:T(8,128)(2,1)} %get-tuple-element.17), channel_id=1, source_target_pairs={{0,17},{1,18},{2,19},{3,20},{4,21},{5,22},{6,23},{7,24},{8,25},{9,... | collective-permute-start | bytes 73736 | tf_op jit(solution)/shard_map/ppermute | solution.py:555
  69.2 1.7 %copy-start.1 = (bf16[16,768]{1,0:T(8,128)(2,1)}, bf16[16,768]{1,0:T(8,128)(2,1)S(1)}, u32[]{:S(2)}) copy-start(bf16[16,768]{1,0:T(8,128)(2,1)S(1)} %collective-permute-done.4.side_ref) | copy-start | bytes 73732
  70.9 0.6 copy-start.2
  70.9 0.7 copy-start

commit v7 on v6

--- a/solution.py
+++ b/solution.py
@@ -16,7 +16,7 @@
 F32 = jnp.float32
 BF16 = jnp.bfloat16
 VMEM_BYTES = 60 * 2**20
-LAST_BYTES = 62 * 2**20
+LAST_BYTES = 64 * 2**20 - 2**16
 SMEM = pl.BlockSpec(memory_space=pltpu.SMEM)
 ANY = pl.BlockSpec(memory_space=pl.ANY)
 
@@ -481,14 +481,22 @@
 
 
 def last_kernel(
-    entries_ref, own_hbm, rows_ref, side_ref, corner_ref, features_hbm, packed_ref,
-    marks_ref, held, own_ref, features_ref, sems, slot_sems,
+    entries_ref, own_hbm, rows_hbm, side_hbm, corner_hbm, features_hbm, packed_ref,
+    marks_ref, held, own_ref, features_ref, rows_ref, side_ref, corner_ref, sems, slot_sems,
 ):
     slots = packed_ref.shape[0]
     marks_copy = pltpu.make_async_copy(entries_ref.at[:, pl.ds(24, 1)], marks_ref, sems.at[0])
     own_copy = pltpu.make_async_copy(own_hbm, own_ref, sems.at[1])
     marks_copy.start()
     own_copy.start()
+    halos = [
+        pltpu.make_async_copy(src, dst, sems.at[3 + n])
+        for n, (src, dst) in enumerate(
+            [(rows_hbm, rows_ref), (side_hbm, side_ref), (corner_hbm, corner_ref)]
+        )
+    ]
+    for copy in halos:
+        copy.start()
     marks_copy.wait()
     marks = marks_ref[...][:, 0].astype(F32)
     lane = lax.broadcasted_iota(jnp.int32, marks.shape, 2).astype(F32)
@@ -501,6 +509,8 @@
     for copy in windows:
         copy.start()
     own_copy.wait()
+    for copy in halos:
+        copy.wait()
     merge_features(own_ref, rows_ref, side_ref, corner_ref, features_ref)
     leave = pltpu.make_async_copy(features_ref, features_hbm, sems.at[2])
     leave.start()
@@ -532,14 +542,15 @@
     return pl.pallas_call(
         last_kernel,
         out_shape=(jax.ShapeDtypeStruct(own.shape, BF16), jax.ShapeDtypeStruct((slots, width), BF16)),
-        in_specs=[ANY, ANY] + [pl.BlockSpec(memory_space=pltpu.VMEM)] * 3,
+        in_specs=[ANY] * 5,
         out_specs=(ANY, pl.BlockSpec(memory_space=pltpu.VMEM)),
         scratch_shapes=[
             pltpu.VMEM((arrived.shape[0], 1, 4, 128), BF16),
             pltpu.VMEM((slots,) + arrived.shape[1:], BF16),
         ]
         + [pltpu.VMEM(own.shape, BF16)] * 2
-        + [pltpu.SemaphoreType.DMA((3,)), pltpu.SemaphoreType.DMA((slots,))],
+        + [pltpu.VMEM(a.shape, BF16) for a in (rows, side, corner)]
+        + [pltpu.SemaphoreType.DMA((6,)), pltpu.SemaphoreType.DMA((slots,))],
         compiler_params=pltpu.CompilerParams(vmem_limit_bytes=LAST_BYTES),
         name="last_steps",
     )(arrived, own, rows, side, corner)

time: 76.3 us -> 74.9 us (0.982)
  Pallas kernels: 30.7 us -> 29.7 us
    pallas_call x1, Pallas kernels: 4.16 us -> 3.25 us  [last_steps(): pl.pallas_call(last_kernel, out_shape=(jax.ShapeDtypeStruct(own.shape, BF...]
where the time goes in v7:
time: 74.9 us; the launch traced here: 74.6 us
  Pallas kernels  29.7 us (40%)
  waiting for transfers between devices  24.2 us (32%)
  starting transfers between devices  18.5 us (25%)
  between operations  0.86 us (1%)
    ppermute x6, waiting for transfers between devices, moved(): return lax.ppermute(block, ('row', 'col'), route)  24.2 us
    pallas_call x1, Pallas kernels, second_layer(): pl.pallas_call(functools.partial(second_kernel, groups), grid=(n_half //...  14 us
    ppermute x6, starting transfers between devices, moved(): return lax.ppermute(block, ('row', 'col'), route)  12.6 us
    pallas_call x1, Pallas kernels, first_layer(): pl.pallas_call(functools.partial(first_kernel, groups), grid=(columns //...  12.4 us
    all_to_all x1, starting transfers between devices, local(): lax.all_to_all(send, ('row', 'col'), split_axis=0, concat_axis=0, tiled=T...  5.93 us
    pallas_call x1, Pallas kernels, last_steps(): pl.pallas_call(last_kernel, out_shape=(jax.ShapeDtypeStruct(own.shape, BF...  3.25 us
  transfers between devices with their start and end apart: 7, of which 2 were waited for; matrix products, arithmetic and copies ran while one was open for 1% of the time, Pallas kernels for 19%

profile of v7, /device:TPU:0, one launch (start us, length us, event | category | flops | bytes accessed | tf_op | source)
XLA Modules:
  0.0 74.6 jit_solution(1908946941639992331)
XLA Ops:
  0.6 12.4 %first_layer.1 = (bf16[32,32,192]{2,1,0:T(8,128)(2,1)}, bf16[32,32,192]{2,1,0:T(8,128)(2,1)}, bf16[32,16,192]{2,1,0:T(8,128)(2,1)}, bf16[80,192]{1,0:T(8,128)(2,1)}, bf16[128,25,4,128]{3,2,1,0:T(4,128)(2,1)}) custom-call(s32[2,16]{1,0:T(2,128)} %targets.1, s32[2,16]{1,0:T(2,128)} %slots.1, f32[2,6]{1,0:T(2,128)} %temper.3, bf16[16,24576]{1,0:T(8,128)(2,1)} %emb_ref.1, ...), custom_call_target="tpu_custom_call" | custom-call | flops 2000000000 | bytes 6000000 | tf_op jit(solution)/shard_map/first_layer/pallas_call | solution.py:309
  13.1 2.6 %collective-permute-start = (bf16[32,16,192]{2,1,0:T(8,128)(2,1)}, bf16[32,16,192]{2,1,0:T(8,128)(2,1)S(1)}, u32[]{:S(2)}, u32[]{:S(2)}) collective-permute-start(bf16[32,16,192]{2,1,0:T(8,128)(2,1)} %get-tuple-element.13), channel_id=1, source_target_pairs={{0,112},{1,113},{2,114},{3,115},{4,116},{5,117},{6,118},{7,119},{8... | collective-permute-start | bytes 589832 | tf_op jit(solution)/shard_map/ppermute | solution.py:566
  15.6 6.3 %collective-permute-start.1 = (bf16[80,192]{1,0:T(8,128)(2,1)}, bf16[80,192]{1,0:T(8,128)(2,1)S(1)}, u32[]{:S(2)}, u32[]{:S(2)}) collective-permute-start(bf16[80,192]{1,0:T(8,128)(2,1)} %get-tuple-element.14), channel_id=1, source_target_pairs={{0,15},{1,0},{2,1},{3,2},{4,3},{5,4},{6,5},{7,6},{8,7},{9,8},{10,9... | collective-permute-start | bytes 92168 | tf_op jit(solution)/shard_map/ppermute | solution.py:566
  21.9 0.7 collective-permute-start.2
  22.6 5.9 %all-to-all-start = ((bf16[128,25,4,128]{3,2,1,0:T(4,128)(2,1)}), bf16[128,25,4,128]{3,2,1,0:T(4,128)(2,1)}, u32[]{:S(2)}, u32[]{:S(2)}) async-start(bf16[128,25,4,128]{3,2,1,0:T(4,128)(2,1)} %get-tuple-element.10), calls=%async_computation | async-start | bytes 6553600 | tf_op jit(solution)/shard_map/all_to_all | solution.py:605
  28.5 0.6 pad_add_fusion.place
  29.1 0.0 collective-permute-done.1.right_ref
  29.1 0.0 copy-start.1
  29.1 0.0 collective-permute-done.2.corner_ref
  29.2 0.0 copy-start.2
  29.2 0.0 collective-permute-done.below_ref
  29.2 0.0 copy-start
  29.2 0.6 copy-done.1
  29.8 0.0 copy-done.2
  29.8 0.1 copy-done
  29.9 14.0 %second_layer.1 = (bf16[16,24576]{1,0:T(8,128)(2,1)}, bf16[16,6144]{1,0:T(8,128)(2,1)}, bf16[16,768]{1,0:T(8,128)(2,1)}) custom-call(s32[4]{0:T(128)} %pad_add_fusion.place, f32[2,6]{1,0:T(2,128)} %temper.3, bf16[32,32,192]{2,1,0:T(8,128)(2,1)} %get-tuple-element.11.mid0_ref, bf16[32,32,192]{2,1,0:T(8,128)(2,1)} %get-tuple-element.12.mid1_ref, ...), custom_call_target="tpu_custom_call" | custom-call | flops 99999997952 | bytes 10000000 | tf_op jit(solution)/shard_map/second_layer/pallas_call | solution.py:445
  43.9 0.0 collective-permute-start.3
  43.9 0.7 collective-permute-start.4
  44.7 2.3 %collective-permute-start.5 = (bf16[16,768]{1,0:T(8,128)(2,1)}, bf16[16,768]{1,0:T(8,128)(2,1)}, u32[]{:S(2)}, u32[]{:S(2)}) collective-permute-start(bf16[16,768]{1,0:T(8,128)(2,1)} %get-tuple-element.17), channel_id=1, source_target_pairs={{0,17},{1,18},{2,19},{3,20},{4,21},{5,22},{6,23},{7,24},{8,25},{9,... | collective-permute-start | bytes 73736 | tf_op jit(solution)/shard_map/ppermute | solution.py:566
  47.0 22.4 %collective-permute-done.4.side_hbm = bf16[16,768]{1,0:T(8,128)(2,1)} collective-permute-done((bf16[16,768]{1,0:T(8,128)(2,1)}, bf16[16,768]{1,0:T(8,128)(2,1)}, u32[]{:S(2)}, u32[]{:S(2)}) %collective-permute-start.4) | collective-permute-done | bytes 24608 | tf_op jit(solution)/shard_map/ppermute | solution.py:566
  69.4 1.7 %collective-permute-done.5.corner_hbm = bf16[16,768]{1,0:T(8,128)(2,1)} collective-permute-done((bf16[16,768]{1,0:T(8,128)(2,1)}, bf16[16,768]{1,0:T(8,128)(2,1)}, u32[]{:S(2)}, u32[]{:S(2)}) %collective-permute-start.5) | collective-permute-done | bytes 24608 | tf_op jit(solution)/shard_map/ppermute | solution.py:566
  71.1 0.0 collective-permute-done.3.rows_hbm
  71.1 0.0 all-to-all-done.entries_ref
  71.1 3.3 %last_steps.1 = (bf16[16,24576]{1,0:T(8,128)(2,1)}, bf16[16,12288]{1,0:T(8,128)(2,1)}) custom-call(bf16[128,25,4,128]{3,2,1,0:T(4,128)(2,1)} %all-to-all-done.entries_ref, bf16[16,24576]{1,0:T(8,128)(2,1)} %get-tuple-element.15.own_hbm, bf16[16,6144]{1,0:T(8,128)(2,1)} %collective-permute-done.3.rows_hbm, bf16[16,768]{1,0:T(8,128)(2,1)} %collective-permute-done.4.side_hbm, ...), custom_call_target="tpu_custom_call" | custom-call | tf_op jit(solution)/shard_map/last_steps/pallas_call | solution.py:542
Async XLA Ops:
  13.1 16.1 %collective-permute-start = (bf16[32,16,192]{2,1,0:T(8,128)(2,1)}, bf16[32,16,192]{2,1,0:T(8,128)(2,1)S(1)}, u32[]{:S(2)}, u32[]{:S(2)}) collective-permute-start(bf16[32,16,192]{2,1,0:T(8,128)(2,1)} %get-tuple-element.13), channel_id=1, source_target_pairs={{0,112},{1,113},{2,114},{3,115},{4,116},{5,117},{6,118},{7,119},{8... | collective-permute-start | bytes 589832 | tf_op jit(solution)/shard_map/ppermute | solution.py:566
  15.6 13.5 %collective-permute-start.1 = (bf16[80,192]{1,0:T(8,128)(2,1)}, bf16[80,192]{1,0:T(8,128)(2,1)S(1)}, u32[]{:S(2)}, u32[]{:S(2)}) collective-permute-start(bf16[80,192]{1,0:T(8,128)(2,1)} %get-tuple-element.14), channel_id=1, source_target_pairs={{0,15},{1,0},{2,1},{3,2},{4,3},{5,4},{6,5},{7,6},{8,7},{9,8},{10,9... | collective-permute-start | bytes 92168 | tf_op jit(solution)/shard_map/ppermute | solution.py:566
  21.9 7.2 %collective-permute-start.2 = (bf16[80,192]{1,0:T(8,128)(2,1)}, bf16[80,192]{1,0:T(8,128)(2,1)S(1)}, u32[]{:S(2)}, u32[]{:S(2)}) collective-permute-start(bf16[80,192]{1,0:T(8,128)(2,1)} %get-tuple-element.14), channel_id=1, source_target_pairs={{0,127},{1,112},{2,113},{3,114},{4,115},{5,116},{6,117},{7,118},{8... | collective-permute-start | bytes 92168 | tf_op jit(solution)/shard_map/ppermute | solution.py:566
  22.6 48.5 %all-to-all-start = ((bf16[128,25,4,128]{3,2,1,0:T(4,128)(2,1)}), bf16[128,25,4,128]{3,2,1,0:T(4,128)(2,1)}, u32[]{:S(2)}, u32[]{:S(2)}) async-start(bf16[128,25,4,128]{3,2,1,0:T(4,128)(2,1)} %get-tuple-element.10), calls=%async_computation | async-start | bytes 6553600 | tf_op jit(solution)/shard_map/all_to_all | solution.py:605
  29.1 0.6 copy-start.1
  29.2 0.6 copy-start.2
  29.2 0.7 copy-start
  43.9 27.2 %collective-permute-start.3 = (bf16[16,6144]{1,0:T(8,128)(2,1)}, bf16[16,6144]{1,0:T(8,128)(2,1)}, u32[]{:S(2)}, u32[]{:S(2)}) collective-permute-start(bf16[16,6144]{1,0:T(8,128)(2,1)} %get-tuple-element.16), channel_id=1, source_target_pairs={{0,16},{1,17},{2,18},{3,19},{4,20},{5,21},{6,22},{7,23},{8,24},{9,... | collective-permute-start | bytes 589832 | tf_op jit(solution)/shard_map/ppermute | solution.py:566
  43.9 25.5 %collective-permute-start.4 = (bf16[16,768]{1,0:T(8,128)(2,1)}, bf16[16,768]{1,0:T(8,128)(2,1)}, u32[]{:S(2)}, u32[]{:S(2)}) collective-permute-start(bf16[16,768]{1,0:T(8,128)(2,1)} %get-tuple-element.17), channel_id=1, source_target_pairs={{0,1},{1,2},{2,3},{3,4},{4,5},{5,6},{6,7},{7,8},{8,9},{9,10},{10,1... | collective-permute-start | bytes 73736 | tf_op jit(solution)/shard_map/ppermute | solution.py:566
  44.7 26.5 %collective-permute-start.5 = (bf16[16,768]{1,0:T(8,128)(2,1)}, bf16[16,768]{1,0:T(8,128)(2,1)}, u32[]{:S(2)}, u32[]{:S(2)}) collective-permute-start(bf16[16,768]{1,0:T(8,128)(2,1)} %get-tuple-element.17), channel_id=1, source_target_pairs={{0,17},{1,18},{2,19},{3,20},{4,21},{5,22},{6,23},{7,24},{8,25},{9,... | collective-permute-start | bytes 73736 | tf_op jit(solution)/shard_map/ppermute | solution.py:566

commit v8 on v7

--- a/solution.py
+++ b/solution.py
@@ -173,13 +173,15 @@
         even = tile[2 * pair * WIN : (2 * pair + 1) * WIN]
         odd = tile[(2 * pair + 1) * WIN : (2 * pair + 2) * WIN]
         pairs.append(jnp.where(first, even, pltpu.roll(odd, HALF, 0)))
-    return jnp.concatenate(pairs, 0)
+    tails = jnp.concatenate([pair[:, 128:] for pair in pairs], 1)
+    return jnp.concatenate([pair[:, :128] for pair in pairs] + [tails], 0)
 
 
 def whole_rows(halves):
     tiles = []
     for pair in range(2):
-        rows = halves[pair * WIN : (pair + 1) * WIN]
+        tails = halves[2 * WIN :, pair * 64 : (pair + 1) * 64]
+        rows = jnp.concatenate([halves[pair * WIN : (pair + 1) * WIN], tails], 1)
         tiles += [rows, pltpu.roll(rows, HALF, 0)]
     return jnp.concatenate(tiles, 0)
 
@@ -188,7 +190,7 @@
     groups,
     targets, slots, temper, emb_ref, token_ref, coords_ref, heads_ref, ones_ref, mask_ref,
     net_in, net_first, net_out, qkv_ref, proj_ref, up_ref, down_ref, gain_ref,
-    mid0_ref, mid1_ref, upper_ref, left_ref, send_ref,
+    mid0_ref, mid1_ref, upper_ref, left_ref, corner_ref, send_ref,
     bias_ref, strips_ref, q_w, k_w, v_w, p_ref, staging, blank, sems, blank_sem,
 ):
     step = pl.program_id(0)
@@ -254,7 +256,7 @@
                 def _(i=i, rows=rows, halves=halves):
                     left_ref[i * 32 : (i + 1) * 32] = rows[:32]
                     if i == 0:
-                        left_ref[64:] = halves[0]
+                        corner_ref[...] = halves[0]
 
             slot = j * 2 + i
             staging[slot, :16] = tile[:, :128].reshape(16, 4, 128).astype(BF16)
@@ -302,18 +304,19 @@
 def first_layer(embedded, targets, slots, temper, token, consts, params, devices, groups=16):
     n_heads, n_feat = consts[3].shape
     columns = embedded.shape[1] // (WIN * n_feat)
-    side = jax.ShapeDtypeStruct((80, n_feat), BF16)
-    upper = jax.ShapeDtypeStruct((2 * columns, 16, n_feat), BF16)
+    side = jax.ShapeDtypeStruct((64, n_feat), BF16)
+    upper = jax.ShapeDtypeStruct((2 * columns, 24, 128), BF16)
+    corner = jax.ShapeDtypeStruct((24, 128), BF16)
     mid = jax.ShapeDtypeStruct((2 * columns, 32, n_feat), BF16)
     mid_spec = pl.BlockSpec((2 * groups, 32, n_feat), lambda g: (g, 0, 0))
     return pl.pallas_call(
         functools.partial(first_kernel, groups),
         grid=(columns // groups,),
-        out_shape=(mid, mid, upper, side, jax.ShapeDtypeStruct((devices, 25, 4, 128), BF16)),
+        out_shape=(mid, mid, upper, side, corner, jax.ShapeDtypeStruct((devices, 25, 4, 128), BF16)),
         in_specs=[SMEM, SMEM, SMEM, pl.BlockSpec((2 * WIN, groups * WIN * n_feat), lambda g: (0, g))]
         + [whole(a) for a in (token,) + consts]
         + [layer_spec(a, n, 0) for n, a in enumerate(params)],
-        out_specs=(mid_spec, mid_spec, pl.BlockSpec((2 * groups, 16, n_feat), lambda g: (g, 0, 0)), whole(side), ANY),
+        out_specs=(mid_spec, mid_spec, pl.BlockSpec((2 * groups, 24, 128), lambda g: (g, 0, 0)), whole(side), whole(corner), ANY),
         scratch_shapes=[pltpu.VMEM((CELLS, n_heads * CELLS), F32)]
         + layer_scratch(n_heads, n_feat)
         + [
@@ -355,7 +358,7 @@
                     (right_ref.at[pl.ds(0, 32)], ext.at[0, n_half]),
                     (right_ref.at[pl.ds(32, 32)], ext.at[1, n_half]),
                     (below_ref, ring.at[own]),
-                    (corner_ref.at[pl.ds(64, 16)], ring.at[n_half]),
+                    (corner_ref, ring.at[n_half]),
                 ]
             )
         ]
@@ -455,7 +458,7 @@
         + layer_scratch(n_heads, n_feat)
         + [
             pltpu.VMEM((2, n_half + 1, 32, n_feat), BF16),
-            pltpu.VMEM((n_half + 1, 16, n_feat), BF16),
+            pltpu.VMEM((n_half + 1, 24, 128), BF16),
             pltpu.VMEM((groups * 2 * CELLS, n_heads * CELLS), BF16),
             pltpu.SemaphoreType.DMA((6,)),
         ],
@@ -597,11 +600,11 @@
         jnp.swapaxes(down_weight, 1, 2),
         norm_gain_values,
     )
-    mid0, mid1, upper, left, send = first_layer(
+    mid0, mid1, upper, left, corner, send = first_layer(
         embedded, window_target_device, window_device_slot, temper, cloud_mask_token, consts, params,
         n_row * n_col,
     )
-    pieces = (mid0, mid1, moved(upper, -1, 0), moved(left, 0, -1), moved(left, -1, -1))
+    pieces = (mid0, mid1, moved(upper, -1, 0), moved(left, 0, -1), moved(corner, -1, -1))
     arrived = lax.all_to_all(send, ("row", "col"), split_axis=0, concat_axis=0, tiled=True)
     own, rows, side = second_layer(place, temper, pieces, consts, params)
     return last_steps(

time: 74.9 us -> 74.8 us (level)
  no operation moved by 1% of the time
where the time goes in v8:
time: 74.8 us; the launch traced here: 74.4 us
  Pallas kernels  29.7 us (40%)
  waiting for transfers between devices  24.1 us (32%)
  starting transfers between devices  18.4 us (25%)
  between operations  0.86 us (1%)
    ppermute x6, waiting for transfers between devices, moved(): return lax.ppermute(block, ('row', 'col'), route)  24.1 us
    pallas_call x1, Pallas kernels, second_layer(): pl.pallas_call(functools.partial(second_kernel, groups), grid=(n_half //...  14 us
    ppermute x6, starting transfers between devices, moved(): return lax.ppermute(block, ('row', 'col'), route)  12.5 us
    pallas_call x1, Pallas kernels, first_layer(): pl.pallas_call(functools.partial(first_kernel, groups), grid=(columns //...  12.4 us
    all_to_all x1, starting transfers between devices, local(): lax.all_to_all(send, ('row', 'col'), split_axis=0, concat_axis=0, tiled=T...  5.93 us
    pallas_call x1, Pallas kernels, last_steps(): pl.pallas_call(last_kernel, out_shape=(jax.ShapeDtypeStruct(own.shape, BF...  3.25 us
  transfers between devices with their start and end apart: 7, of which 2 were waited for; matrix products, arithmetic and copies ran while one was open for 1% of the time, Pallas kernels for 19%

profile of v8, /device:TPU:0, one launch (start us, length us, event | category | flops | bytes accessed | tf_op | source)
XLA Modules:
  0.0 74.4 jit_solution(3064321017502069232)
XLA Ops:
  0.6 12.4 %first_layer.1 = (bf16[32,32,192]{2,1,0:T(8,128)(2,1)}, bf16[32,32,192]{2,1,0:T(8,128)(2,1)}, bf16[32,24,128]{2,1,0:T(8,128)(2,1)}, bf16[64,192]{1,0:T(8,128)(2,...) custom-call(s32[2,16]{1,0:T(2,128)} %targets.1, s32[2,16]{1,0:T(2,128)} %slots.1, f32[2,6]{1,0:T(2,128)} %temper.3, ...), custom_call_target="tpu_custom_call" | custom-call | flops 2000000000 | bytes 6000000 | tf_op jit(solution)/shard_map/first_layer/pallas_call | solution.py:312
  13.1 2.5 %collective-permute-start = (bf16[32,24,128]{2,1,0:T(8,128)(2,1)}, bf16[32,24,128]{2,1,0:T(8,128)(2,1)S(1)}, u32[]{:S(2)}, u32[]{:S(2)}) collective-permute-start(bf16[32,24,128]{2,1,0:T(8,128)(2,1)} %get-tuple-element.14), channel_id=1, source_target_pairs={{0,112},{1,113},{2,114},{3,115},{4,116},{5,117},{6,118},{7,119},{8... | collective-permute-start | bytes 589832 | tf_op jit(solution)/shard_map/ppermute | solution.py:569
  15.6 6.2 %collective-permute-start.1 = (bf16[64,192]{1,0:T(8,128)(2,1)}, bf16[64,192]{1,0:T(8,128)(2,1)S(1)}, u32[]{:S(2)}, u32[]{:S(2)}) collective-permute-start(bf16[64,192]{1,0:T(8,128)(2,1)} %get-tuple-element.15), channel_id=1, source_target_pairs={{0,15},{1,0},{2,1},{3,2},{4,3},{5,4},{6,5},{7,6},{8,7},{9,8},{10,9... | collective-permute-start | bytes 73736 | tf_op jit(solution)/shard_map/ppermute | solution.py:569
  21.8 0.7 collective-permute-start.2
  22.5 5.9 %all-to-all-start = ((bf16[128,25,4,128]{3,2,1,0:T(4,128)(2,1)}), bf16[128,25,4,128]{3,2,1,0:T(4,128)(2,1)}, u32[]{:S(2)}, u32[]{:S(2)}) async-start(bf16[128,25,4,128]{3,2,1,0:T(4,128)(2,1)} %get-tuple-element.11), calls=%async_computation | async-start | bytes 6553600 | tf_op jit(solution)/shard_map/all_to_all | solution.py:608
  28.4 0.7 pad_add_fusion.place
  29.1 0.0 collective-permute-done.2.corner_ref
  29.1 0.0 copy-start.2
  29.1 0.0 collective-permute-done.1.right_ref
  29.1 0.0 copy-start.1
  29.1 0.0 collective-permute-done.below_ref
  29.1 0.0 copy-start
  29.1 0.6 copy-done.2
  29.7 0.0 copy-done.1
  29.7 0.1 copy-done
  29.8 14.0 %second_layer.1 = (bf16[16,24576]{1,0:T(8,128)(2,1)}, bf16[16,6144]{1,0:T(8,128)(2,1)}, bf16[16,768]{1,0:T(8,128)(2,1)}) custom-call(s32[4]{0:T(128)} %pad_add_fusion.place, f32[2,6]{1,0:T(2,128)} %temper.3, bf16[32,32,192]{2,1,0:T(8,128)(2,1)} %get-tuple-element.12.mid0_ref, bf16[32,32,192]{2,1,0:T(8,128)(2,1)} %get-tuple-element.13.mid1_ref, ...), custom_call_target="tpu_custom_call" | custom-call | flops 99999997952 | bytes 10000000 | tf_op jit(solution)/shard_map/second_layer/pallas_call | solution.py:448
  43.8 0.0 collective-permute-start.3
  43.9 0.7 collective-permute-start.4
  44.6 2.3 %collective-permute-start.5 = (bf16[16,768]{1,0:T(8,128)(2,1)}, bf16[16,768]{1,0:T(8,128)(2,1)}, u32[]{:S(2)}, u32[]{:S(2)}) collective-permute-start(bf16[16,768]{1,0:T(8,128)(2,1)} %get-tuple-element.19), channel_id=1, source_target_pairs={{0,17},{1,18},{2,19},{3,20},{4,21},{5,22},{6,23},{7,24},{8,25},{9,... | collective-permute-start | bytes 73736 | tf_op jit(solution)/shard_map/ppermute | solution.py:569
  46.9 22.4 %collective-permute-done.4.side_hbm = bf16[16,768]{1,0:T(8,128)(2,1)} collective-permute-done((bf16[16,768]{1,0:T(8,128)(2,1)}, bf16[16,768]{1,0:T(8,128)(2,1)}, u32[]{:S(2)}, u32[]{:S(2)}) %collective-permute-start.4) | collective-permute-done | bytes 24608 | tf_op jit(solution)/shard_map/ppermute | solution.py:569
  69.3 1.7 %collective-permute-done.5.corner_hbm = bf16[16,768]{1,0:T(8,128)(2,1)} collective-permute-done((bf16[16,768]{1,0:T(8,128)(2,1)}, bf16[16,768]{1,0:T(8,128)(2,1)}, u32[]{:S(2)}, u32[]{:S(2)}) %collective-permute-start.5) | collective-permute-done | bytes 24608 | tf_op jit(solution)/shard_map/ppermute | solution.py:569
  71.0 0.0 collective-permute-done.3.rows_hbm
  71.0 0.0 all-to-all-done.entries_ref
  71.0 3.3 %last_steps.1 = (bf16[16,24576]{1,0:T(8,128)(2,1)}, bf16[16,12288]{1,0:T(8,128)(2,1)}) custom-call(bf16[128,25,4,128]{3,2,1,0:T(4,128)(2,1)} %all-to-all-done.entries_ref, bf16[16,24576]{1,0:T(8,128)(2,1)} %get-tuple-element.17.own_hbm, bf16[16,6144]{1,0:T(8,128)(2,1)} %collective-permute-done.3.rows_hbm, bf16[16,768]{1,0:T(8,128)(2,1)} %collective-permute-done.4.side_hbm, ...), custom_call_target="tpu_custom_call" | custom-call | tf_op jit(solution)/shard_map/last_steps/pallas_call | solution.py:545
Async XLA Ops:
  13.1 16.0 %collective-permute-start = (bf16[32,24,128]{2,1,0:T(8,128)(2,1)}, bf16[32,24,128]{2,1,0:T(8,128)(2,1)S(1)}, u32[]{:S(2)}, u32[]{:S(2)}) collective-permute-start(bf16[32,24,128]{2,1,0:T(8,128)(2,1)} %get-tuple-element.14), channel_id=1, source_target_pairs={{0,112},{1,113},{2,114},{3,115},{4,116},{5,117},{6,118},{7,119},{8... | collective-permute-start | bytes 589832 | tf_op jit(solution)/shard_map/ppermute | solution.py:569
  15.6 13.5 %collective-permute-start.1 = (bf16[64,192]{1,0:T(8,128)(2,1)}, bf16[64,192]{1,0:T(8,128)(2,1)S(1)}, u32[]{:S(2)}, u32[]{:S(2)}) collective-permute-start(bf16[64,192]{1,0:T(8,128)(2,1)} %get-tuple-element.15), channel_id=1, source_target_pairs={{0,15},{1,0},{2,1},{3,2},{4,3},{5,4},{6,5},{7,6},{8,7},{9,8},{10,9... | collective-permute-start | bytes 73736 | tf_op jit(solution)/shard_map/ppermute | solution.py:569
  21.8 7.3 %collective-permute-start.2 = (bf16[24,128]{1,0:T(8,128)(2,1)}, bf16[24,128]{1,0:T(8,128)(2,1)S(1)}, u32[]{:S(2)}, u32[]{:S(2)}) collective-permute-start(bf16[24,128]{1,0:T(8,128)(2,1)} %get-tuple-element.16), channel_id=1, source_target_pairs={{0,127},{1,112},{2,113},{3,114},{4,115},{5,116},{6,117},{7,118},{8... | collective-permute-start | bytes 18440 | tf_op jit(solution)/shard_map/ppermute | solution.py:569
  22.5 48.5 %all-to-all-start = ((bf16[128,25,4,128]{3,2,1,0:T(4,128)(2,1)}), bf16[128,25,4,128]{3,2,1,0:T(4,128)(2,1)}, u32[]{:S(2)}, u32[]{:S(2)}) async-start(bf16[128,25,4,128]{3,2,1,0:T(4,128)(2,1)} %get-tuple-element.11), calls=%async_computation | async-start | bytes 6553600 | tf_op jit(solution)/shard_map/all_to_all | solution.py:608
  29.1 0.6 copy-start.2
  29.1 0.6 copy-start.1
  29.1 0.7 copy-start
  43.8 27.2 %collective-permute-start.3 = (bf16[16,6144]{1,0:T(8,128)(2,1)}, bf16[16,6144]{1,0:T(8,128)(2,1)}, u32[]{:S(2)}, u32[]{:S(2)}) collective-permute-start(bf16[16,6144]{1,0:T(8,128)(2,1)} %get-tuple-element.18), channel_id=1, source_target_pairs={{0,16},{1,17},{2,18},{3,19},{4,20},{5,21},{6,22},{7,23},{8,24},{9,... | collective-permute-start | bytes 589832 | tf_op jit(solution)/shard_map/ppermute | solution.py:569
  43.9 25.4 %collective-permute-start.4 = (bf16[16,768]{1,0:T(8,128)(2,1)}, bf16[16,768]{1,0:T(8,128)(2,1)}, u32[]{:S(2)}, u32[]{:S(2)}) collective-permute-start(bf16[16,768]{1,0:T(8,128)(2,1)} %get-tuple-element.19), channel_id=1, source_target_pairs={{0,1},{1,2},{2,3},{3,4},{4,5},{5,6},{6,7},{7,8},{8,9},{9,10},{10,1... | collective-permute-start | bytes 73736 | tf_op jit(solution)/shard_map/ppermute | solution.py:569
  44.6 26.4 %collective-permute-start.5 = (bf16[16,768]{1,0:T(8,128)(2,1)}, bf16[16,768]{1,0:T(8,128)(2,1)}, u32[]{:S(2)}, u32[]{:S(2)}) collective-permute-start(bf16[16,768]{1,0:T(8,128)(2,1)} %get-tuple-element.19), channel_id=1, source_target_pairs={{0,17},{1,18},{2,19},{3,20},{4,21},{5,22},{6,23},{7,24},{8,25},{9,... | collective-permute-start | bytes 73736 | tf_op jit(solution)/shard_map/ppermute | solution.py:569
